TPU v7x, 512 devices: a whole 4x4x16 slice. The times are simulated.
512 devices in a mesh: section: 4 (over x), dp: 16 (over z), mp: 8 (over y, core).
Axes of the slice: x: 4, y: 4, z: 16, core: 2. Of those that a mesh axis runs over, the one named last changes fastest.
Arguments:
- images: bfloat16 [32, 2, 8, 12, 768], P('dp'), may hold values from -6 to 6
- token_grads: bfloat16 [32, 2, 8, 12, 768], P('dp'), may hold values from -0.119628906 to 0.119628906
- counts: int32 [32], P('dp'), may hold values from 1 to 2
- dw_kernel: float32 [4, 7, 7, 768], P('section'), may hold values from -0.875 to 0.875
- ln_gain: float32 [4, 768], P('section'), may hold values from 0.5 to 1.5
- w_in: bfloat16 [4, 768, 3072], P('section', None, 'mp'), may hold values from -0.21875 to 0.21875
- w_out: bfloat16 [4, 3072, 768], P('section', 'mp'), may hold values from -0.109375 to 0.109375
- layer_scale: float32 [4, 768], P('section'), may hold values from 0.3 to 1.5
Outputs:
- grad_in: bfloat16 [4, 768, 3072], P('section', 'dp', 'mp')
- grad_out_t: bfloat16 [4, 768, 3072], P('section', 'dp', 'mp')
Inputs may be any that keep to these rules, and one draw needn't show every extreme that they name: Each sample has at least one image; its first counts images are live.
All inputs are finite; a program needn't handle non-finite values.
Results may differ from a plain program's by a relative error of at most 0.04.
Values may be sent and summed in bfloat16 or wider, within the bound.
No kernel may reach another device: no remote copies, remote signals or barrier semaphores. Data moves between devices by JAX's collectives and lax.ppermute only.
A program may use at most 128 MiB of HBM per device.

v0:
```python
import jax
import jax.numpy as jnp
from jax import lax
from jax.sharding import PartitionSpec as P


def shifted(value, axis, by):
    count = lax.axis_size(axis)
    pairs = [(i, i + by) for i in range(count) if 0 <= i + by < count]
    return lax.ppermute(value, axis, pairs)


def mix_in(block_in, kernel, gain):
    values = block_in.astype(jnp.float32)
    rows = values.shape[-3]
    cols = values.shape[-2]
    widths = [(0, 0)] * (values.ndim - 3) + [(3, 3), (3, 3), (0, 0)]
    padded = jnp.pad(values, widths)
    total = jnp.zeros_like(values)
    for first in range(7):
        for second in range(7):
            total = (
                total
                + padded[..., first : first + rows, second : second + cols, :]
                * kernel[first, second]
            )
    center = jnp.mean(total, axis=-1, keepdims=True)
    spread = jnp.mean((total - center) ** 2, axis=-1, keepdims=True)
    return (total - center) * lax.rsqrt(spread + 1e-06) * gain


def shards(images, token_grads, counts, dw_kernel, ln_gain, w_in, w_out, layer_scale):
    section = lax.axis_index("section")
    depth = lax.axis_size("section")
    micro = images.shape[0]
    shape = images.shape[1:]
    channels = shape[-1]
    kernel = dw_kernel[0]
    gain = ln_gain[0]
    wide_in = w_in[0]
    wide_out = w_out[0]
    scale = layer_scale[0]
    live = (jnp.arange(shape[0])[None, :] < counts[:, None]).astype(jnp.bfloat16)[
        :, :, None, None, None
    ]
    ticks = micro + depth - 1

    def forward_tick(tick, carry):
        sent, stored = carry
        arrived = shifted(sent, "section", 1)
        index = tick - section
        valid = (index >= 0) & (index < micro)
        slot = jnp.clip(index, 0, micro - 1)
        block_in = jnp.where(section == 0, images[slot] * live[slot], arrived)
        normed = mix_in(block_in, kernel, gain).astype(jnp.bfloat16).reshape(-1, channels)
        hidden = jax.nn.gelu(
            jnp.dot(normed, wide_in, preferred_element_type=jnp.float32), approximate=False
        ).astype(jnp.bfloat16)
        partial_value = jnp.dot(hidden, wide_out, preferred_element_type=jnp.float32)
        mixed = lax.psum(partial_value.astype(jnp.bfloat16), "mp").astype(jnp.float32)
        block_out = (block_in.astype(jnp.float32) + scale * mixed.reshape(shape)).astype(
            jnp.bfloat16
        )
        stored = jnp.where(valid, stored.at[slot].set(block_in), stored)
        return (block_out, stored)

    start = (jnp.zeros(shape, jnp.bfloat16), jnp.zeros(images.shape, jnp.bfloat16))
    last_out, stored = lax.fori_loop(0, ticks, forward_tick, start)

    def backward_tick(tick, carry):
        sent, grad_in, grad_out = carry
        arrived = shifted(sent, "section", -1)
        index = tick - (depth - 1 - section)
        valid = (index >= 0) & (index < micro)
        slot = jnp.clip(index, 0, micro - 1)
        upstream = jnp.where(section == depth - 1, token_grads[slot] * live[slot], arrived)
        block_in = stored[slot]
        normed32, pull = jax.vjp(lambda v: mix_in(v, kernel, gain), block_in.astype(jnp.float32))
        normed = normed32.astype(jnp.bfloat16).reshape(-1, channels)
        before = jnp.dot(normed, wide_in, preferred_element_type=jnp.float32)
        hidden = jax.nn.gelu(before, approximate=False).astype(jnp.bfloat16)
        branch = (upstream.astype(jnp.float32) * scale).astype(jnp.bfloat16).reshape(-1, channels)
        out_term = jnp.einsum("tc,tf->cf", branch, hidden, preferred_element_type=jnp.float32)
        back_hidden = jnp.einsum("tc,fc->tf", branch, wide_out, preferred_element_type=jnp.float32)
        gelu_out, gelu_pull = jax.vjp(lambda v: jax.nn.gelu(v, approximate=False), before)
        back = gelu_pull(back_hidden)[0].astype(jnp.bfloat16)
        in_term = jnp.einsum("tc,tf->cf", normed, back, preferred_element_type=jnp.float32)
        partial_value = jnp.einsum("tf,cf->tc", back, wide_in, preferred_element_type=jnp.float32)
        dnorm = lax.psum(partial_value.astype(jnp.bfloat16), "mp").astype(jnp.float32)
        back_input = pull(dnorm.reshape(shape))[0]
        sent = (upstream.astype(jnp.float32) + back_input).astype(jnp.bfloat16)
        grad_in = grad_in + jnp.where(valid, in_term, 0.0)
        grad_out = grad_out + jnp.where(valid, out_term, 0.0)
        return (sent, grad_in, grad_out)

    empty = jnp.zeros((channels, wide_in.shape[1]), jnp.float32)
    start = (jnp.zeros(shape, jnp.bfloat16), empty, empty)
    sent, grad_in, grad_out = lax.fori_loop(0, ticks, backward_tick, start)
    summed_in, summed_out = (
        lax.psum(grad_in.astype(jnp.bfloat16), "dp").astype(jnp.float32),
        lax.psum(grad_out.astype(jnp.bfloat16), "dp").astype(jnp.float32),
    )
    share = channels // lax.axis_size("dp")
    offset = lax.axis_index("dp") * share
    part_in = lax.dynamic_slice_in_dim(summed_in, offset, share, 0)
    part_out = lax.dynamic_slice_in_dim(summed_out, offset, share, 0)
    return (part_in.astype(jnp.bfloat16)[None], part_out.astype(jnp.bfloat16)[None])


def solution(mesh):
    return jax.shard_map(
        shards,
        mesh=mesh,
        in_specs=(
            P("dp", None, None, None, None),
            P("dp", None, None, None, None),
            P("dp"),
            P("section", None, None, None),
            P("section", None),
            P("section", None, "mp"),
            P("section", "mp", None),
            P("section", None),
        ),
        out_specs=(P("section", "dp", "mp"), P("section", "dp", "mp")),
        check_vma=False,
    )
```

profile of v0, /device:TPU:6, one launch (start us, length us, event | category | flops | bytes accessed | tf_op | source)
XLA Modules:
  0.0 1263.0 jit_solution(814159084452280619)
XLA Ops:
  10.7 516.3 %while.39 = (s32[]{:T(128)}, bf16[2,8,12,768]{3,2,1,0:T(8,128)(2,1)}, bf16[2,2,8,12,768]{4,3,2,1,0:T(8,128)(2,1)}, pred[]{:T(512)}, s32[]{:T(128)}, /*index=5*/b...) while((s32[]{:T(128)}, ...), condition=%wide.region_5.6_spmd.clone, body=%wide.region_0.5_spmd.clone.sunk | while | flops 249716944 | bytes 21330928 | solution.py:68
  18.0 5.5 collective-permute-done
  23.6 6.5 fusion.337
  35.5 79.4 %all-reduce.58.cloned.1.call-done = bf16[2,8,12,768]{3,2,1,0:T(8,128)(2,1)} async-done(((bf16[2,8,12,768]{3,2,1,0:T(8,128)(2,1)}), bf16[2,8,12,768]{3,2,1,0:T(8,128)(2,1)}) %all-reduce.58.cloned.1.call-update) | async-done | bytes 294928 | tf_op jit(solution)/shard_map/while/body/eval_jaxpr/psum | solution.py:60
  125.3 3.4 collective-permute-done
  128.9 6.5 fusion.337
  140.7 76.7 %all-reduce.58.cloned.1.call-done = bf16[2,8,12,768]{3,2,1,0:T(8,128)(2,1)} async-done(((bf16[2,8,12,768]{3,2,1,0:T(8,128)(2,1)}), bf16[2,8,12,768]{3,2,1,0:T(8,128)(2,1)}) %all-reduce.58.cloned.1.call-update) | async-done | bytes 294928 | tf_op jit(solution)/shard_map/while/body/eval_jaxpr/psum | solution.py:60
  227.8 3.4 collective-permute-done
  231.4 6.5 fusion.337
  243.2 76.7 %all-reduce.58.cloned.1.call-done = bf16[2,8,12,768]{3,2,1,0:T(8,128)(2,1)} async-done(((bf16[2,8,12,768]{3,2,1,0:T(8,128)(2,1)}), bf16[2,8,12,768]{3,2,1,0:T(8,128)(2,1)}) %all-reduce.58.cloned.1.call-update) | async-done | bytes 294928 | tf_op jit(solution)/shard_map/while/body/eval_jaxpr/psum | solution.py:60
  330.3 3.4 collective-permute-done
  333.9 6.5 fusion.337
  345.7 76.7 %all-reduce.58.cloned.1.call-done = bf16[2,8,12,768]{3,2,1,0:T(8,128)(2,1)} async-done(((bf16[2,8,12,768]{3,2,1,0:T(8,128)(2,1)}), bf16[2,8,12,768]{3,2,1,0:T(8,128)(2,1)}) %all-reduce.58.cloned.1.call-update) | async-done | bytes 294928 | tf_op jit(solution)/shard_map/while/body/eval_jaxpr/psum | solution.py:60
  432.8 3.4 collective-permute-done
  436.4 6.5 fusion.337
  448.2 76.7 %all-reduce.58.cloned.1.call-done = bf16[2,8,12,768]{3,2,1,0:T(8,128)(2,1)} async-done(((bf16[2,8,12,768]{3,2,1,0:T(8,128)(2,1)}), bf16[2,8,12,768]{3,2,1,0:T(8,128)(2,1)}) %all-reduce.58.cloned.1.call-update) | async-done | bytes 294928 | tf_op jit(solution)/shard_map/while/body/eval_jaxpr/psum | solution.py:60
  527.0 585.0 %while.40 = (s32[]{:T(128)}, bf16[2,8,12,768]{3,2,1,0:T(8,128)(2,1)S(1)}, f32[768,384]{1,0:T(8,128)}, f32[768,384]{1,0:T(8,128)}, pred[]{:T(512)}, /*index=5*/s3...) while((s32[]{:T(128)}, ...), condition=%wide.region_13.14_spmd.clone, body=%wide.region_6.13_spmd.clone.sunk | while | flops 622523904 | bytes 92937968 | solution.py:98
  533.3 5.6 fusion.348
  546.8 72.7 %all-reduce.60.cloned.1.call-done = bf16[192,768]{1,0:T(8,128)(2,1)} async-done(((bf16[192,768]{1,0:T(8,128)(2,1)}), bf16[192,768]{1,0:T(8,128)(2,1)}) %all-reduce.60.cloned.1.call-update) | async-done | bytes 294928 | tf_op jit(solution)/shard_map/while/body/eval_jaxpr/psum | solution.py:89
  623.6 3.8 broadcast_multiply_fusion.60
  629.1 3.8 broadcast_multiply_fusion.61
  632.9 9.5 pad_add_fusion.8
  645.1 2.9 collective-permute-start.1
  650.7 5.6 fusion.348
  660.8 3.3 fusion.355
  666.8 69.7 %all-reduce.60.cloned.1.call-done = bf16[192,768]{1,0:T(8,128)(2,1)} async-done(((bf16[192,768]{1,0:T(8,128)(2,1)}), bf16[192,768]{1,0:T(8,128)(2,1)}) %all-reduce.60.cloned.1.call-update) | async-done | bytes 294928 | tf_op jit(solution)/shard_map/while/body/eval_jaxpr/psum | solution.py:89
  740.5 3.8 broadcast_multiply_fusion.60
  746.0 3.8 broadcast_multiply_fusion.61
  749.9 9.5 pad_add_fusion.8
  767.6 5.6 fusion.348
  777.7 3.3 fusion.355
  783.7 69.7 %all-reduce.60.cloned.1.call-done = bf16[192,768]{1,0:T(8,128)(2,1)} async-done(((bf16[192,768]{1,0:T(8,128)(2,1)}), bf16[192,768]{1,0:T(8,128)(2,1)}) %all-reduce.60.cloned.1.call-update) | async-done | bytes 294928 | tf_op jit(solution)/shard_map/while/body/eval_jaxpr/psum | solution.py:89
  857.4 3.8 broadcast_multiply_fusion.60
  863.0 3.8 broadcast_multiply_fusion.61
  866.8 9.5 pad_add_fusion.8
  884.5 5.6 fusion.348
  894.6 3.3 fusion.355
  900.6 69.7 %all-reduce.60.cloned.1.call-done = bf16[192,768]{1,0:T(8,128)(2,1)} async-done(((bf16[192,768]{1,0:T(8,128)(2,1)}), bf16[192,768]{1,0:T(8,128)(2,1)}) %all-reduce.60.cloned.1.call-update) | async-done | bytes 294928 | tf_op jit(solution)/shard_map/while/body/eval_jaxpr/psum | solution.py:89
  974.3 3.8 broadcast_multiply_fusion.60
  979.9 3.8 broadcast_multiply_fusion.61
  983.7 9.5 pad_add_fusion.8
  1001.4 5.6 fusion.348
  1011.6 3.3 fusion.355
  1017.5 69.7 %all-reduce.60.cloned.1.call-done = bf16[192,768]{1,0:T(8,128)(2,1)} async-done(((bf16[192,768]{1,0:T(8,128)(2,1)}), bf16[192,768]{1,0:T(8,128)(2,1)}) %all-reduce.60.cloned.1.call-update) | async-done | bytes 294928 | tf_op jit(solution)/shard_map/while/body/eval_jaxpr/psum | solution.py:89
  1091.2 3.8 broadcast_multiply_fusion.60
  1096.8 3.8 broadcast_multiply_fusion.61
  1100.6 9.5 pad_add_fusion.8
  1115.2 139.0 %all-reduce.56.cloned.1.call-done = (bf16[768,384]{1,0:T(8,128)(2,1)}, bf16[768,384]{1,0:T(8,128)(2,1)}) async-done(((bf16[768,384]{1,0:T(8,128)(2,1)}, bf16[768,384]{1,0:T(8,128)(2,1)}), (bf16[768,384]{1,0:T(8,128)(2,1)}, bf16[768,384]{1,0:T(8,128)(2,1)})) %all-reduce.56.cloned.1.call-update) | async-done | bytes 1179664 | tf_op jit(solution)/shard_map/psum | solution.py:100
  (499 shorter events, 186.5 us)
Async XLA Ops:
  10.7 12.9 %copy-start.16 = (bf16[2,2,1,1,1]{1,4,3,2,0:T(2,128)(2,1)}, bf16[2,2,1,1,1]{1,4,3,2,0:T(2,128)(2,1)S(1)}, u32[]{:S(2)}) copy-start(bf16[2,2,1,1,1]{1,4,3,2,0:T(2,128)(2,1)S(1)} %get-tuple-element.1462) | copy-start | bytes 28 | tf_op jit(solution)/shard_map/while
  10.7 104.2 %all-reduce.58.cloned.1.call-start = ((), (), s32[]{:S(2)}) async-start(), calls=%async_computation.1 | async-start | bytes 786432 | tf_op jit(solution)/shard_map/while/body/eval_jaxpr/psum | solution.py:60
  10.7 12.7 %collective-permute-start = (bf16[2,8,12,768]{3,2,1,0:T(8,128)(2,1)S(1)}, bf16[2,8,12,768]{3,2,1,0:T(8,128)(2,1)S(1)}, u32[]{:S(2)}, u32[]{:S(2)}) collective-permute-start(bf16[2,8,12,768]{3,2,1,0:T(8,128)(2,1)S(1)} %broadcast_select_fusion.4), channel_id=1, source_target_pairs={{0,128},{128,256},{256,384},{1,129},{129,257},{257,385},{2,130},{1... | collective-permute-start | bytes 884744 | tf_op jit(solution)/shard_map/while/body/eval_jaxpr/ppermute | solution.py:10
  33.6 81.3 %copy-start.9 = (f32[768]{0:T(1024)S(1)}, f32[768]{0:T(1024)}, u32[]{:S(2)}) copy-start(f32[768]{0:T(1024)} %reduce.237) | copy-start | bytes 9220 | tf_op jit(solution)/shard_map/while
  33.6 83.3 %copy-start.17 = (bf16[2,2,1,1,1]{1,4,3,2,0:T(2,128)(2,1)S(1)}, bf16[2,2,1,1,1]{1,4,3,2,0:T(2,128)(2,1)}, u32[]{:S(2)}) copy-start(bf16[2,2,1,1,1]{1,4,3,2,0:T(2,128)(2,1)} %copy-done.16) | copy-start | bytes 28 | tf_op jit(solution)/shard_map/while
  35.5 81.5 %copy-start.5 = (bf16[2,2,8,12,768]{4,3,2,1,0:T(8,128)(2,1)}, bf16[2,2,8,12,768]{4,3,2,1,0:T(8,128)(2,1)S(1)}, u32[]{:S(2)}) copy-start(bf16[2,2,8,12,768]{4,3,2,1,0:T(8,128)(2,1)S(1)} %fusion.338) | copy-start | bytes 1769476 | tf_op jit(solution)/shard_map/while
  116.9 100.5 %all-reduce.58.cloned.1.call-start = ((), (), s32[]{:S(2)}) async-start(), calls=%async_computation.1 | async-start | bytes 786432 | tf_op jit(solution)/shard_map/while/body/eval_jaxpr/psum | solution.py:60
  118.0 10.7 collective-permute-start
  138.9 78.6 %copy-start.9 = (f32[768]{0:T(1024)S(1)}, f32[768]{0:T(1024)}, u32[]{:S(2)}) copy-start(f32[768]{0:T(1024)} %reduce.237) | copy-start | bytes 9220 | tf_op jit(solution)/shard_map/while
  138.9 80.6 %copy-start.17 = (bf16[2,2,1,1,1]{1,4,3,2,0:T(2,128)(2,1)S(1)}, bf16[2,2,1,1,1]{1,4,3,2,0:T(2,128)(2,1)}, u32[]{:S(2)}) copy-start(bf16[2,2,1,1,1]{1,4,3,2,0:T(2,128)(2,1)} %copy-done.16) | copy-start | bytes 28 | tf_op jit(solution)/shard_map/while
  140.7 78.7 %copy-start.5 = (bf16[2,2,8,12,768]{4,3,2,1,0:T(8,128)(2,1)}, bf16[2,2,8,12,768]{4,3,2,1,0:T(8,128)(2,1)S(1)}, u32[]{:S(2)}) copy-start(bf16[2,2,8,12,768]{4,3,2,1,0:T(8,128)(2,1)S(1)} %fusion.338) | copy-start | bytes 1769476 | tf_op jit(solution)/shard_map/while
  219.4 11.9 copy-start.16
  219.4 100.5 %all-reduce.58.cloned.1.call-start = ((), (), s32[]{:S(2)}) async-start(), calls=%async_computation.1 | async-start | bytes 786432 | tf_op jit(solution)/shard_map/while/body/eval_jaxpr/psum | solution.py:60
  220.5 10.7 collective-permute-start
  241.4 78.6 %copy-start.9 = (f32[768]{0:T(1024)S(1)}, f32[768]{0:T(1024)}, u32[]{:S(2)}) copy-start(f32[768]{0:T(1024)} %reduce.237) | copy-start | bytes 9220 | tf_op jit(solution)/shard_map/while
  241.4 80.6 %copy-start.17 = (bf16[2,2,1,1,1]{1,4,3,2,0:T(2,128)(2,1)S(1)}, bf16[2,2,1,1,1]{1,4,3,2,0:T(2,128)(2,1)}, u32[]{:S(2)}) copy-start(bf16[2,2,1,1,1]{1,4,3,2,0:T(2,128)(2,1)} %copy-done.16) | copy-start | bytes 28 | tf_op jit(solution)/shard_map/while
  243.2 78.7 %copy-start.5 = (bf16[2,2,8,12,768]{4,3,2,1,0:T(8,128)(2,1)}, bf16[2,2,8,12,768]{4,3,2,1,0:T(8,128)(2,1)S(1)}, u32[]{:S(2)}) copy-start(bf16[2,2,8,12,768]{4,3,2,1,0:T(8,128)(2,1)S(1)} %fusion.338) | copy-start | bytes 1769476 | tf_op jit(solution)/shard_map/while
  321.9 100.5 %all-reduce.58.cloned.1.call-start = ((), (), s32[]{:S(2)}) async-start(), calls=%async_computation.1 | async-start | bytes 786432 | tf_op jit(solution)/shard_map/while/body/eval_jaxpr/psum | solution.py:60
  323.0 10.7 collective-permute-start
  343.9 78.6 %copy-start.9 = (f32[768]{0:T(1024)S(1)}, f32[768]{0:T(1024)}, u32[]{:S(2)}) copy-start(f32[768]{0:T(1024)} %reduce.237) | copy-start | bytes 9220 | tf_op jit(solution)/shard_map/while
  343.9 80.6 %copy-start.17 = (bf16[2,2,1,1,1]{1,4,3,2,0:T(2,128)(2,1)S(1)}, bf16[2,2,1,1,1]{1,4,3,2,0:T(2,128)(2,1)}, u32[]{:S(2)}) copy-start(bf16[2,2,1,1,1]{1,4,3,2,0:T(2,128)(2,1)} %copy-done.16) | copy-start | bytes 28 | tf_op jit(solution)/shard_map/while
  345.7 78.7 %copy-start.5 = (bf16[2,2,8,12,768]{4,3,2,1,0:T(8,128)(2,1)}, bf16[2,2,8,12,768]{4,3,2,1,0:T(8,128)(2,1)S(1)}, u32[]{:S(2)}) copy-start(bf16[2,2,8,12,768]{4,3,2,1,0:T(8,128)(2,1)S(1)} %fusion.338) | copy-start | bytes 1769476 | tf_op jit(solution)/shard_map/while
  424.4 100.5 %all-reduce.58.cloned.1.call-start = ((), (), s32[]{:S(2)}) async-start(), calls=%async_computation.1 | async-start | bytes 786432 | tf_op jit(solution)/shard_map/while/body/eval_jaxpr/psum | solution.py:60
  425.5 10.7 collective-permute-start
  446.4 78.6 %copy-start.9 = (f32[768]{0:T(1024)S(1)}, f32[768]{0:T(1024)}, u32[]{:S(2)}) copy-start(f32[768]{0:T(1024)} %reduce.237) | copy-start | bytes 9220 | tf_op jit(solution)/shard_map/while
  446.4 80.6 %copy-start.17 = (bf16[2,2,1,1,1]{1,4,3,2,0:T(2,128)(2,1)S(1)}, bf16[2,2,1,1,1]{1,4,3,2,0:T(2,128)(2,1)}, u32[]{:S(2)}) copy-start(bf16[2,2,1,1,1]{1,4,3,2,0:T(2,128)(2,1)} %copy-done.16) | copy-start | bytes 28 | tf_op jit(solution)/shard_map/while
  448.2 78.7 %copy-start.5 = (bf16[2,2,8,12,768]{4,3,2,1,0:T(8,128)(2,1)}, bf16[2,2,8,12,768]{4,3,2,1,0:T(8,128)(2,1)S(1)}, u32[]{:S(2)}) copy-start(bf16[2,2,8,12,768]{4,3,2,1,0:T(8,128)(2,1)S(1)} %fusion.338) | copy-start | bytes 1769476 | tf_op jit(solution)/shard_map/while
  527.0 11.9 copy-start.6
  527.0 12.4 copy-start.18
  527.0 92.6 %all-reduce.60.cloned.1.call-start = ((), (), s32[]{:S(2)}) async-start(), calls=%async_computation.2 | async-start | bytes 589824 | tf_op jit(solution)/shard_map/while/body/eval_jaxpr/psum | solution.py:89
  527.8 12.2 collective-permute-start.1
  644.3 12.1 copy-start.6
  644.3 12.6 copy-start.18
  644.3 92.2 %all-reduce.60.cloned.1.call-start = ((), (), s32[]{:S(2)}) async-start(), calls=%async_computation.2 | async-start | bytes 589824 | tf_op jit(solution)/shard_map/while/body/eval_jaxpr/psum | solution.py:89
  645.1 12.3 collective-permute-start.1
  761.2 12.1 copy-start.6
  761.2 12.6 copy-start.18
  761.2 92.2 %all-reduce.60.cloned.1.call-start = ((), (), s32[]{:S(2)}) async-start(), calls=%async_computation.2 | async-start | bytes 589824 | tf_op jit(solution)/shard_map/while/body/eval_jaxpr/psum | solution.py:89
  762.1 12.3 collective-permute-start.1
  878.1 12.1 copy-start.6
  878.1 12.6 copy-start.18
  878.1 92.2 %all-reduce.60.cloned.1.call-start = ((), (), s32[]{:S(2)}) async-start(), calls=%async_computation.2 | async-start | bytes 589824 | tf_op jit(solution)/shard_map/while/body/eval_jaxpr/psum | solution.py:89
  879.0 12.3 collective-permute-start.1
  995.0 12.1 copy-start.6
  995.0 12.6 copy-start.18
  995.0 92.2 %all-reduce.60.cloned.1.call-start = ((), (), s32[]{:S(2)}) async-start(), calls=%async_computation.2 | async-start | bytes 589824 | tf_op jit(solution)/shard_map/while/body/eval_jaxpr/psum | solution.py:89
  995.9 12.3 collective-permute-start.1
  1111.9 142.2 %all-reduce.56.cloned.1.call-start = ((), (), s32[]{:S(2)}) async-start(), calls=%async_computation | async-start | bytes 2359296 | tf_op jit(solution)/shard_map/psum | solution.py:100
  (69 other events, 364.4 us)
Sparse Core Ops, SparseCore 0:
  34.6 80.2 all-reduce.57
  139.8 77.5 all-reduce.57
  242.3 77.5 all-reduce.57
  344.9 77.5 all-reduce.57
  447.4 77.5 all-reduce.57
  543.5 76.0 all-reduce.59
  660.9 75.4 all-reduce.59
  777.9 75.4 all-reduce.59
  894.8 75.4 all-reduce.59
  1011.7 75.4 all-reduce.59
Sparse Core Ops, SparseCore 1:
  1115.3 138.9 all-reduce.55
where the time goes:
time: 1270 us; the launch traced here: 1260 us
  waiting for transfers between devices  896 us (71%)
  other arithmetic  241 us (19%)
  matrix products  55.3 us (4%)
  local copies, waits for them, and re-layouts  31 us (2%)
  starting transfers between devices  21.2 us (2%)
  between operations  15.5 us (1%)
    psum x5, waiting for transfers between devices, forward_tick(): lax.psum(partial_value.astype(jnp.bfloat16), 'mp').astype(jnp.float32)  386 us
    psum x5, waiting for transfers between devices, backward_tick(): lax.psum(partial_value.astype(jnp.bfloat16), 'mp').astype(jnp.float32)  351 us
    psum x1, waiting for transfers between devices, shards(): lax.psum(grad_in.astype(jnp.bfloat16), 'dp').astype(jnp.float32)  139 us
    reduce_sum x10, other arithmetic, mix_in(): center = jnp.mean(total, axis=-1, keepdims=True)  60.6 us
    mul x20, other arithmetic, mix_in(): padded[..., first:first + rows, second:second + cols, :]  52.8 us
    add_any x5, other arithmetic, mix_in(): padded[..., first:first + rows, second:second + cols, :]  47.7 us
  transfers between devices with their start and end apart: 21, of which 16 were waited for; matrix products, arithmetic and copies ran while one was open for 9% of the time, Pallas kernels for 0%

commit v1 on v0

v1 whole, which is shorter than its diff:
```python
import functools

import jax
import jax.numpy as jnp
from jax import lax
from jax.experimental import pallas as pl
from jax.experimental.pallas import tpu as pltpu
from jax.sharding import PartitionSpec as P

F32 = jnp.float32
BF16 = jnp.bfloat16

MP = 8
CHIPS = 4
DP = 16
SIDE = 4
DEPTH = 4
ROWS, COLS, TAPS = 8, 12, 7
TOK = ROWS * COLS
HALF = TOK // 2
C = 768
HALF_C = C // 2
HID = 384
LANES = 128
TAP_ROWS = TAPS * TAPS
GAIN, SCALE, INVERSE, PARAM_ROWS = TAP_ROWS, TAP_ROWS + 1, TAP_ROWS + 2, 56
OUT_ROWS = C // DP
PARAMS = pltpu.CompilerParams(vmem_limit_bytes=56 * 1024 * 1024)


def dot(a, b, contract=((1,), (0,))):
    return lax.dot_general(a, b, (contract, ((), ())), preferred_element_type=F32)


def depthwise(values, kernel_ref, lanes, flip):
    values = values.reshape(COLS, ROWS, LANES)
    row = lax.broadcasted_iota(jnp.int32, (COLS, ROWS, LANES), 1)
    edge = jnp.zeros((3, ROWS, LANES), F32)
    total = jnp.zeros((COLS, ROWS, LANES), F32)
    for a in range(TAPS):
        by = a - 3
        moved = values
        if by != 0:
            moved = pltpu.roll(moved, (-by) % ROWS, 1)
            moved = jnp.where((row + by >= 0) & (row + by < ROWS), moved, 0.0)
        wide = jnp.concatenate([edge, moved, edge], axis=0)
        for e in range(TAPS):
            at = a * TAPS + e
            if flip:
                at = TAPS * TAPS - 1 - at
            total = total + wide[e : e + COLS] * kernel_ref[at : at + 1, lanes][None]
    return total.reshape(TOK, LANES)


def each_lanes(body):
    @pl.loop(0, C // LANES)
    def _(tile):
        body(pl.ds(pl.multiple_of(tile * LANES, LANES), LANES))


def gelu_parts(before):
    half = 0.5 * (1.0 + lax.erf(before * (0.5**0.5)))
    density = jnp.exp(-0.5 * before * before) * 0.3989422804014327
    return (before * half).astype(BF16), half + before * density


class Weights:
    AHEAD = 3

    def __init__(self, refs, places, buffer, sems, slope=None, slopes=None):
        self.places = places
        self.copies = []
        for at, (ref, group) in enumerate(zip(refs, places)):
            copies = [pltpu.make_async_copy(ref, buffer.at[group], sems.at[at])]
            if slope is not None:
                copies.append(
                    pltpu.make_async_copy(
                        slope.at[group], slopes.at[group], sems.at[MP + group]
                    )
                )
            self.copies.append(copies)
        for at in range(min(self.AHEAD, len(places))):
            self.start(at)

    def start(self, at):
        for copy in self.copies[at]:
            copy.start()

    def __iter__(self):
        for at, group in enumerate(self.places):
            for copy in self.copies[at]:
                copy.wait()
            if at + self.AHEAD < len(self.places):
                self.start(at + self.AHEAD)
            yield group


class Moves:
    def __init__(self, sems, base):
        self.sems, self.at, self.copies = sems, base, []

    def start(self, source, target):
        copy = pltpu.make_async_copy(source, target, self.sems.at[self.at])
        self.at += 1
        copy.start()
        self.copies.append(copy)

    def wait(self):
        for copy in self.copies:
            copy.wait()
        self.copies = []


def normalise(x, params, conv, normed_out):
    def convolve(lanes):
        conv[:, lanes] = depthwise(x[:, lanes].astype(F32), params, lanes, False)

    each_lanes(convolve)
    values = conv[...]
    mean = jnp.sum(values, axis=1, keepdims=True) * (1.0 / C)
    centered = values - mean
    var = jnp.sum(centered * centered, axis=1, keepdims=True) * (1.0 / C)
    rstd = lax.rsqrt(var + 1e-6)
    normed_out[...] = (centered * rstd * params[GAIN : GAIN + 1]).astype(BF16)
    return rstd


def expand(normed, buffer, group):
    before = dot(normed[:, :HALF_C], buffer[group, :HID, :HID])
    return before + dot(normed[:, HALF_C:], buffer[group, :HID, HID:])


WIDE = jax.ShapeDtypeStruct((TOK, C), BF16)
SUMS = jax.ShapeDtypeStruct((TOK, C), F32)
RSTD = jax.ShapeDtypeStruct((TOK, LANES), F32)
SLOPE = jax.ShapeDtypeStruct((MP, TOK, HID), F32)
SCRATCH = {
    "tokens": pltpu.VMEM((TOK, C), BF16),
    "grads": pltpu.VMEM((TOK, C), BF16),
    "branch": pltpu.VMEM((TOK, C), BF16),
    "normed_here": pltpu.VMEM((TOK, C), BF16),
    "params_here": pltpu.VMEM((PARAM_ROWS, C), F32),
    "rstd_here": pltpu.VMEM((TOK, LANES), F32),
    "total": pltpu.VMEM((TOK, C), F32),
    "slopes": pltpu.VMEM((MP, TOK, HID), F32),
    "buffer": pltpu.VMEM((MP, C, C), BF16),
    "sems": pltpu.SemaphoreType.DMA((40,)),
}


def forward_body(r, weights, places):
    loads, saves = Moves(r["sems"], 2 * MP), Moves(r["sems"], 2 * MP + 8)
    total, normed, params = r["total"], r["normed_here"], r["params_here"]
    first, save = "x" in r, "slope" in r
    if first:
        loads.start(r["x"], r["tokens"])
        loads.start(r["params"], params)
    else:
        loads.start(r["normed_in"], normed)
        loads.start(r["sums_in"], total)
    groups = Weights(weights, places, r["buffer"], r["sems"])
    loads.wait()
    if first:
        rstd = normalise(r["tokens"], params, total, normed)
        saves.start(normed, r["normed"])
        total[...] = jnp.zeros((TOK, C), F32)
    if save:
        r["rstd_here"][...] = jnp.broadcast_to(rstd, (TOK, LANES))
        saves.start(r["rstd_here"], r["rstd"])
    for group in groups:
        hidden, slope = gelu_parts(expand(normed, r["buffer"], group))
        if save:
            r["slopes"][group] = slope
            saves.start(r["slopes"].at[group], r["slope"].at[group])
        part = dot(hidden, r["buffer"][group, HID:, :])
        total[...] += part.astype(BF16).astype(F32)
    if "out" in r:
        x = r["tokens"][...].astype(F32)
        scale = params[SCALE : SCALE + 1]
        r["branch"][...] = (x + scale * total[...]).astype(BF16)
        saves.start(r["branch"], r["out"])
    else:
        saves.start(total, r["sums"])
    saves.wait()


def pull_back(r, groups, rstd):
    g, params, total, branch = r["grads"], r["params_here"], r["total"], r["branch"]
    branch[...] = (g[...].astype(F32) * params[SCALE : SCALE + 1]).astype(BF16)
    total[...] = jnp.zeros((TOK, C), F32)
    for group in groups:
        spread = dot(branch[...], r["buffer"][group, HID:, :], ((1,), (1,)))
        back = (spread * r["slopes"][group]).astype(BF16)
        for half in range(2):
            lanes = slice(half * HALF_C, (half + 1) * HALF_C)
            part = dot(back, r["buffer"][group, :HID, lanes], ((1,), (1,)))
            total[:, lanes] += part.astype(BF16).astype(F32)
    inner = total[...] * params[GAIN : GAIN + 1]
    xhat = r["normed_here"][...].astype(F32) * params[INVERSE : INVERSE + 1]
    first = jnp.sum(inner, axis=1, keepdims=True) * (1.0 / C)
    second = jnp.sum(inner * xhat, axis=1, keepdims=True) * (1.0 / C)
    total[...] = (inner - first - xhat * second) * rstd

    def convolve(lanes):
        value = depthwise(total[:, lanes], params, lanes, True)
        branch[:, lanes] = (g[:, lanes].astype(F32) + value).astype(BF16)

    each_lanes(convolve)


def backward_body(r, weights, places):
    loads, saves = Moves(r["sems"], 2 * MP), Moves(r["sems"], 2 * MP + 8)
    loads.start(r["g"], r["grads"])
    loads.start(r["params"], r["params_here"])
    loads.start(r["normed_in"], r["normed_here"])
    loads.start(r["rstd_in"], r["rstd_here"])
    groups = Weights(
        weights, places, r["buffer"], r["sems"], r["slope_in"], r["slopes"]
    )
    loads.wait()
    pull_back(r, groups, r["rstd_here"][:, :1])
    saves.start(r["branch"], r["out"])
    saves.wait()


def turn_body(r, weights, places):
    loads, saves = Moves(r["sems"], 2 * MP), Moves(r["sems"], 2 * MP + 8)
    loads.start(r["x"], r["tokens"])
    loads.start(r["params"], r["params_here"])
    loads.start(r["g"], r["grads"])
    groups = Weights(weights, places, r["buffer"], r["sems"])
    loads.wait()
    rstd = normalise(r["tokens"], r["params_here"], r["total"], r["normed_here"])
    saves.start(r["normed_here"], r["normed"])
    for group in groups:
        r["slopes"][group] = gelu_parts(expand(r["normed_here"], r["buffer"], group))[1]
    pull_back(r, range(MP), rstd)
    saves.start(r["branch"], r["out"])
    saves.wait()


def block_kernel(body, names, places, sc, *refs):
    r = dict(zip(names, refs))

    @pl.when(sc[0] == 1)
    def _():
        body(r, [r[at] for at in range(len(places))], places)


def call_block(body, active, operands, weights, places, outs):
    anywhere = pl.BlockSpec(memory_space=pl.ANY)
    pieces = len(weights)
    names = list(operands) + list(range(pieces)) + list(outs) + list(SCRATCH)
    results = pl.pallas_call(
        functools.partial(block_kernel, body, names, places),
        in_specs=[pl.BlockSpec(memory_space=pltpu.SMEM)]
        + [anywhere] * (len(operands) + pieces),
        out_specs=[anywhere] * len(outs),
        out_shape=list(outs.values()),
        scratch_shapes=list(SCRATCH.values()),
        cost_estimate=pl.CostEstimate(
            flops=4 * TOK * C * HID * pieces,
            bytes_accessed=2 * C * C * pieces,
            transcendentals=0,
        ),
        compiler_params=PARAMS,
    )(active, *operands.values(), *weights)
    return dict(zip(outs, results))


def grads_kernel(sc, recv, scale, w_in, w_out, keep, give):
    place = sc[0]
    normed = jnp.concatenate([recv[k, :HALF] for k in range(MP)], axis=0)
    g = jnp.concatenate([recv[k, HALF:] for k in range(MP)], axis=0)
    branch = (g.astype(F32) * scale[...]).astype(BF16)
    hidden, slope = gelu_parts(dot(normed, w_in[...]))
    back = (dot(branch, w_out[...], ((1,), (1,))) * slope).astype(BF16)
    for half in range(2):
        lanes = slice(half * HALF_C, (half + 1) * HALF_C)
        gin = dot(normed[:, lanes], back, ((0,), (0,))).astype(BF16)
        gout = dot(branch[:, lanes], hidden, ((0,), (0,))).astype(BF16)
        for part in range(DP // 2):
            rows = slice(part * OUT_ROWS, (part + 1) * OUT_ROWS)
            block = jnp.concatenate([gin[rows], gout[rows]], axis=1)
            owner = half * (DP // 2) + part
            low, high = owner % 2, owner % SIDE // 2
            slot = jnp.where(high == place // 2, 0, SIDE) + owner // SIDE

            @pl.when(low == lax.rem(place, 2))
            def _():
                keep[slot] = block

            @pl.when(low != lax.rem(place, 2))
            def _():
                give[slot] = block


def run_grads(sc, recv, scale, w_in, w_out):
    vmem = pl.BlockSpec(memory_space=pltpu.VMEM)
    eight = jax.ShapeDtypeStruct((DP // 2, OUT_ROWS, 2 * HID), BF16)
    return pl.pallas_call(
        grads_kernel,
        in_specs=[pl.BlockSpec(memory_space=pltpu.SMEM)] + [vmem] * 4,
        out_specs=[vmem] * 2,
        out_shape=[eight, eight],
        compiler_params=PARAMS,
    )(sc, recv, scale, w_in, w_out)


def sum_over_dp(keep, give):
    add = lambda a, b: (a.astype(F32) + b.astype(F32)).astype(BF16)
    trade = lambda v, by: lax.ppermute(v, "dp", [(z, z ^ by) for z in range(DP)])
    value = add(keep, trade(give, 1))
    value = add(value[:SIDE], trade(value[SIDE:], 2))
    groups = [[low + SIDE * k for k in range(SIDE)] for low in range(SIDE)]
    value = lax.all_to_all(value, "dp", 0, 0, axis_index_groups=groups, tiled=True)
    total = jnp.sum(value.astype(F32), axis=0)
    return total.astype(BF16)


def shards(images, token_grads, counts, dw_kernel, ln_gain, w_in, w_out, layer_scale):
    s = lax.axis_index("section")
    j = lax.axis_index("mp")
    chip, core = j // 2, j % 2
    w_in, w_out = w_in[0], w_out[0]

    up = [(i, (i + 2) % MP) for i in range(MP)]
    down = [(i, (i - 2) % MP) for i in range(MP)]
    swap = [(i, i ^ 1) for i in range(MP)]
    move = lambda v, pairs: lax.ppermute(v, "mp", pairs)
    own = jnp.concatenate(
        [jnp.concatenate([w_in[:HALF_C], w_in[HALF_C:]], axis=1), w_out], axis=0
    )
    sample, image = chip // 2, chip % 2
    live = (image < lax.dynamic_index_in_dim(counts, sample, 0, keepdims=False)).astype(BF16)
    one = lambda v: (
        lax.dynamic_index_in_dim(
            v.reshape((CHIPS,) + v.shape[2:]), chip, 0, keepdims=False
        )
        * live
    ).transpose(1, 0, 2).reshape(TOK, C)

    x, g = one(images), one(token_grads)
    params = jnp.concatenate(
        [
            dw_kernel.reshape(TAP_ROWS, C),
            ln_gain,
            layer_scale,
            1.0 / ln_gain,
            jnp.zeros((PARAM_ROWS - TAP_ROWS - 3, C), F32),
        ]
    )
    around = [(i, (i + 2 - 4 * (i % 2)) % MP) for i in range(MP)]
    counter = [(i, (i - 2 + 4 * (i % 2)) % MP) for i in range(MP)]
    first = move(own, around)
    first, own, x, g, params = lax.optimization_barrier((first, own, x, g, params))
    second = move(own, counter)
    third = move(first, around)

    active = [(s == block).astype(jnp.int32)[None] for block in range(DEPTH)]
    send = lambda v, source, to: lax.ppermute(v, "section", [(source, to)])

    result = call_block(
        forward_body,
        active[0],
        dict(x=x, params=params),
        [own, first],
        [0, 1],
        dict(normed=WIDE, sums=SUMS),
    )
    normed = result["normed"]
    swap_own, swap_first, sums = lax.optimization_barrier((own, first, result["sums"]))
    result = call_block(
        forward_body,
        active[0],
        dict(normed_in=normed, sums_in=sums),
        [second, third],
        [0, 1],
        dict(sums=SUMS),
    )
    mixed = result["sums"].astype(BF16)
    mixed = mixed.astype(F32) + move(mixed, swap).astype(F32)
    out = (x.astype(F32) + layer_scale * mixed).astype(BF16)

    weights = [own, first, move(swap_own, swap), move(swap_first, swap)]
    weights += [second, third, move(second, swap), move(third, swap)]
    places = list(range(MP))
    normed_of, saved = [normed], [None]
    for block in range(1, DEPTH - 1):
        result = call_block(
            forward_body,
            active[block],
            dict(x=send(out, block - 1, block), params=params),
            weights,
            places,
            dict(out=WIDE, normed=WIDE, rstd=RSTD, slope=SLOPE),
        )
        out = result["out"]
        normed_of.append(result["normed"])
        saved.append(result)
    result = call_block(
        turn_body,
        active[DEPTH - 1],
        dict(x=send(out, DEPTH - 2, DEPTH - 1), g=g, params=params),
        weights,
        places,
        dict(out=WIDE, normed=WIDE),
    )
    normed_of.append(result["normed"])
    g_of = [g]
    for block in range(DEPTH - 2, 0, -1):
        g = send(result["out"], block + 1, block)
        g_of.append(g)
        kept = saved[block]
        result = call_block(
            backward_body,
            active[block],
            dict(
                g=g,
                params=params,
                normed_in=kept["normed"],
                rstd_in=kept["rstd"],
                slope_in=kept["slope"],
            ),
            weights,
            places,
            dict(out=WIDE),
        )
    g_of.append(send(result["out"], 1, 0))

    pick = lambda values: lax.select_n(s, *values)
    mine = jnp.stack([pick(normed_of), pick(g_of[::-1])])
    mine = jnp.where(core == 0, mine[:, :HALF], mine[:, HALF:]).reshape(TOK, C)
    recv = lax.all_to_all(
        jnp.broadcast_to(mine[None], (MP, TOK, C)), "mp", 0, 0, tiled=True
    )
    z = lax.axis_index("dp")
    place = (z % SIDE).astype(jnp.int32)[None]
    total = sum_over_dp(*run_grads(place, recv, layer_scale, w_in, w_out))
    return total[None, :, :HID], total[None, :, HID:]


def solution(mesh):
    return jax.shard_map(
        shards,
        mesh=mesh,
        in_specs=(
            P("dp", None, None, None, None),
            P("dp", None, None, None, None),
            P("dp"),
            P("section", None, None, None),
            P("section", None),
            P("section", None, "mp"),
            P("section", "mp", None),
            P("section", None),
        ),
        out_specs=(P("section", "dp", "mp"), P("section", "dp", "mp")),
        check_vma=False,
    )
```

time: 1270 us -> 251 us (0.20)
  the two profiles are of different devices: /device:TPU:6 before, /device:TPU:32 now
where the time goes in v1:
time: 251 us; the launch traced here: 250 us
  waiting for transfers between devices  143 us (57%)
  starting transfers between devices  38.4 us (15%)
  blocking collectives  34.7 us (14%)
  Pallas kernels  14.6 us (6%)
  local copies, waits for them, and re-layouts  10.5 us (4%)
  other arithmetic  7.1 us (3%)
    ppermute x6, waiting for transfers between devices, shards(): send = lambda v, source, to: lax.ppermute(v, 'section', [(source, to)])  73.2 us
    all_to_all x1, blocking collectives, sum_over_dp(): lax.all_to_all(value, 'dp', 0, 0, axis_index_groups=groups, tiled=True)  34.7 us
    ppermute x8, waiting for transfers between devices, shards(): move = lambda v, pairs: lax.ppermute(v, 'mp', pairs)  27.7 us
    ppermute x2, waiting for transfers between devices, sum_over_dp(): lax.ppermute(v, 'dp', [(z, z ^ by) for z in range(DP)])  24.7 us
    ppermute x8, starting transfers between devices, shards(): move = lambda v, pairs: lax.ppermute(v, 'mp', pairs)  19.9 us
    all_to_all x1, waiting for transfers between devices, shards(): lax.all_to_all(jnp.broadcast_to(mine[None], (MP, TOK, C)), 'mp', 0, 0, ti...  17.1 us
    pallas_call x7, Pallas kernels, call_block(): pl.pallas_call(functools.partial(block_kernel, body, names, places), in_s...  9.95 us
    ppermute x2, starting transfers between devices, sum_over_dp(): lax.ppermute(v, 'dp', [(z, z ^ by) for z in range(DP)])  8.8 us
  transfers between devices with their start and end apart: 17, of which 8 were waited for; matrix products, arithmetic and copies ran while one was open for 3% of the time, Pallas kernels for 3%

profile of v1, /device:TPU:32, one launch (start us, length us, event | category | flops | bytes accessed | tf_op | source)
XLA Modules:
  0.0 249.8 jit_solution(3715926955735057419)
XLA Ops:
  0.6 1.2 slice_bitcast_fusion.1
  2.0 3.5 %collective-permute-start = (bf16[768,768]{1,0:T(8,128)(2,1)S(1)}, bf16[768,768]{1,0:T(8,128)(2,1)}, u32[]{:S(2)}, u32[]{:S(2)}) collective-permute-start(bf16[768,768]{1,0:T(8,128)(2,1)S(1)} %pad_maximum_fusion.refs_2_.refs_3_.refs_5_), channel_id=1, source_target_pairs={{0,2},{1,7},{2,4},{3,1},{4,6},{5,3},{6,0},{7,5},{8,10},{9,15},{10,... | collective-permute-start | bytes 3538952 | tf_op jit(solution)/shard_map/ppermute | solution.py:330
  5.5 0.6 dynamic_slice.12
  6.8 0.4 reduce.1
  7.3 2.0 concatenate.11.refs_1_.refs_2_
  9.3 1.7 multiply_bitcast_fusion
  11.0 10.4 %collective-permute-done.refs_3_.refs_4_.refs_6_ = bf16[768,768]{1,0:T(8,128)(2,1)} collective-permute-done((bf16[768,768]{1,0:T(8,128)(2,1)S(1)}, bf16[768,768]{1,0:T(8,128)(2,1)}, u32[]{:S(2)}, u32[]{:S(2)}) %collective-permute-start) | collective-permute-done | bytes 1179680 | tf_op jit(solution)/shard_map/ppermute | solution.py:330
  21.4 3.7 %collective-permute-start.1 = (bf16[768,768]{1,0:T(8,128)(2,1)S(1)}, bf16[768,768]{1,0:T(8,128)(2,1)S(1)}, u32[]{:S(2)}, u32[]{:S(2)}) collective-permute-start(bf16[768,768]{1,0:T(8,128)(2,1)S(1)} %pad_maximum_fusion.refs_2_.refs_3_.refs_5_), channel_id=1, source_target_pairs={{0,6},{1,3},{2,0},{3,5},{4,2},{5,7},{6,4},{7,1},{8,14},{9,11},{10,... | collective-permute-start | bytes 3538952 | tf_op jit(solution)/shard_map/ppermute | solution.py:330
  25.1 2.1 collective-permute-start.2
  27.3 4.6 %shard_map.95 = (bf16[96,768]{1,0:T(8,128)(2,1)}, f32[96,768]{1,0:T(8,128)}) custom-call(s32[1]{0:T(128)} %bitcast.1.sc, bf16[96,768]{1,0:T(8,128)(2,1)} %get-tuple-element.24.refs_0_, f32[56,768]{1,0:T(8,128)} %concatenate.11.refs_1_.refs_2_, bf16[768,768]{1,0:T(8,128)(2,1)} %copy-done, bf16[768,768]{1,0:T(8,128)(2,1)} %collective-permute-done.refs_3_.refs_4_.refs_6_), custom_call_target="tpu_custom_call" | custom-call | flops 226492416 | bytes 2359296 | tf_op jit(solution)/shard_map/pallas_call | solution.py:254
  31.9 1.9 collective-permute-start.5
  33.8 2.4 collective-permute-start.6
  36.2 15.7 %collective-permute-done.1.refs_2_.refs_6_.refs_7_.refs_9_ = bf16[768,768]{1,0:T(8,128)(2,1)S(1)} collective-permute-done((bf16[768,768]{1,0:T(8,128)(2,1)S(1)}, bf16[768,768]{1,0:T(8,128)(2,1)S(1)}, u32[]{:S(2)}, u32[]{:S(2)}) %collective-permute-start.1) | collective-permute-done | bytes 1179680 | tf_op jit(solution)/shard_map/ppermute | solution.py:330
  51.9 1.9 collective-permute-start.7
  53.8 2.4 collective-permute-start.8
  56.3 3.5 %shard_map.96 = f32[96,768]{1,0:T(8,128)} custom-call(s32[1]{0:T(128)} %bitcast.1.sc, bf16[96,768]{1,0:T(8,128)(2,1)} %get-tuple-element.28.refs_0_, f32[96,768]{1,0:T(8,128)} %get-tuple-element.30.refs_1_, bf16[768,768]{1,0:T(8,128)(2,1)} %copy-done.1, bf16[768,768]{1,0:T(8,128)(2,1)} %copy-done.2), custom_call_target="tpu_custom_call" | custom-call | flops 226492416 | bytes 2359296 | tf_op jit(solution)/shard_map/pallas_call | solution.py:254
  59.8 1.6 convert_element_type.44
  61.5 1.9 collective-permute-start.3
  63.4 1.7 collective-permute-done.3
  65.1 1.8 add_convert_fusion.2
  66.9 1.9 collective-permute-start.4
  68.8 3.3 %collective-permute-done.4.refs_0_ = bf16[96,768]{1,0:T(8,128)(2,1)} collective-permute-done((bf16[96,768]{1,0:T(8,128)(2,1)}, bf16[96,768]{1,0:T(8,128)(2,1)}, u32[]{:S(2)}, u32[]{:S(2)}) %collective-permute-start.4) | collective-permute-done | bytes 147488 | tf_op jit(solution)/shard_map/ppermute | solution.py:361
  72.2 1.1 copy-done.3
  73.3 0.4 shard_map.97
  73.6 0.7 collective-permute-start.9
  74.3 0.7 copy-done.15
  75.4 0.7 collective-permute-start.10
  76.1 0.7 copy-done.16
  76.7 0.4 shard_map.99
  77.1 0.7 collective-permute-start.11
  77.8 0.7 copy-done.10
  78.8 0.7 collective-permute-start.12
  79.5 0.6 copy-done.12
  80.2 0.4 shard_map.101
  80.6 1.3 collective-permute-start.13
  82.0 69.9 %collective-permute-done.13 = bf16[96,768]{1,0:T(8,128)(2,1)S(1)} collective-permute-done((bf16[96,768]{1,0:T(8,128)(2,1)}, bf16[96,768]{1,0:T(8,128)(2,1)S(1)}, u32[]{:S(2)}, u32[]{:S(2)}) %collective-permute-start.13) | collective-permute-done | bytes 147488 | tf_op jit(solution)/shard_map/ppermute | solution.py:361
  151.9 1.1 broadcast_in_dim.50
  153.0 3.8 %all-to-all-start = ((bf16[8,96,768]{2,1,0:T(8,128)(2,1)}), bf16[8,96,768]{2,1,0:T(8,128)(2,1)S(1)}, u32[]{:S(2)}, u32[]{:S(2)}) async-start(bf16[8,96,768]{2,1,0:T(8,128)(2,1)} %broadcast_in_dim.50), calls=%async_computation | async-start | bytes 2359296 | tf_op jit(solution)/shard_map/all_to_all | solution.py:434
  156.8 17.1 %all-to-all-done.recv = bf16[8,96,768]{2,1,0:T(8,128)(2,1)S(1)} async-done(((bf16[8,96,768]{2,1,0:T(8,128)(2,1)}), bf16[8,96,768]{2,1,0:T(8,128)(2,1)S(1)}, u32[]{:S(2)}, u32[]{:S(2)}) %all-to-all-start) | async-done | bytes 1179680 | tf_op jit(solution)/shard_map/all_to_all | solution.py:434
  173.9 1.0 copy-done.4
  174.9 4.6 %shard_map.102 = (bf16[8,48,768]{2,1,0:T(8,128)(2,1)}, bf16[8,48,768]{2,1,0:T(8,128)(2,1)}) custom-call(s32[1]{0:T(128)} %bitcast.sc, bf16[8,96,768]{2,1,0:T(8,128)(2,1)} %copy-done.4, f32[1,768]{1,0:T(1,128)} %scale.1, bf16[768,384]{1,0:T(8,128)(2,1)} %bitcast.35, bf16[384,768]{1,0:T(8,128)(2,1)} %bitcast.36), custom_call_target="tpu_custom_call" | custom-call | tf_op jit(solution)/shard_map/pallas_call | solution.py:301
  179.5 4.1 %collective-permute-start.14 = (bf16[8,48,768]{2,1,0:T(8,128)(2,1)}, bf16[8,48,768]{2,1,0:T(8,128)(2,1)S(1)}, u32[]{:S(2)}, u32[]{:S(2)}) collective-permute-start(bf16[8,48,768]{2,1,0:T(8,128)(2,1)} %get-tuple-element.45), channel_id=1, source_target_pairs={{0,8},{8,0},{16,24},{24,16},{32,40},{40,32},{48,56},{56,48},{64,72... | collective-permute-start | bytes 1769480 | tf_op jit(solution)/shard_map/ppermute | solution.py:312
  183.7 13.3 %collective-permute-done.14 = bf16[8,48,768]{2,1,0:T(8,128)(2,1)S(1)} collective-permute-done((bf16[8,48,768]{2,1,0:T(8,128)(2,1)}, bf16[8,48,768]{2,1,0:T(8,128)(2,1)S(1)}, u32[]{:S(2)}, u32[]{:S(2)}) %collective-permute-start.14) | collective-permute-done | bytes 589856 | tf_op jit(solution)/shard_map/ppermute | solution.py:312
  197.0 1.2 add_convert_fusion
  198.2 4.7 %collective-permute-start.15 = (bf16[4,48,768]{2,1,0:T(8,128)(2,1)S(1)}, bf16[4,48,768]{2,1,0:T(8,128)(2,1)S(1)}, u32[]{:S(2)}, u32[]{:S(2)}) collective-permute-start(bf16[4,48,768]{2,1,0:T(8,128)(2,1)S(1)} %slice.43), channel_id=1, source_target_pairs={{0,16},{8,24},{16,0},{24,8},{32,48},{40,56},{48,32},{56,40},{64,80... | collective-permute-start | bytes 884744 | tf_op jit(solution)/shard_map/ppermute | solution.py:312
  202.9 11.4 %collective-permute-done.15 = bf16[4,48,768]{2,1,0:T(8,128)(2,1)S(1)} collective-permute-done((bf16[4,48,768]{2,1,0:T(8,128)(2,1)S(1)}, bf16[4,48,768]{2,1,0:T(8,128)(2,1)S(1)}, u32[]{:S(2)}, u32[]{:S(2)}) %collective-permute-start.15) | collective-permute-done | bytes 294944 | tf_op jit(solution)/shard_map/ppermute | solution.py:312
  214.4 34.7 %all_to_all.10 = bf16[4,48,768]{2,1,0:T(8,128)(2,1)S(1)} all-to-all(bf16[4,48,768]{2,1,0:T(8,128)(2,1)S(1)} %add_convert_fusion.1), channel_id=1, replica_groups={{0,32,64,96},{8,40,72,104},{16,48,80,112},{24,56,88,120},{1,33,65,97},{..., dimensions={0} | all-to-all | bytes 589824 | tf_op jit(solution)/shard_map/all_to_all | solution.py:316
  249.2 0.6 slice_bitcast_fusion.2
  (56 shorter events, 1.2 us)
Async XLA Ops:
  0.6 1.2 copy-start.5
  1.9 3.7 %copy-start.19 = (s32[2]{0:T(128)S(1)}, s32[2]{0:T(128)}, u32[]{:S(2)}) copy-start(s32[2]{0:T(128)} %param.10) | copy-start | bytes 28
  1.9 4.9 %copy-start.13 = (f32[1,7,7,768]{3,0,2,1:T(1,128)S(1)}, f32[1,7,7,768]{3,0,2,1:T(1,128)}, u32[]{:S(2)}) copy-start(f32[1,7,7,768]{3,0,2,1:T(1,128)} %param.11) | copy-start | bytes 451588
  1.9 5.3 %copy-start.18 = (f32[1,768]{1,0:T(1,128)S(1)}, f32[1,768]{1,0:T(1,128)}, u32[]{:S(2)}) copy-start(f32[1,768]{1,0:T(1,128)} %param.12) | copy-start | bytes 9220
  1.9 5.4 %copy-start.17 = (f32[1,768]{1,0:T(1,128)S(1)}, f32[1,768]{1,0:T(1,128)}, u32[]{:S(2)}) copy-start(f32[1,768]{1,0:T(1,128)} %scale.1) | copy-start | bytes 9220
  2.0 25.3 %copy-start = (bf16[768,768]{1,0:T(8,128)(2,1)}, bf16[768,768]{1,0:T(8,128)(2,1)S(1)}, u32[]{:S(2)}) copy-start(bf16[768,768]{1,0:T(8,128)(2,1)S(1)} %pad_maximum_fusion.refs_2_.refs_3_.refs_5_) | copy-start | bytes 3538948
  2.0 19.4 %collective-permute-start = (bf16[768,768]{1,0:T(8,128)(2,1)S(1)}, bf16[768,768]{1,0:T(8,128)(2,1)}, u32[]{:S(2)}, u32[]{:S(2)}) collective-permute-start(bf16[768,768]{1,0:T(8,128)(2,1)S(1)} %pad_maximum_fusion.refs_2_.refs_3_.refs_5_), channel_id=1, source_target_pairs={{0,2},{1,7},{2,4},{3,1},{4,6},{5,3},{6,0},{7,5},{8,10},{9,15},{10,... | collective-permute-start | bytes 3538952 | tf_op jit(solution)/shard_map/ppermute | solution.py:330
  21.4 30.5 %collective-permute-start.1 = (bf16[768,768]{1,0:T(8,128)(2,1)S(1)}, bf16[768,768]{1,0:T(8,128)(2,1)S(1)}, u32[]{:S(2)}, u32[]{:S(2)}) collective-permute-start(bf16[768,768]{1,0:T(8,128)(2,1)S(1)} %pad_maximum_fusion.refs_2_.refs_3_.refs_5_), channel_id=1, source_target_pairs={{0,6},{1,3},{2,0},{3,5},{4,2},{5,7},{6,4},{7,1},{8,14},{9,11},{10,... | collective-permute-start | bytes 3538952 | tf_op jit(solution)/shard_map/ppermute | solution.py:330
  25.1 28.7 %collective-permute-start.2 = (bf16[768,768]{1,0:T(8,128)(2,1)}, bf16[768,768]{1,0:T(8,128)(2,1)S(1)}, u32[]{:S(2)}, u32[]{:S(2)}) collective-permute-start(bf16[768,768]{1,0:T(8,128)(2,1)} %collective-permute-done.refs_3_.refs_4_.refs_6_), channel_id=1, source_target_pairs={{0,2},{1,7},{2,4},{3,1},{4,6},{5,3},{6,0},{7,5},{8,10},{9,15},{10,... | collective-permute-start | bytes 3538952 | tf_op jit(solution)/shard_map/ppermute | solution.py:330
  31.9 36.9 %collective-permute-start.5 = (bf16[768,768]{1,0:T(8,128)(2,1)}, bf16[768,768]{1,0:T(8,128)(2,1)}, u32[]{:S(2)}, u32[]{:S(2)}) collective-permute-start(bf16[768,768]{1,0:T(8,128)(2,1)} %copy-done), channel_id=1, source_target_pairs={{0,1},{1,0},{2,3},{3,2},{4,5},{5,4},{6,7},{7,6},{8,9},{9,8},{10,11... | collective-permute-start | bytes 3538952 | tf_op jit(solution)/shard_map/ppermute | solution.py:330
  33.8 35.0 %collective-permute-start.6 = (bf16[768,768]{1,0:T(8,128)(2,1)}, bf16[768,768]{1,0:T(8,128)(2,1)}, u32[]{:S(2)}, u32[]{:S(2)}) collective-permute-start(bf16[768,768]{1,0:T(8,128)(2,1)} %collective-permute-done.refs_3_.refs_4_.refs_6_), channel_id=1, source_target_pairs={{0,1},{1,0},{2,3},{3,2},{4,5},{5,4},{6,7},{7,6},{8,9},{9,8},{10,11... | collective-permute-start | bytes 3538952 | tf_op jit(solution)/shard_map/ppermute | solution.py:330
  51.9 4.4 %copy-start.1 = (bf16[768,768]{1,0:T(8,128)(2,1)}, bf16[768,768]{1,0:T(8,128)(2,1)S(1)}, u32[]{:S(2)}) copy-start(bf16[768,768]{1,0:T(8,128)(2,1)S(1)} %collective-permute-done.1.refs_2_.refs_6_.refs_7_.refs_9_) | copy-start | bytes 3538948
  51.9 20.3 %collective-permute-start.7 = (bf16[768,768]{1,0:T(8,128)(2,1)S(1)}, bf16[768,768]{1,0:T(8,128)(2,1)S(1)}, u32[]{:S(2)}, u32[]{:S(2)}) collective-permute-start(bf16[768,768]{1,0:T(8,128)(2,1)S(1)} %collective-permute-done.1.refs_2_.refs_6_.refs_7_.refs_9_), channel_id=1, source_target_pairs={{0,1},{1,0},{2,3},{3,2},{4,5},{5,4},{6,7},{7,6},{8,9},{9,8},{10,11... | collective-permute-start | bytes 3538952 | tf_op jit(solution)/shard_map/ppermute | solution.py:330
  53.8 2.4 copy-start.2
  53.8 18.3 %collective-permute-start.8 = (bf16[768,768]{1,0:T(8,128)(2,1)S(1)}, bf16[768,768]{1,0:T(8,128)(2,1)}, u32[]{:S(2)}, u32[]{:S(2)}) collective-permute-start(bf16[768,768]{1,0:T(8,128)(2,1)S(1)} %collective-permute-done.2.refs_3_.refs_7_.refs_8_.refs_10_), channel_id=1, source_target_pairs={{0,1},{1,0},{2,3},{3,2},{4,5},{5,4},{6,7},{7,6},{8,9},{9,8},{10,11... | collective-permute-start | bytes 3538952 | tf_op jit(solution)/shard_map/ppermute | solution.py:330
  61.5 3.6 %collective-permute-start.3 = (bf16[96,768]{1,0:T(8,128)(2,1)}, bf16[96,768]{1,0:T(8,128)(2,1)}, u32[]{:S(2)}, u32[]{:S(2)}) collective-permute-start(bf16[96,768]{1,0:T(8,128)(2,1)} %convert_element_type.44), channel_id=1, source_target_pairs={{0,1},{1,0},{2,3},{3,2},{4,5},{5,4},{6,7},{7,6},{8,9},{9,8},{10,11... | collective-permute-start | bytes 442376 | tf_op jit(solution)/shard_map/ppermute | solution.py:330
  66.9 5.3 %collective-permute-start.4 = (bf16[96,768]{1,0:T(8,128)(2,1)}, bf16[96,768]{1,0:T(8,128)(2,1)}, u32[]{:S(2)}, u32[]{:S(2)}) collective-permute-start(bf16[96,768]{1,0:T(8,128)(2,1)} %add_convert_fusion.2), channel_id=1, source_target_pairs={{0,128},{1,129},{2,130},{3,131},{4,132},{5,133},{6,134},{7,135},{8... | collective-permute-start | bytes 442376 | tf_op jit(solution)/shard_map/ppermute | solution.py:361
  72.2 1.1 copy-start.3
  73.6 0.7 collective-permute-start.9
  74.3 0.7 copy-start.15
  75.4 0.7 collective-permute-start.10
  76.0 0.7 copy-start.16
  77.1 0.7 collective-permute-start.11
  77.8 0.7 copy-start.10
  78.8 0.7 collective-permute-start.12
  79.5 0.7 copy-start.12
  80.2 1.7 copy-start.7
  80.2 1.7 copy-start.8
  80.2 1.7 copy-start.9
  80.2 1.7 copy-start.14
  80.2 71.6 %copy-start.6 = (bf16[96,768]{1,0:T(8,128)(2,1)S(1)}, bf16[96,768]{1,0:T(8,128)(2,1)}, u32[]{:S(2)}) copy-start(bf16[96,768]{1,0:T(8,128)(2,1)} %get-tuple-element.37.refs_1_) | copy-start | bytes 442372
  80.2 71.6 %copy-start.11 = (bf16[96,768]{1,0:T(8,128)(2,1)S(1)}, bf16[96,768]{1,0:T(8,128)(2,1)}, u32[]{:S(2)}) copy-start(bf16[96,768]{1,0:T(8,128)(2,1)} %copy-done.10) | copy-start | bytes 442372
  80.6 71.2 %collective-permute-start.13 = (bf16[96,768]{1,0:T(8,128)(2,1)}, bf16[96,768]{1,0:T(8,128)(2,1)S(1)}, u32[]{:S(2)}, u32[]{:S(2)}) collective-permute-start(bf16[96,768]{1,0:T(8,128)(2,1)} %shard_map.101), channel_id=1, source_target_pairs={{128,0},{129,1},{130,2},{131,3},{132,4},{133,5},{134,6},{135,7},{1... | collective-permute-start | bytes 442376 | tf_op jit(solution)/shard_map/ppermute | solution.py:361
  153.0 20.9 %all-to-all-start = ((bf16[8,96,768]{2,1,0:T(8,128)(2,1)}), bf16[8,96,768]{2,1,0:T(8,128)(2,1)S(1)}, u32[]{:S(2)}, u32[]{:S(2)}) async-start(bf16[8,96,768]{2,1,0:T(8,128)(2,1)} %broadcast_in_dim.50), calls=%async_computation | async-start | bytes 2359296 | tf_op jit(solution)/shard_map/all_to_all | solution.py:434
  173.9 1.0 copy-start.4
  179.5 17.4 %collective-permute-start.14 = (bf16[8,48,768]{2,1,0:T(8,128)(2,1)}, bf16[8,48,768]{2,1,0:T(8,128)(2,1)S(1)}, u32[]{:S(2)}, u32[]{:S(2)}) collective-permute-start(bf16[8,48,768]{2,1,0:T(8,128)(2,1)} %get-tuple-element.45), channel_id=1, source_target_pairs={{0,8},{8,0},{16,24},{24,16},{32,40},{40,32},{48,56},{56,48},{64,72... | collective-permute-start | bytes 1769480 | tf_op jit(solution)/shard_map/ppermute | solution.py:312
  198.2 16.1 %collective-permute-start.15 = (bf16[4,48,768]{2,1,0:T(8,128)(2,1)S(1)}, bf16[4,48,768]{2,1,0:T(8,128)(2,1)S(1)}, u32[]{:S(2)}, u32[]{:S(2)}) collective-permute-start(bf16[4,48,768]{2,1,0:T(8,128)(2,1)S(1)} %slice.43), channel_id=1, source_target_pairs={{0,16},{8,24},{16,0},{24,8},{32,48},{40,56},{48,32},{56,40},{64,80... | collective-permute-start | bytes 884744 | tf_op jit(solution)/shard_map/ppermute | solution.py:312

commit v2 on v1

--- a/solution.py
+++ b/solution.py
@@ -26,6 +26,7 @@
 GAIN, SCALE, INVERSE, PARAM_ROWS = TAP_ROWS, TAP_ROWS + 1, TAP_ROWS + 2, 56
 OUT_ROWS = C // DP
 PARAMS = pltpu.CompilerParams(vmem_limit_bytes=56 * 1024 * 1024)
+SMALL = pltpu.CompilerParams(vmem_limit_bytes=24 * 1024 * 1024)
 
 
 def dot(a, b, contract=((1,), (0,))):
@@ -179,8 +180,26 @@
         scale = params[SCALE : SCALE + 1]
         r["branch"][...] = (x + scale * total[...]).astype(BF16)
         saves.start(r["branch"], r["out"])
+    elif "part" in r:
+        r["branch"][...] = total[...].astype(BF16)
+        saves.start(r["branch"], r["part"])
     else:
         saves.start(total, r["sums"])
+    saves.wait()
+
+
+def join_body(r, weights, places):
+    loads, saves = Moves(r["sems"], 2 * MP), Moves(r["sems"], 2 * MP + 8)
+    loads.start(r["x"], r["tokens"])
+    loads.start(r["params"], r["params_here"])
+    loads.start(r["mine"], r["grads"])
+    loads.start(r["other"], r["normed_here"])
+    loads.wait()
+    mixed = r["grads"][...].astype(F32) + r["normed_here"][...].astype(F32)
+    x = r["tokens"][...].astype(F32)
+    scale = r["params_here"][SCALE : SCALE + 1]
+    r["branch"][...] = (x + scale * mixed).astype(BF16)
+    saves.start(r["branch"], r["out"])
     saves.wait()
 
 
@@ -259,8 +278,8 @@
         out_shape=list(outs.values()),
         scratch_shapes=list(SCRATCH.values()),
         cost_estimate=pl.CostEstimate(
-            flops=4 * TOK * C * HID * pieces,
-            bytes_accessed=2 * C * C * pieces,
+            flops=4 * TOK * C * HID * max(pieces, 1),
+            bytes_accessed=2 * C * C * max(pieces, 1),
             transcendentals=0,
         ),
         compiler_params=PARAMS,
@@ -268,10 +287,11 @@
     return dict(zip(outs, results))
 
 
-def grads_kernel(sc, recv, scale, w_in, w_out, keep, give):
-    place = sc[0]
-    normed = jnp.concatenate([recv[k, :HALF] for k in range(MP)], axis=0)
-    g = jnp.concatenate([recv[k, HALF:] for k in range(MP)], axis=0)
+def grads_kernel(sc, recv, other, scale, w_in, w_out, keep, give):
+    early_here, late_here, core = sc[0], sc[1], sc[2]
+    shares = [ref[k] for ref in (recv, other) for k in range(CHIPS)]
+    normed = jnp.concatenate([share[:HALF] for share in shares], axis=0)
+    g = jnp.concatenate([share[HALF:] for share in shares], axis=0)
     branch = (g.astype(F32) * scale[...]).astype(BF16)
     hidden, slope = gelu_parts(dot(normed, w_in[...]))
     back = (dot(branch, w_out[...], ((1,), (1,))) * slope).astype(BF16)
@@ -284,37 +304,48 @@
             block = jnp.concatenate([gin[rows], gout[rows]], axis=1)
             owner = half * (DP // 2) + part
             low, high = owner % 2, owner % SIDE // 2
-            slot = jnp.where(high == place // 2, 0, SIDE) + owner // SIDE
-
-            @pl.when(low == lax.rem(place, 2))
+            early = jnp.where(core == 0, low, high)
+            late = jnp.where(core == 0, high, low)
+            slot = jnp.where(late == late_here, 0, SIDE) + owner // SIDE
+
+            @pl.when(early == early_here)
             def _():
                 keep[slot] = block
 
-            @pl.when(low != lax.rem(place, 2))
+            @pl.when(early != early_here)
             def _():
                 give[slot] = block
 
 
-def run_grads(sc, recv, scale, w_in, w_out):
+def run_grads(sc, recv, other, scale, w_in, w_out):
     vmem = pl.BlockSpec(memory_space=pltpu.VMEM)
     eight = jax.ShapeDtypeStruct((DP // 2, OUT_ROWS, 2 * HID), BF16)
     return pl.pallas_call(
         grads_kernel,
-        in_specs=[pl.BlockSpec(memory_space=pltpu.SMEM)] + [vmem] * 4,
+        in_specs=[pl.BlockSpec(memory_space=pltpu.SMEM)] + [vmem] * 5,
         out_specs=[vmem] * 2,
         out_shape=[eight, eight],
-        compiler_params=PARAMS,
-    )(sc, recv, scale, w_in, w_out)
+        compiler_params=SMALL,
+    )(sc, recv, other, scale, w_in, w_out)
 
 
 def sum_over_dp(keep, give):
     add = lambda a, b: (a.astype(F32) + b.astype(F32)).astype(BF16)
-    trade = lambda v, by: lax.ppermute(v, "dp", [(z, z ^ by) for z in range(DP)])
-    value = add(keep, trade(give, 1))
-    value = add(value[:SIDE], trade(value[SIDE:], 2))
-    groups = [[low + SIDE * k for k in range(SIDE)] for low in range(SIDE)]
-    value = lax.all_to_all(value, "dp", 0, 0, axis_index_groups=groups, tiled=True)
-    total = jnp.sum(value.astype(F32), axis=0)
+    trade = lambda v, by: lax.ppermute(
+        v,
+        ("dp", "mp"),
+        [(z * MP + j, (z ^ by[j % 2]) * MP + j) for z in range(DP) for j in range(MP)],
+    )
+    value = add(keep, trade(give, (1, 2)))
+    value = add(value[:SIDE], trade(value[SIDE:], (2, 1)))
+    here = lax.axis_index("dp") // SIDE
+    block = lambda ahead: lax.dynamic_index_in_dim(
+        value, (here + ahead) % SIDE, 0, keepdims=False
+    )
+    total = block(0).astype(F32)
+    for ahead in range(1, SIDE):
+        pairs = [(z, (z + ahead * SIDE) % DP) for z in range(DP)]
+        total = total + lax.ppermute(block(ahead), "dp", pairs).astype(F32)
     return total.astype(BF16)
 
 
@@ -376,14 +407,21 @@
         dict(normed_in=normed, sums_in=sums),
         [second, third],
         [0, 1],
-        dict(sums=SUMS),
-    )
-    mixed = result["sums"].astype(BF16)
-    mixed = mixed.astype(F32) + move(mixed, swap).astype(F32)
-    out = (x.astype(F32) + layer_scale * mixed).astype(BF16)
+        dict(part=WIDE),
+    )
+    swap_second, swap_third, part = lax.optimization_barrier((second, third, result["part"]))
+    result = call_block(
+        join_body,
+        active[0],
+        dict(x=x, params=params, mine=part, other=move(part, swap)),
+        [],
+        [],
+        dict(out=WIDE),
+    )
+    out = result["out"]
 
     weights = [own, first, move(swap_own, swap), move(swap_first, swap)]
-    weights += [second, third, move(second, swap), move(third, swap)]
+    weights += [second, third, move(swap_second, swap), move(swap_third, swap)]
     places = list(range(MP))
     normed_of, saved = [normed], [None]
     for block in range(1, DEPTH - 1):
@@ -432,11 +470,19 @@
     mine = jnp.stack([pick(normed_of), pick(g_of[::-1])])
     mine = jnp.where(core == 0, mine[:, :HALF], mine[:, HALF:]).reshape(TOK, C)
     recv = lax.all_to_all(
-        jnp.broadcast_to(mine[None], (MP, TOK, C)), "mp", 0, 0, tiled=True
-    )
+        jnp.broadcast_to(mine[None], (CHIPS, TOK, C)),
+        "mp",
+        0,
+        0,
+        axis_index_groups=[list(range(0, MP, 2)), list(range(1, MP, 2))],
+        tiled=True,
+    )
+    other = move(recv, swap)
     z = lax.axis_index("dp")
-    place = (z % SIDE).astype(jnp.int32)[None]
-    total = sum_over_dp(*run_grads(place, recv, layer_scale, w_in, w_out))
+    low, high = z % 2, z % SIDE // 2
+    place = [jnp.where(core == 0, low, high), jnp.where(core == 0, high, low), core]
+    place = jnp.stack([jnp.asarray(v, jnp.int32) for v in place])
+    total = sum_over_dp(*run_grads(place, recv, other, layer_scale, w_in, w_out))
     return total[None, :, :HID], total[None, :, HID:]
 
 

time: 251 us -> 233 us (0.928)
  the two profiles are of different devices: /device:TPU:32 before, /device:TPU:8 now
where the time goes in v2:
time: 233 us; the launch traced here: 232 us
  waiting for transfers between devices  133 us (57%)
  starting transfers between devices  58 us (25%)
  Pallas kernels  14.7 us (6%)
  blocking collectives  12 us (5%)
  local copies, waits for them, and re-layouts  10.4 us (4%)
  other arithmetic  2.64 us (1%)
    ppermute x6, waiting for transfers between devices, shards(): send = lambda v, source, to: lax.ppermute(v, 'section', [(source, to)])  73.9 us
    ppermute x9, waiting for transfers between devices, shards(): move = lambda v, pairs: lax.ppermute(v, 'mp', pairs)  28.3 us
    ppermute x2, waiting for transfers between devices, sum_over_dp(): lax.ppermute(v, ('dp', 'mp'), [(z * MP + j, (z ^ by[j % 2]) * MP + j) for...  25.1 us
    ppermute x3, starting transfers between devices, sum_over_dp(): total = total + lax.ppermute(block(ahead), 'dp', pairs).astype(F32)  24 us
    ppermute x9, starting transfers between devices, shards(): move = lambda v, pairs: lax.ppermute(v, 'mp', pairs)  23.8 us
    pallas_call x8, Pallas kernels, call_block(): pl.pallas_call(functools.partial(block_kernel, body, names, places), in_s...  12.1 us
    all_to_all x1, blocking collectives, shards(): lax.all_to_all(jnp.broadcast_to(mine[None], (CHIPS, TOK, C)), 'mp', 0, 0,...  12 us
    unnamed x44, local copies, waits for them, and re-layouts  5.85 us
  transfers between devices with their start and end apart: 20, of which 10 were waited for; matrix products, arithmetic and copies ran while one was open for 2% of the time, Pallas kernels for 4%

profile of v2, /device:TPU:8, one launch (start us, length us, event | category | flops | bytes accessed | tf_op | source)
XLA Modules:
  0.0 232.3 jit_solution(14188678538099641407)
XLA Ops:
  0.6 1.2 slice_bitcast_fusion.1
  2.0 3.5 %collective-permute-start = (bf16[768,768]{1,0:T(8,128)(2,1)S(1)}, bf16[768,768]{1,0:T(8,128)(2,1)}, u32[]{:S(2)}, u32[]{:S(2)}) collective-permute-start(bf16[768,768]{1,0:T(8,128)(2,1)S(1)} %pad_maximum_fusion.refs_2_.refs_3_.refs_5_), channel_id=1, source_target_pairs={{0,2},{1,7},{2,4},{3,1},{4,6},{5,3},{6,0},{7,5},{8,10},{9,15},{10,... | collective-permute-start | bytes 3538952 | tf_op jit(solution)/shard_map/ppermute | solution.py:361
  5.5 0.6 dynamic_slice.25
  7.3 2.0 concatenate.11.refs_1_.refs_2_
  9.3 1.7 multiply_bitcast_fusion
  11.0 13.2 %collective-permute-done.refs_3_.refs_4_.refs_6_ = bf16[768,768]{1,0:T(8,128)(2,1)} collective-permute-done((bf16[768,768]{1,0:T(8,128)(2,1)S(1)}, bf16[768,768]{1,0:T(8,128)(2,1)}, u32[]{:S(2)}, u32[]{:S(2)}) %collective-permute-start) | collective-permute-done | bytes 1179680 | tf_op jit(solution)/shard_map/ppermute | solution.py:361
  24.2 5.7 %collective-permute-start.1 = (bf16[768,768]{1,0:T(8,128)(2,1)S(1)}, bf16[768,768]{1,0:T(8,128)(2,1)S(1)}, u32[]{:S(2)}, u32[]{:S(2)}) collective-permute-start(bf16[768,768]{1,0:T(8,128)(2,1)S(1)} %pad_maximum_fusion.refs_2_.refs_3_.refs_5_), channel_id=1, source_target_pairs={{0,6},{1,3},{2,0},{3,5},{4,2},{5,7},{6,4},{7,1},{8,14},{9,11},{10,... | collective-permute-start | bytes 3538952 | tf_op jit(solution)/shard_map/ppermute | solution.py:361
  29.9 1.9 collective-permute-start.2
  31.8 4.6 %shard_map.95 = (bf16[96,768]{1,0:T(8,128)(2,1)}, f32[96,768]{1,0:T(8,128)}) custom-call(s32[1]{0:T(128)} %bitcast.3.sc, bf16[96,768]{1,0:T(8,128)(2,1)} %get-tuple-element.27.refs_0_, f32[56,768]{1,0:T(8,128)} %concatenate.11.refs_1_.refs_2_, bf16[768,768]{1,0:T(8,128)(2,1)} %copy-done.3, bf16[768,768]{1,0:T(8,128)(2,1)} %collective-permute-done.refs_3_.refs_4_.refs_6_), custom_call_target="tpu_custom_call" | custom-call | flops 226492416 | bytes 2359296 | tf_op jit(solution)/shard_map/pallas_call | solution.py:273
  36.5 1.9 collective-permute-start.5
  38.4 2.4 %collective-permute-start.6 = (bf16[768,768]{1,0:T(8,128)(2,1)}, bf16[768,768]{1,0:T(8,128)(2,1)}, u32[]{:S(2)}, u32[]{:S(2)}) collective-permute-start(bf16[768,768]{1,0:T(8,128)(2,1)} %collective-permute-done.refs_3_.refs_4_.refs_6_), channel_id=1, source_target_pairs={{0,1},{1,0},{2,3},{3,2},{4,5},{5,4},{6,7},{7,6},{8,9},{9,8},{10,11... | collective-permute-start | bytes 3538952 | tf_op jit(solution)/shard_map/ppermute | solution.py:361
  40.8 12.0 %collective-permute-done.1.refs_2_.refs_6_.refs_7_.refs_9_ = bf16[768,768]{1,0:T(8,128)(2,1)S(1)} collective-permute-done((bf16[768,768]{1,0:T(8,128)(2,1)S(1)}, bf16[768,768]{1,0:T(8,128)(2,1)S(1)}, u32[]{:S(2)}, u32[]{:S(2)}) %collective-permute-start.1) | collective-permute-done | bytes 1179680 | tf_op jit(solution)/shard_map/ppermute | solution.py:361
  52.8 1.0 copy-done.4
  53.8 3.5 %shard_map.96.refs_2_ = bf16[96,768]{1,0:T(8,128)(2,1)} custom-call(s32[1]{0:T(128)} %bitcast.3.sc, bf16[96,768]{1,0:T(8,128)(2,1)} %get-tuple-element.31.refs_0_, f32[96,768]{1,0:T(8,128)} %get-tuple-element.33.refs_1_, bf16[768,768]{1,0:T(8,128)(2,1)} %copy-done.4, bf16[768,768]{1,0:T(8,128)(2,1)} %collective-permute-done.2.refs_3_.refs_7_.refs_8_.refs_10_), custom_call_target="tpu_custom_call" | custom-call | flops 226492416 | bytes 2359296 | tf_op jit(solution)/shard_map/pallas_call | solution.py:273
  57.3 1.9 collective-permute-start.7
  59.3 2.4 %collective-permute-start.8 = (bf16[768,768]{1,0:T(8,128)(2,1)}, bf16[768,768]{1,0:T(8,128)(2,1)S(1)}, u32[]{:S(2)}, u32[]{:S(2)}) collective-permute-start(bf16[768,768]{1,0:T(8,128)(2,1)} %collective-permute-done.2.refs_3_.refs_7_.refs_8_.refs_10_), channel_id=1, source_target_pairs={{0,1},{1,0},{2,3},{3,2},{4,5},{5,4},{6,7},{7,6},{8,9},{9,8},{10,11... | collective-permute-start | bytes 3538952 | tf_op jit(solution)/shard_map/ppermute | solution.py:361
  61.7 1.9 collective-permute-start.3
  63.6 1.5 collective-permute-done.3.refs_3_
  65.2 0.6 copy-done.16
  65.8 2.2 shard_map.97
  68.0 1.3 collective-permute-start.4
  69.4 4.0 %collective-permute-done.4.refs_0_ = bf16[96,768]{1,0:T(8,128)(2,1)S(1)} collective-permute-done((bf16[96,768]{1,0:T(8,128)(2,1)}, bf16[96,768]{1,0:T(8,128)(2,1)S(1)}, u32[]{:S(2)}, u32[]{:S(2)}) %collective-permute-start.4) | collective-permute-done | bytes 147488 | tf_op jit(solution)/shard_map/ppermute | solution.py:392
  73.3 0.6 copy-done.17
  74.0 0.5 copy-done.5
  75.2 0.7 collective-permute-start.9
  75.9 0.6 copy-done.18
  76.9 0.7 collective-permute-start.10
  77.6 0.6 copy-done.19
  78.6 0.7 collective-permute-start.11
  79.3 0.6 copy-done.11
  80.3 0.7 collective-permute-start.12
  81.1 0.6 copy-done.13
  82.1 1.3 collective-permute-start.13
  83.5 69.9 %collective-permute-done.13 = bf16[96,768]{1,0:T(8,128)(2,1)S(1)} collective-permute-done((bf16[96,768]{1,0:T(8,128)(2,1)}, bf16[96,768]{1,0:T(8,128)(2,1)S(1)}, u32[]{:S(2)}, u32[]{:S(2)}) %collective-permute-start.13) | collective-permute-done | bytes 147488 | tf_op jit(solution)/shard_map/ppermute | solution.py:392
  153.5 12.0 %all_to_all.5.recv = bf16[4,96,768]{2,1,0:T(8,128)(2,1)S(1)} all-to-all(bf16[4,96,768]{2,1,0:T(8,128)(2,1)S(1)} %broadcast_in_dim.46), channel_id=1, replica_groups={{0,2,4,6},{1,3,5,7},{8,10,12,14},{9,11,13,15},{16,18,20,22},{17,19,21,2..., dimensions={0} | all-to-all | bytes 1179648 | tf_op jit(solution)/shard_map/all_to_all | solution.py:472
  165.5 2.1 collective-permute-start.14
  167.8 1.6 collective-permute-done.14.other
  169.4 2.5 %shard_map.103 = (bf16[8,48,768]{2,1,0:T(8,128)(2,1)S(1)}, bf16[8,48,768]{2,1,0:T(8,128)(2,1)S(1)}) custom-call(s32[3]{0:T(128)S(1)} %pad_add_fusion.sc, bf16[4,96,768]{2,1,0:T(8,128)(2,1)S(1)} %all_to_all.5.recv, bf16[4,96,768]{2,1,0:T(8,128)(2,1)S(1)} %collective-permute-done.14.other, f32[1,768]{1,0:T(1,128)S(1)} %copy-done.2, ...), custom_call_target="tpu_custom_call" | custom-call | tf_op jit(solution)/shard_map/pallas_call | solution.py:323
  172.0 1.9 collective-permute-start.15
  173.9 15.6 %collective-permute-done.15 = bf16[8,48,768]{2,1,0:T(8,128)(2,1)S(1)} collective-permute-done((bf16[8,48,768]{2,1,0:T(8,128)(2,1)S(1)}, bf16[8,48,768]{2,1,0:T(8,128)(2,1)S(1)}, u32[]{:S(2)}, u32[]{:S(2)}) %collective-permute-start.15) | collective-permute-done | bytes 589856 | tf_op jit(solution)/shard_map/ppermute | solution.py:334
  189.6 3.0 %collective-permute-start.16 = (bf16[4,48,768]{2,1,0:T(8,128)(2,1)S(1)}, bf16[4,48,768]{2,1,0:T(8,128)(2,1)S(1)}, u32[]{:S(2)}, u32[]{:S(2)}) collective-permute-start(bf16[4,48,768]{2,1,0:T(8,128)(2,1)S(1)} %slice.43), channel_id=1, source_target_pairs={{0,16},{1,9},{2,18},{3,11},{4,20},{5,13},{6,22},{7,15},{8,24},{9,1... | collective-permute-start | bytes 884744 | tf_op jit(solution)/shard_map/ppermute | solution.py:334
  192.7 9.6 %collective-permute-done.16 = bf16[4,48,768]{2,1,0:T(8,128)(2,1)S(1)} collective-permute-done((bf16[4,48,768]{2,1,0:T(8,128)(2,1)S(1)}, bf16[4,48,768]{2,1,0:T(8,128)(2,1)S(1)}, u32[]{:S(2)}, u32[]{:S(2)}) %collective-permute-start.16) | collective-permute-done | bytes 294944 | tf_op jit(solution)/shard_map/ppermute | solution.py:334
  202.4 11.2 %collective-permute-start.19 = (bf16[48,768]{1,0:T(8,128)(2,1)S(1)}, bf16[48,768]{1,0:T(8,128)(2,1)S(1)}, u32[]{:S(2)}, u32[]{:S(2)}) collective-permute-start(bf16[48,768]{1,0:T(8,128)(2,1)S(1)} %get-tuple-element.55), channel_id=1, source_target_pairs={{0,96},{8,104},{16,112},{24,120},{32,0},{40,8},{48,16},{56,24},{64... | collective-permute-start | bytes 221192 | tf_op jit(solution)/shard_map/ppermute | solution.py:348
  213.6 4.9 %collective-permute-start.18 = (bf16[48,768]{1,0:T(8,128)(2,1)S(1)}, bf16[48,768]{1,0:T(8,128)(2,1)S(1)}, u32[]{:S(2)}, u32[]{:S(2)}) collective-permute-start(bf16[48,768]{1,0:T(8,128)(2,1)S(1)} %get-tuple-element.56), channel_id=1, source_target_pairs={{0,64},{8,72},{16,80},{24,88},{32,96},{40,104},{48,112},{56,120},{... | collective-permute-start | bytes 221192 | tf_op jit(solution)/shard_map/ppermute | solution.py:348
  218.6 7.8 %collective-permute-start.17 = (bf16[48,768]{1,0:T(8,128)(2,1)S(1)}, bf16[48,768]{1,0:T(8,128)(2,1)S(1)}, u32[]{:S(2)}, u32[]{:S(2)}) collective-permute-start(bf16[48,768]{1,0:T(8,128)(2,1)S(1)} %get-tuple-element.54), channel_id=1, source_target_pairs={{0,32},{8,40},{16,48},{24,56},{32,64},{40,72},{48,80},{56,88},{64,... | collective-permute-start | bytes 221192 | tf_op jit(solution)/shard_map/ppermute | solution.py:348
  226.4 4.5 %collective-permute-done.18 = bf16[48,768]{1,0:T(8,128)(2,1)S(1)} collective-permute-done((bf16[48,768]{1,0:T(8,128)(2,1)S(1)}, bf16[48,768]{1,0:T(8,128)(2,1)S(1)}, u32[]{:S(2)}, u32[]{:S(2)}) %collective-permute-start.18) | collective-permute-done | bytes 73760 | tf_op jit(solution)/shard_map/ppermute | solution.py:348
  230.9 0.7 collective-permute-done.17
  231.7 0.6 slice_bitcast_fusion.2
  (66 shorter events, 3.3 us)
Async XLA Ops:
  0.6 1.2 copy-start.1
  1.9 3.7 %copy-start.21 = (s32[2]{0:T(128)S(1)}, s32[2]{0:T(128)}, u32[]{:S(2)}) copy-start(s32[2]{0:T(128)} %param.10) | copy-start | bytes 28
  1.9 4.9 %copy-start.14 = (f32[1,7,7,768]{3,0,2,1:T(1,128)S(1)}, f32[1,7,7,768]{3,0,2,1:T(1,128)}, u32[]{:S(2)}) copy-start(f32[1,7,7,768]{3,0,2,1:T(1,128)} %param.11) | copy-start | bytes 451588
  1.9 5.3 %copy-start.20 = (f32[1,768]{1,0:T(1,128)S(1)}, f32[1,768]{1,0:T(1,128)}, u32[]{:S(2)}) copy-start(f32[1,768]{1,0:T(1,128)} %param.12) | copy-start | bytes 9220
  1.9 5.4 %copy-start.2 = (f32[1,768]{1,0:T(1,128)S(1)}, f32[1,768]{1,0:T(1,128)}, u32[]{:S(2)}) copy-start(f32[1,768]{1,0:T(1,128)} %scale.1) | copy-start | bytes 9220
  2.0 29.8 %copy-start.3 = (bf16[768,768]{1,0:T(8,128)(2,1)}, bf16[768,768]{1,0:T(8,128)(2,1)S(1)}, u32[]{:S(2)}) copy-start(bf16[768,768]{1,0:T(8,128)(2,1)S(1)} %pad_maximum_fusion.refs_2_.refs_3_.refs_5_) | copy-start | bytes 3538948
  2.0 22.2 %collective-permute-start = (bf16[768,768]{1,0:T(8,128)(2,1)S(1)}, bf16[768,768]{1,0:T(8,128)(2,1)}, u32[]{:S(2)}, u32[]{:S(2)}) collective-permute-start(bf16[768,768]{1,0:T(8,128)(2,1)S(1)} %pad_maximum_fusion.refs_2_.refs_3_.refs_5_), channel_id=1, source_target_pairs={{0,2},{1,7},{2,4},{3,1},{4,6},{5,3},{6,0},{7,5},{8,10},{9,15},{10,... | collective-permute-start | bytes 3538952 | tf_op jit(solution)/shard_map/ppermute | solution.py:361
  24.2 28.6 %collective-permute-start.1 = (bf16[768,768]{1,0:T(8,128)(2,1)S(1)}, bf16[768,768]{1,0:T(8,128)(2,1)S(1)}, u32[]{:S(2)}, u32[]{:S(2)}) collective-permute-start(bf16[768,768]{1,0:T(8,128)(2,1)S(1)} %pad_maximum_fusion.refs_2_.refs_3_.refs_5_), channel_id=1, source_target_pairs={{0,6},{1,3},{2,0},{3,5},{4,2},{5,7},{6,4},{7,1},{8,14},{9,11},{10,... | collective-permute-start | bytes 3538952 | tf_op jit(solution)/shard_map/ppermute | solution.py:361
  29.9 22.9 %collective-permute-start.2 = (bf16[768,768]{1,0:T(8,128)(2,1)}, bf16[768,768]{1,0:T(8,128)(2,1)}, u32[]{:S(2)}, u32[]{:S(2)}) collective-permute-start(bf16[768,768]{1,0:T(8,128)(2,1)} %collective-permute-done.refs_3_.refs_4_.refs_6_), channel_id=1, source_target_pairs={{0,2},{1,7},{2,4},{3,1},{4,6},{5,3},{6,0},{7,5},{8,10},{9,15},{10,... | collective-permute-start | bytes 3538952 | tf_op jit(solution)/shard_map/ppermute | solution.py:361
  36.5 32.9 %collective-permute-start.5 = (bf16[768,768]{1,0:T(8,128)(2,1)}, bf16[768,768]{1,0:T(8,128)(2,1)}, u32[]{:S(2)}, u32[]{:S(2)}) collective-permute-start(bf16[768,768]{1,0:T(8,128)(2,1)} %copy-done.3), channel_id=1, source_target_pairs={{0,1},{1,0},{2,3},{3,2},{4,5},{5,4},{6,7},{7,6},{8,9},{9,8},{10,11... | collective-permute-start | bytes 3538952 | tf_op jit(solution)/shard_map/ppermute | solution.py:361
  38.4 31.0 %collective-permute-start.6 = (bf16[768,768]{1,0:T(8,128)(2,1)}, bf16[768,768]{1,0:T(8,128)(2,1)}, u32[]{:S(2)}, u32[]{:S(2)}) collective-permute-start(bf16[768,768]{1,0:T(8,128)(2,1)} %collective-permute-done.refs_3_.refs_4_.refs_6_), channel_id=1, source_target_pairs={{0,1},{1,0},{2,3},{3,2},{4,5},{5,4},{6,7},{7,6},{8,9},{9,8},{10,11... | collective-permute-start | bytes 3538952 | tf_op jit(solution)/shard_map/ppermute | solution.py:361
  52.8 1.0 copy-start.4
  57.3 16.0 %collective-permute-start.7 = (bf16[768,768]{1,0:T(8,128)(2,1)}, bf16[768,768]{1,0:T(8,128)(2,1)S(1)}, u32[]{:S(2)}, u32[]{:S(2)}) collective-permute-start(bf16[768,768]{1,0:T(8,128)(2,1)} %copy-done.4), channel_id=1, source_target_pairs={{0,1},{1,0},{2,3},{3,2},{4,5},{5,4},{6,7},{7,6},{8,9},{9,8},{10,11... | collective-permute-start | bytes 3538952 | tf_op jit(solution)/shard_map/ppermute | solution.py:361
  59.3 14.1 %collective-permute-start.8 = (bf16[768,768]{1,0:T(8,128)(2,1)}, bf16[768,768]{1,0:T(8,128)(2,1)S(1)}, u32[]{:S(2)}, u32[]{:S(2)}) collective-permute-start(bf16[768,768]{1,0:T(8,128)(2,1)} %collective-permute-done.2.refs_3_.refs_7_.refs_8_.refs_10_), channel_id=1, source_target_pairs={{0,1},{1,0},{2,3},{3,2},{4,5},{5,4},{6,7},{7,6},{8,9},{9,8},{10,11... | collective-permute-start | bytes 3538952 | tf_op jit(solution)/shard_map/ppermute | solution.py:361
  61.7 3.5 %collective-permute-start.3 = (bf16[96,768]{1,0:T(8,128)(2,1)}, bf16[96,768]{1,0:T(8,128)(2,1)S(1)}, u32[]{:S(2)}, u32[]{:S(2)}) collective-permute-start(bf16[96,768]{1,0:T(8,128)(2,1)} %shard_map.96.refs_2_), channel_id=1, source_target_pairs={{0,1},{1,0},{2,3},{3,2},{4,5},{5,4},{6,7},{7,6},{8,9},{9,8},{10,11... | collective-permute-start | bytes 442376 | tf_op jit(solution)/shard_map/ppermute | solution.py:361
  65.2 0.6 copy-start.16
  68.0 5.3 %collective-permute-start.4 = (bf16[96,768]{1,0:T(8,128)(2,1)}, bf16[96,768]{1,0:T(8,128)(2,1)S(1)}, u32[]{:S(2)}, u32[]{:S(2)}) collective-permute-start(bf16[96,768]{1,0:T(8,128)(2,1)} %shard_map.97), channel_id=1, source_target_pairs={{0,128},{1,129},{2,130},{3,131},{4,132},{5,133},{6,134},{7,135},{8... | collective-permute-start | bytes 442376 | tf_op jit(solution)/shard_map/ppermute | solution.py:392
  73.3 0.7 copy-start.17
  73.3 1.2 copy-start.5
  73.3 1.5 copy-start.6
  75.2 0.7 collective-permute-start.9
  75.9 0.7 copy-start.18
  76.9 0.7 collective-permute-start.10
  77.6 0.7 copy-start.19
  78.6 0.7 collective-permute-start.11
  79.3 0.7 copy-start.11
  80.3 0.7 collective-permute-start.12
  81.0 0.7 copy-start.13
  81.7 1.7 copy-start.8
  81.7 1.7 copy-start.9
  81.7 1.7 copy-start.10
  81.7 1.7 copy-start.15
  81.7 71.7 %copy-start.7 = (bf16[96,768]{1,0:T(8,128)(2,1)S(1)}, bf16[96,768]{1,0:T(8,128)(2,1)}, u32[]{:S(2)}) copy-start(bf16[96,768]{1,0:T(8,128)(2,1)} %get-tuple-element.43.refs_1_) | copy-start | bytes 442372
  81.7 71.7 %copy-start.12 = (bf16[96,768]{1,0:T(8,128)(2,1)S(1)}, bf16[96,768]{1,0:T(8,128)(2,1)}, u32[]{:S(2)}) copy-start(bf16[96,768]{1,0:T(8,128)(2,1)} %copy-done.11) | copy-start | bytes 442372
  82.1 71.3 %collective-permute-start.13 = (bf16[96,768]{1,0:T(8,128)(2,1)}, bf16[96,768]{1,0:T(8,128)(2,1)S(1)}, u32[]{:S(2)}, u32[]{:S(2)}) collective-permute-start(bf16[96,768]{1,0:T(8,128)(2,1)} %shard_map.102), channel_id=1, source_target_pairs={{128,0},{129,1},{130,2},{131,3},{132,4},{133,5},{134,6},{135,7},{1... | collective-permute-start | bytes 442376 | tf_op jit(solution)/shard_map/ppermute | solution.py:392
  153.4 16.0 %copy-start = (bf16[1,768,384]{2,1,0:T(8,128)(2,1)S(1)}, bf16[1,768,384]{2,1,0:T(8,128)(2,1)}, u32[]{:S(2)}) copy-start(bf16[1,768,384]{2,1,0:T(8,128)(2,1)} %param.13) | copy-start | bytes 1769476
  165.5 3.9 %collective-permute-start.14 = (bf16[4,96,768]{2,1,0:T(8,128)(2,1)S(1)}, bf16[4,96,768]{2,1,0:T(8,128)(2,1)S(1)}, u32[]{:S(2)}, u32[]{:S(2)}) collective-permute-start(bf16[4,96,768]{2,1,0:T(8,128)(2,1)S(1)} %all_to_all.5.recv), channel_id=1, source_target_pairs={{0,1},{1,0},{2,3},{3,2},{4,5},{5,4},{6,7},{7,6},{8,9},{9,8},{10,11... | collective-permute-start | bytes 1769480 | tf_op jit(solution)/shard_map/ppermute | solution.py:361
  172.0 17.5 %collective-permute-start.15 = (bf16[8,48,768]{2,1,0:T(8,128)(2,1)S(1)}, bf16[8,48,768]{2,1,0:T(8,128)(2,1)S(1)}, u32[]{:S(2)}, u32[]{:S(2)}) collective-permute-start(bf16[8,48,768]{2,1,0:T(8,128)(2,1)S(1)} %get-tuple-element.51), channel_id=1, source_target_pairs={{0,8},{1,17},{2,10},{3,19},{4,12},{5,21},{6,14},{7,23},{8,0},{9,25... | collective-permute-start | bytes 1769480 | tf_op jit(solution)/shard_map/ppermute | solution.py:334
  189.6 12.7 %collective-permute-start.16 = (bf16[4,48,768]{2,1,0:T(8,128)(2,1)S(1)}, bf16[4,48,768]{2,1,0:T(8,128)(2,1)S(1)}, u32[]{:S(2)}, u32[]{:S(2)}) collective-permute-start(bf16[4,48,768]{2,1,0:T(8,128)(2,1)S(1)} %slice.43), channel_id=1, source_target_pairs={{0,16},{1,9},{2,18},{3,11},{4,20},{5,13},{6,22},{7,15},{8,24},{9,1... | collective-permute-start | bytes 884744 | tf_op jit(solution)/shard_map/ppermute | solution.py:334
  202.4 24.0 %collective-permute-start.19 = (bf16[48,768]{1,0:T(8,128)(2,1)S(1)}, bf16[48,768]{1,0:T(8,128)(2,1)S(1)}, u32[]{:S(2)}, u32[]{:S(2)}) collective-permute-start(bf16[48,768]{1,0:T(8,128)(2,1)S(1)} %get-tuple-element.55), channel_id=1, source_target_pairs={{0,96},{8,104},{16,112},{24,120},{32,0},{40,8},{48,16},{56,24},{64... | collective-permute-start | bytes 221192 | tf_op jit(solution)/shard_map/ppermute | solution.py:348
  213.6 17.3 %collective-permute-start.18 = (bf16[48,768]{1,0:T(8,128)(2,1)S(1)}, bf16[48,768]{1,0:T(8,128)(2,1)S(1)}, u32[]{:S(2)}, u32[]{:S(2)}) collective-permute-start(bf16[48,768]{1,0:T(8,128)(2,1)S(1)} %get-tuple-element.56), channel_id=1, source_target_pairs={{0,64},{8,72},{16,80},{24,88},{32,96},{40,104},{48,112},{56,120},{... | collective-permute-start | bytes 221192 | tf_op jit(solution)/shard_map/ppermute | solution.py:348
  218.6 13.1 %collective-permute-start.17 = (bf16[48,768]{1,0:T(8,128)(2,1)S(1)}, bf16[48,768]{1,0:T(8,128)(2,1)S(1)}, u32[]{:S(2)}, u32[]{:S(2)}) collective-permute-start(bf16[48,768]{1,0:T(8,128)(2,1)S(1)} %get-tuple-element.54), channel_id=1, source_target_pairs={{0,32},{8,40},{16,48},{24,56},{32,64},{40,72},{48,80},{56,88},{64,... | collective-permute-start | bytes 221192 | tf_op jit(solution)/shard_map/ppermute | solution.py:348

commit v3 on v2

--- a/solution.py
+++ b/solution.py
@@ -25,7 +25,6 @@
 TAP_ROWS = TAPS * TAPS
 GAIN, SCALE, INVERSE, PARAM_ROWS = TAP_ROWS, TAP_ROWS + 1, TAP_ROWS + 2, 56
 OUT_ROWS = C // DP
-PARAMS = pltpu.CompilerParams(vmem_limit_bytes=56 * 1024 * 1024)
 SMALL = pltpu.CompilerParams(vmem_limit_bytes=24 * 1024 * 1024)
 
 
@@ -66,10 +65,9 @@
 
 
 class Weights:
-    AHEAD = 3
-
     def __init__(self, refs, places, buffer, sems, slope=None, slopes=None):
         self.places = places
+        self.ahead = len(places) if slope is None else 3
         self.copies = []
         for at, (ref, group) in enumerate(zip(refs, places)):
             copies = [pltpu.make_async_copy(ref, buffer.at[group], sems.at[at])]
@@ -80,7 +78,7 @@
                     )
                 )
             self.copies.append(copies)
-        for at in range(min(self.AHEAD, len(places))):
+        for at in range(min(self.ahead, len(places))):
             self.start(at)
 
     def start(self, at):
@@ -91,8 +89,8 @@
         for at, group in enumerate(self.places):
             for copy in self.copies[at]:
                 copy.wait()
-            if at + self.AHEAD < len(self.places):
-                self.start(at + self.AHEAD)
+            if at + self.ahead < len(self.places):
+                self.start(at + self.ahead)
             yield group
 
 
@@ -282,7 +280,7 @@
             bytes_accessed=2 * C * C * max(pieces, 1),
             transcendentals=0,
         ),
-        compiler_params=PARAMS,
+        compiler_params=SMALL,
     )(active, *operands.values(), *weights)
     return dict(zip(outs, results))
 

time: 233 us -> 244 us (1.047)
  local copies, waits for them, and re-layouts: 10.4 us -> 19 us
  starting transfers between devices: 58 us -> 62.2 us
    unnamed x44 -> x72, local copies, waits for them, and re-layouts: 5.85 us -> 14.4 us
    ppermute x6, starting transfers between devices: 5.27 us -> 7.96 us  [shards(): send = lambda v, source, to: lax.ppermute(v, 'section', [(source, to)])]
  transfers between devices with their start and end apart: 20 -> 20, of which waited for: 10 -> 10; matrix products, arithmetic and copies ran while one was open for 2% -> 2% of each run, Pallas kernels for 4% -> 3%
where the time goes in v3:
time: 244 us; the launch traced here: 243 us
  waiting for transfers between devices  133 us (55%)
  starting transfers between devices  62.2 us (25%)
  local copies, waits for them, and re-layouts  19 us (8%)
  Pallas kernels  12.3 us (5%)
  blocking collectives  12 us (5%)
  other arithmetic  2.68 us (1%)
    ppermute x6, waiting for transfers between devices, shards(): send = lambda v, source, to: lax.ppermute(v, 'section', [(source, to)])  76 us
    ppermute x9, waiting for transfers between devices, shards(): move = lambda v, pairs: lax.ppermute(v, 'mp', pairs)  27.2 us
    ppermute x2, waiting for transfers between devices, sum_over_dp(): lax.ppermute(v, ('dp', 'mp'), [(z * MP + j, (z ^ by[j % 2]) * MP + j) for...  24.6 us
    ppermute x3, starting transfers between devices, sum_over_dp(): total = total + lax.ppermute(block(ahead), 'dp', pairs).astype(F32)  24.3 us
    ppermute x9, starting transfers between devices, shards(): move = lambda v, pairs: lax.ppermute(v, 'mp', pairs)  23.8 us
    unnamed x72, local copies, waits for them, and re-layouts  14.4 us
    all_to_all x1, blocking collectives, shards(): lax.all_to_all(jnp.broadcast_to(mine[None], (CHIPS, TOK, C)), 'mp', 0, 0,...  12 us
    pallas_call x8, Pallas kernels, call_block(): pl.pallas_call(functools.partial(block_kernel, body, names, places), in_s...  9.71 us
  transfers between devices with their start and end apart: 20, of which 10 were waited for; matrix products, arithmetic and copies ran while one was open for 2% of the time, Pallas kernels for 3%

profile of v3, /device:TPU:8, one launch (start us, length us, event | category | flops | bytes accessed | tf_op | source)
XLA Modules:
  0.0 243.2 jit_solution(9549785736852124850)
XLA Ops:
  0.6 1.2 slice_bitcast_fusion.1
  2.0 3.5 %collective-permute-start = (bf16[768,768]{1,0:T(8,128)(2,1)S(1)}, bf16[768,768]{1,0:T(8,128)(2,1)}, u32[]{:S(2)}, u32[]{:S(2)}) collective-permute-start(bf16[768,768]{1,0:T(8,128)(2,1)S(1)} %pad_maximum_fusion.refs_2_.refs_3_.refs_5_), channel_id=1, source_target_pairs={{0,2},{1,7},{2,4},{3,1},{4,6},{5,3},{6,0},{7,5},{8,10},{9,15},{10,... | collective-permute-start | bytes 3538952 | tf_op jit(solution)/shard_map/ppermute | solution.py:359
  7.3 2.0 concatenate.11.refs_1_.refs_2_
  9.3 1.7 multiply_bitcast_fusion
  11.0 13.2 %collective-permute-done.refs_3_.refs_4_.refs_6_ = bf16[768,768]{1,0:T(8,128)(2,1)} collective-permute-done((bf16[768,768]{1,0:T(8,128)(2,1)S(1)}, bf16[768,768]{1,0:T(8,128)(2,1)}, u32[]{:S(2)}, u32[]{:S(2)}) %collective-permute-start) | collective-permute-done | bytes 1179680 | tf_op jit(solution)/shard_map/ppermute | solution.py:359
  24.2 5.7 %collective-permute-start.1 = (bf16[768,768]{1,0:T(8,128)(2,1)S(1)}, bf16[768,768]{1,0:T(8,128)(2,1)S(1)}, u32[]{:S(2)}, u32[]{:S(2)}) collective-permute-start(bf16[768,768]{1,0:T(8,128)(2,1)S(1)} %pad_maximum_fusion.refs_2_.refs_3_.refs_5_), channel_id=1, source_target_pairs={{0,6},{1,3},{2,0},{3,5},{4,2},{5,7},{6,4},{7,1},{8,14},{9,11},{10,... | collective-permute-start | bytes 3538952 | tf_op jit(solution)/shard_map/ppermute | solution.py:359
  29.9 1.9 collective-permute-start.2
  31.8 0.9 copy-done
  32.7 0.9 copy-done.9
  33.6 3.8 %shard_map.95 = (bf16[96,768]{1,0:T(8,128)(2,1)S(1)}, f32[96,768]{1,0:T(8,128)S(1)}) custom-call(s32[1]{0:T(128)} %bitcast.3.sc, bf16[96,768]{1,0:T(8,128)(2,1)S(1)} %copy-done.9, f32[56,768]{1,0:T(8,128)S(1)} %copy-done, bf16[768,768]{1,0:T(8,128)(2,1)S(1)} %pad_maximum_fusion.refs_2_.refs_3_.refs_5_, ...), custom_call_target="tpu_custom_call" | custom-call | flops 226492416 | bytes 2359296 | tf_op jit(solution)/shard_map/pallas_call | solution.py:271
  37.4 1.9 collective-permute-start.5
  39.4 2.4 collective-permute-start.6
  41.8 11.0 %collective-permute-done.1.refs_2_.refs_6_.refs_7_.refs_9_ = bf16[768,768]{1,0:T(8,128)(2,1)S(1)} collective-permute-done((bf16[768,768]{1,0:T(8,128)(2,1)S(1)}, bf16[768,768]{1,0:T(8,128)(2,1)S(1)}, u32[]{:S(2)}, u32[]{:S(2)}) %collective-permute-start.1) | collective-permute-done | bytes 1179680 | tf_op jit(solution)/shard_map/ppermute | solution.py:359
  52.8 2.3 shard_map.96.refs_2_
  55.1 1.9 collective-permute-start.7
  57.0 2.4 collective-permute-start.8
  59.5 1.9 collective-permute-start.3
  61.4 1.3 collective-permute-done.3.refs_3_
  62.7 1.9 shard_map.97
  64.6 1.9 collective-permute-start.4
  66.6 3.3 %collective-permute-done.4.refs_0_ = bf16[96,768]{1,0:T(8,128)(2,1)} collective-permute-done((bf16[96,768]{1,0:T(8,128)(2,1)}, bf16[96,768]{1,0:T(8,128)(2,1)}, u32[]{:S(2)}, u32[]{:S(2)}) %collective-permute-start.4) | collective-permute-done | bytes 147488 | tf_op jit(solution)/shard_map/ppermute | solution.py:390
  69.9 0.9 copy-done.2
  71.2 1.0 copy-done.13
  73.5 1.3 collective-permute-start.9
  74.8 0.9 copy-done.3
  76.1 1.1 copy-done.15
  78.4 1.3 collective-permute-start.10
  79.7 0.9 copy-done.4
  80.7 0.9 copy-done.11
  82.0 0.8 collective-permute-start.11
  83.4 1.3 collective-permute-start.12
  84.7 0.9 copy-done.5
  85.7 1.3 copy-done.14
  86.9 0.9 copy-done.20
  89.0 1.3 collective-permute-start.13
  90.4 72.7 %collective-permute-done.13 = bf16[96,768]{1,0:T(8,128)(2,1)S(1)} collective-permute-done((bf16[96,768]{1,0:T(8,128)(2,1)S(1)}, bf16[96,768]{1,0:T(8,128)(2,1)S(1)}, u32[]{:S(2)}, u32[]{:S(2)}) %collective-permute-start.13) | collective-permute-done | bytes 147488 | tf_op jit(solution)/shard_map/ppermute | solution.py:390
  163.3 12.0 %all_to_all.5.recv = bf16[4,96,768]{2,1,0:T(8,128)(2,1)S(1)} all-to-all(bf16[4,96,768]{2,1,0:T(8,128)(2,1)S(1)} %broadcast_in_dim.46), channel_id=1, replica_groups={{0,2,4,6},{1,3,5,7},{8,10,12,14},{9,11,13,15},{16,18,20,22},{17,19,21,2..., dimensions={0} | all-to-all | bytes 1179648 | tf_op jit(solution)/shard_map/all_to_all | solution.py:470
  175.3 2.1 collective-permute-start.14
  177.6 1.6 collective-permute-done.14.other
  179.2 2.5 %shard_map.103 = (bf16[8,48,768]{2,1,0:T(8,128)(2,1)S(1)}, bf16[8,48,768]{2,1,0:T(8,128)(2,1)S(1)}) custom-call(s32[3]{0:T(128)S(1)} %pad_add_fusion.sc, bf16[4,96,768]{2,1,0:T(8,128)(2,1)S(1)} %all_to_all.5.recv, bf16[4,96,768]{2,1,0:T(8,128)(2,1)S(1)} %collective-permute-done.14.other, f32[1,768]{1,0:T(1,128)S(1)} %copy-done.32, ...), custom_call_target="tpu_custom_call" | custom-call | tf_op jit(solution)/shard_map/pallas_call | solution.py:321
  181.7 2.7 %collective-permute-start.15 = (bf16[8,48,768]{2,1,0:T(8,128)(2,1)S(1)}, bf16[8,48,768]{2,1,0:T(8,128)(2,1)S(1)}, u32[]{:S(2)}, u32[]{:S(2)}) collective-permute-start(bf16[8,48,768]{2,1,0:T(8,128)(2,1)S(1)} %get-tuple-element.51), channel_id=1, source_target_pairs={{0,8},{1,17},{2,10},{3,19},{4,12},{5,21},{6,14},{7,23},{8,0},{9,25... | collective-permute-start | bytes 1769480 | tf_op jit(solution)/shard_map/ppermute | solution.py:332
  184.4 15.4 %collective-permute-done.15 = bf16[8,48,768]{2,1,0:T(8,128)(2,1)S(1)} collective-permute-done((bf16[8,48,768]{2,1,0:T(8,128)(2,1)S(1)}, bf16[8,48,768]{2,1,0:T(8,128)(2,1)S(1)}, u32[]{:S(2)}, u32[]{:S(2)}) %collective-permute-start.15) | collective-permute-done | bytes 589856 | tf_op jit(solution)/shard_map/ppermute | solution.py:332
  200.0 3.4 %collective-permute-start.16 = (bf16[4,48,768]{2,1,0:T(8,128)(2,1)S(1)}, bf16[4,48,768]{2,1,0:T(8,128)(2,1)S(1)}, u32[]{:S(2)}, u32[]{:S(2)}) collective-permute-start(bf16[4,48,768]{2,1,0:T(8,128)(2,1)S(1)} %slice.43), channel_id=1, source_target_pairs={{0,16},{1,9},{2,18},{3,11},{4,20},{5,13},{6,22},{7,15},{8,24},{9,1... | collective-permute-start | bytes 884744 | tf_op jit(solution)/shard_map/ppermute | solution.py:332
  203.5 9.2 %collective-permute-done.16 = bf16[4,48,768]{2,1,0:T(8,128)(2,1)S(1)} collective-permute-done((bf16[4,48,768]{2,1,0:T(8,128)(2,1)S(1)}, bf16[4,48,768]{2,1,0:T(8,128)(2,1)S(1)}, u32[]{:S(2)}, u32[]{:S(2)}) %collective-permute-start.16) | collective-permute-done | bytes 294944 | tf_op jit(solution)/shard_map/ppermute | solution.py:332
  212.8 11.6 %collective-permute-start.19 = (bf16[48,768]{1,0:T(8,128)(2,1)S(1)}, bf16[48,768]{1,0:T(8,128)(2,1)S(1)}, u32[]{:S(2)}, u32[]{:S(2)}) collective-permute-start(bf16[48,768]{1,0:T(8,128)(2,1)S(1)} %get-tuple-element.55), channel_id=1, source_target_pairs={{0,96},{8,104},{16,112},{24,120},{32,0},{40,8},{48,16},{56,24},{64... | collective-permute-start | bytes 221192 | tf_op jit(solution)/shard_map/ppermute | solution.py:346
  224.4 4.9 %collective-permute-start.18 = (bf16[48,768]{1,0:T(8,128)(2,1)S(1)}, bf16[48,768]{1,0:T(8,128)(2,1)S(1)}, u32[]{:S(2)}, u32[]{:S(2)}) collective-permute-start(bf16[48,768]{1,0:T(8,128)(2,1)S(1)} %get-tuple-element.56), channel_id=1, source_target_pairs={{0,64},{8,72},{16,80},{24,88},{32,96},{40,104},{48,112},{56,120},{... | collective-permute-start | bytes 221192 | tf_op jit(solution)/shard_map/ppermute | solution.py:346
  229.3 7.8 %collective-permute-start.17 = (bf16[48,768]{1,0:T(8,128)(2,1)S(1)}, bf16[48,768]{1,0:T(8,128)(2,1)S(1)}, u32[]{:S(2)}, u32[]{:S(2)}) collective-permute-start(bf16[48,768]{1,0:T(8,128)(2,1)S(1)} %get-tuple-element.54), channel_id=1, source_target_pairs={{0,32},{8,40},{16,48},{24,56},{32,64},{40,72},{48,80},{56,88},{64,... | collective-permute-start | bytes 221192 | tf_op jit(solution)/shard_map/ppermute | solution.py:346
  237.2 4.6 %collective-permute-done.18 = bf16[48,768]{1,0:T(8,128)(2,1)S(1)} collective-permute-done((bf16[48,768]{1,0:T(8,128)(2,1)S(1)}, bf16[48,768]{1,0:T(8,128)(2,1)S(1)}, u32[]{:S(2)}, u32[]{:S(2)}) %collective-permute-start.18) | collective-permute-done | bytes 73760 | tf_op jit(solution)/shard_map/ppermute | solution.py:346
  (94 shorter events, 8.6 us)
Async XLA Ops:
  0.6 1.2 copy-start.7
  1.9 3.7 %copy-start.35 = (s32[2]{0:T(128)S(1)}, s32[2]{0:T(128)}, u32[]{:S(2)}) copy-start(s32[2]{0:T(128)} %param.10) | copy-start | bytes 28
  1.9 4.9 %copy-start.33 = (f32[1,7,7,768]{3,0,2,1:T(1,128)S(1)}, f32[1,7,7,768]{3,0,2,1:T(1,128)}, u32[]{:S(2)}) copy-start(f32[1,7,7,768]{3,0,2,1:T(1,128)} %param.11) | copy-start | bytes 451588
  1.9 5.3 %copy-start.34 = (f32[1,768]{1,0:T(1,128)S(1)}, f32[1,768]{1,0:T(1,128)}, u32[]{:S(2)}) copy-start(f32[1,768]{1,0:T(1,128)} %param.12) | copy-start | bytes 9220
  1.9 5.4 %copy-start.32 = (f32[1,768]{1,0:T(1,128)S(1)}, f32[1,768]{1,0:T(1,128)}, u32[]{:S(2)}) copy-start(f32[1,768]{1,0:T(1,128)} %scale.1) | copy-start | bytes 9220
  2.0 22.2 %collective-permute-start = (bf16[768,768]{1,0:T(8,128)(2,1)S(1)}, bf16[768,768]{1,0:T(8,128)(2,1)}, u32[]{:S(2)}, u32[]{:S(2)}) collective-permute-start(bf16[768,768]{1,0:T(8,128)(2,1)S(1)} %pad_maximum_fusion.refs_2_.refs_3_.refs_5_), channel_id=1, source_target_pairs={{0,2},{1,7},{2,4},{3,1},{4,6},{5,3},{6,0},{7,5},{8,10},{9,15},{10,... | collective-permute-start | bytes 3538952 | tf_op jit(solution)/shard_map/ppermute | solution.py:359
  24.2 28.6 %collective-permute-start.1 = (bf16[768,768]{1,0:T(8,128)(2,1)S(1)}, bf16[768,768]{1,0:T(8,128)(2,1)S(1)}, u32[]{:S(2)}, u32[]{:S(2)}) collective-permute-start(bf16[768,768]{1,0:T(8,128)(2,1)S(1)} %pad_maximum_fusion.refs_2_.refs_3_.refs_5_), channel_id=1, source_target_pairs={{0,6},{1,3},{2,0},{3,5},{4,2},{5,7},{6,4},{7,1},{8,14},{9,11},{10,... | collective-permute-start | bytes 3538952 | tf_op jit(solution)/shard_map/ppermute | solution.py:359
  29.9 22.9 %collective-permute-start.2 = (bf16[768,768]{1,0:T(8,128)(2,1)}, bf16[768,768]{1,0:T(8,128)(2,1)S(1)}, u32[]{:S(2)}, u32[]{:S(2)}) collective-permute-start(bf16[768,768]{1,0:T(8,128)(2,1)} %collective-permute-done.refs_3_.refs_4_.refs_6_), channel_id=1, source_target_pairs={{0,2},{1,7},{2,4},{3,1},{4,6},{5,3},{6,0},{7,5},{8,10},{9,15},{10,... | collective-permute-start | bytes 3538952 | tf_op jit(solution)/shard_map/ppermute | solution.py:359
  31.8 0.9 copy-start
  32.7 0.9 copy-start.9
  37.4 17.7 %copy-start.17 = (bf16[96,768]{1,0:T(8,128)(2,1)}, bf16[96,768]{1,0:T(8,128)(2,1)S(1)}, u32[]{:S(2)}) copy-start(bf16[96,768]{1,0:T(8,128)(2,1)S(1)} %get-tuple-element.31.refs_0_) | copy-start | bytes 442372
  37.4 29.1 %collective-permute-start.5 = (bf16[768,768]{1,0:T(8,128)(2,1)S(1)}, bf16[768,768]{1,0:T(8,128)(2,1)}, u32[]{:S(2)}, u32[]{:S(2)}) collective-permute-start(bf16[768,768]{1,0:T(8,128)(2,1)S(1)} %pad_maximum_fusion.refs_2_.refs_3_.refs_5_), channel_id=1, source_target_pairs={{0,1},{1,0},{2,3},{3,2},{4,5},{5,4},{6,7},{7,6},{8,9},{9,8},{10,11... | collective-permute-start | bytes 3538952 | tf_op jit(solution)/shard_map/ppermute | solution.py:359
  39.4 27.2 %collective-permute-start.6 = (bf16[768,768]{1,0:T(8,128)(2,1)}, bf16[768,768]{1,0:T(8,128)(2,1)}, u32[]{:S(2)}, u32[]{:S(2)}) collective-permute-start(bf16[768,768]{1,0:T(8,128)(2,1)} %collective-permute-done.refs_3_.refs_4_.refs_6_), channel_id=1, source_target_pairs={{0,1},{1,0},{2,3},{3,2},{4,5},{5,4},{6,7},{7,6},{8,9},{9,8},{10,11... | collective-permute-start | bytes 3538952 | tf_op jit(solution)/shard_map/ppermute | solution.py:359
  52.8 9.9 %copy-start.1 = (f32[56,768]{1,0:T(8,128)S(1)}, f32[56,768]{1,0:T(8,128)}, u32[]{:S(2)}) copy-start(f32[56,768]{1,0:T(8,128)} %concatenate.11.refs_1_.refs_2_) | copy-start | bytes 516100
  52.8 9.9 %copy-start.10 = (bf16[96,768]{1,0:T(8,128)(2,1)S(1)}, bf16[96,768]{1,0:T(8,128)(2,1)}, u32[]{:S(2)}) copy-start(bf16[96,768]{1,0:T(8,128)(2,1)} %get-tuple-element.27.refs_0_) | copy-start | bytes 442372
  55.1 14.8 %collective-permute-start.7 = (bf16[768,768]{1,0:T(8,128)(2,1)S(1)}, bf16[768,768]{1,0:T(8,128)(2,1)}, u32[]{:S(2)}, u32[]{:S(2)}) collective-permute-start(bf16[768,768]{1,0:T(8,128)(2,1)S(1)} %collective-permute-done.1.refs_2_.refs_6_.refs_7_.refs_9_), channel_id=1, source_target_pairs={{0,1},{1,0},{2,3},{3,2},{4,5},{5,4},{6,7},{7,6},{8,9},{9,8},{10,11... | collective-permute-start | bytes 3538952 | tf_op jit(solution)/shard_map/ppermute | solution.py:359
  57.0 12.9 %collective-permute-start.8 = (bf16[768,768]{1,0:T(8,128)(2,1)S(1)}, bf16[768,768]{1,0:T(8,128)(2,1)}, u32[]{:S(2)}, u32[]{:S(2)}) collective-permute-start(bf16[768,768]{1,0:T(8,128)(2,1)S(1)} %collective-permute-done.2.refs_3_.refs_7_.refs_8_.refs_10_), channel_id=1, source_target_pairs={{0,1},{1,0},{2,3},{3,2},{4,5},{5,4},{6,7},{7,6},{8,9},{9,8},{10,11... | collective-permute-start | bytes 3538952 | tf_op jit(solution)/shard_map/ppermute | solution.py:359
  59.5 3.3 %collective-permute-start.3 = (bf16[96,768]{1,0:T(8,128)(2,1)S(1)}, bf16[96,768]{1,0:T(8,128)(2,1)S(1)}, u32[]{:S(2)}, u32[]{:S(2)}) collective-permute-start(bf16[96,768]{1,0:T(8,128)(2,1)S(1)} %shard_map.96.refs_2_), channel_id=1, source_target_pairs={{0,1},{1,0},{2,3},{3,2},{4,5},{5,4},{6,7},{7,6},{8,9},{9,8},{10,11... | collective-permute-start | bytes 442376 | tf_op jit(solution)/shard_map/ppermute | solution.py:359
  64.6 5.3 %collective-permute-start.4 = (bf16[96,768]{1,0:T(8,128)(2,1)}, bf16[96,768]{1,0:T(8,128)(2,1)}, u32[]{:S(2)}, u32[]{:S(2)}) collective-permute-start(bf16[96,768]{1,0:T(8,128)(2,1)} %shard_map.97), channel_id=1, source_target_pairs={{0,128},{1,129},{2,130},{3,131},{4,132},{5,133},{6,134},{7,135},{8... | collective-permute-start | bytes 442376 | tf_op jit(solution)/shard_map/ppermute | solution.py:390
  69.9 0.9 copy-start.2
  71.2 1.0 copy-start.13
  73.5 1.3 collective-permute-start.9
  74.8 0.9 copy-start.3
  76.1 1.1 copy-start.15
  78.4 1.3 collective-permute-start.10
  79.7 0.9 copy-start.4
  81.6 1.3 copy-start.16
  81.6 1.3 copy-start.22
  81.6 1.3 copy-start.31
  81.9 1.3 copy-start.26
  82.0 0.8 collective-permute-start.11
  83.4 1.3 collective-permute-start.12
  84.7 0.9 copy-start.5
  85.7 1.3 copy-start.14
  88.6 1.7 copy-start.18
  88.6 1.7 copy-start.23
  88.6 1.7 copy-start.27
  88.6 74.5 %copy-start.12 = (bf16[96,768]{1,0:T(8,128)(2,1)S(1)}, bf16[96,768]{1,0:T(8,128)(2,1)}, u32[]{:S(2)}) copy-start(bf16[96,768]{1,0:T(8,128)(2,1)} %get-tuple-element.43.refs_1_) | copy-start | bytes 442372
  88.6 74.5 %copy-start.25 = (bf16[96,768]{1,0:T(8,128)(2,1)S(1)}, bf16[96,768]{1,0:T(8,128)(2,1)}, u32[]{:S(2)}) copy-start(bf16[96,768]{1,0:T(8,128)(2,1)} %copy-done.24) | copy-start | bytes 442372
  89.0 74.1 %collective-permute-start.13 = (bf16[96,768]{1,0:T(8,128)(2,1)S(1)}, bf16[96,768]{1,0:T(8,128)(2,1)S(1)}, u32[]{:S(2)}, u32[]{:S(2)}) collective-permute-start(bf16[96,768]{1,0:T(8,128)(2,1)S(1)} %shard_map.102), channel_id=1, source_target_pairs={{128,0},{129,1},{130,2},{131,3},{132,4},{133,5},{134,6},{135,7},{1... | collective-permute-start | bytes 442376 | tf_op jit(solution)/shard_map/ppermute | solution.py:390
  163.2 16.0 %copy-start.6 = (bf16[1,768,384]{2,1,0:T(8,128)(2,1)S(1)}, bf16[1,768,384]{2,1,0:T(8,128)(2,1)}, u32[]{:S(2)}) copy-start(bf16[1,768,384]{2,1,0:T(8,128)(2,1)} %param.13) | copy-start | bytes 1769476
  163.2 16.0 %copy-start.8 = (bf16[1,384,768]{2,1,0:T(8,128)(2,1)S(1)}, bf16[1,384,768]{2,1,0:T(8,128)(2,1)}, u32[]{:S(2)}) copy-start(bf16[1,384,768]{2,1,0:T(8,128)(2,1)} %param.14) | copy-start | bytes 1769476
  175.3 3.9 %collective-permute-start.14 = (bf16[4,96,768]{2,1,0:T(8,128)(2,1)S(1)}, bf16[4,96,768]{2,1,0:T(8,128)(2,1)S(1)}, u32[]{:S(2)}, u32[]{:S(2)}) collective-permute-start(bf16[4,96,768]{2,1,0:T(8,128)(2,1)S(1)} %all_to_all.5.recv), channel_id=1, source_target_pairs={{0,1},{1,0},{2,3},{3,2},{4,5},{5,4},{6,7},{7,6},{8,9},{9,8},{10,11... | collective-permute-start | bytes 1769480 | tf_op jit(solution)/shard_map/ppermute | solution.py:359
  181.7 18.1 %collective-permute-start.15 = (bf16[8,48,768]{2,1,0:T(8,128)(2,1)S(1)}, bf16[8,48,768]{2,1,0:T(8,128)(2,1)S(1)}, u32[]{:S(2)}, u32[]{:S(2)}) collective-permute-start(bf16[8,48,768]{2,1,0:T(8,128)(2,1)S(1)} %get-tuple-element.51), channel_id=1, source_target_pairs={{0,8},{1,17},{2,10},{3,19},{4,12},{5,21},{6,14},{7,23},{8,0},{9,25... | collective-permute-start | bytes 1769480 | tf_op jit(solution)/shard_map/ppermute | solution.py:332
  200.0 12.7 %collective-permute-start.16 = (bf16[4,48,768]{2,1,0:T(8,128)(2,1)S(1)}, bf16[4,48,768]{2,1,0:T(8,128)(2,1)S(1)}, u32[]{:S(2)}, u32[]{:S(2)}) collective-permute-start(bf16[4,48,768]{2,1,0:T(8,128)(2,1)S(1)} %slice.43), channel_id=1, source_target_pairs={{0,16},{1,9},{2,18},{3,11},{4,20},{5,13},{6,22},{7,15},{8,24},{9,1... | collective-permute-start | bytes 884744 | tf_op jit(solution)/shard_map/ppermute | solution.py:332
  212.8 24.4 %collective-permute-start.19 = (bf16[48,768]{1,0:T(8,128)(2,1)S(1)}, bf16[48,768]{1,0:T(8,128)(2,1)S(1)}, u32[]{:S(2)}, u32[]{:S(2)}) collective-permute-start(bf16[48,768]{1,0:T(8,128)(2,1)S(1)} %get-tuple-element.55), channel_id=1, source_target_pairs={{0,96},{8,104},{16,112},{24,120},{32,0},{40,8},{48,16},{56,24},{64... | collective-permute-start | bytes 221192 | tf_op jit(solution)/shard_map/ppermute | solution.py:346
  224.4 17.4 %collective-permute-start.18 = (bf16[48,768]{1,0:T(8,128)(2,1)S(1)}, bf16[48,768]{1,0:T(8,128)(2,1)S(1)}, u32[]{:S(2)}, u32[]{:S(2)}) collective-permute-start(bf16[48,768]{1,0:T(8,128)(2,1)S(1)} %get-tuple-element.56), channel_id=1, source_target_pairs={{0,64},{8,72},{16,80},{24,88},{32,96},{40,104},{48,112},{56,120},{... | collective-permute-start | bytes 221192 | tf_op jit(solution)/shard_map/ppermute | solution.py:346
  229.3 13.2 %collective-permute-start.17 = (bf16[48,768]{1,0:T(8,128)(2,1)S(1)}, bf16[48,768]{1,0:T(8,128)(2,1)S(1)}, u32[]{:S(2)}, u32[]{:S(2)}) collective-permute-start(bf16[48,768]{1,0:T(8,128)(2,1)S(1)} %get-tuple-element.54), channel_id=1, source_target_pairs={{0,32},{8,40},{16,48},{24,56},{32,64},{40,72},{48,80},{56,88},{64,... | collective-permute-start | bytes 221192 | tf_op jit(solution)/shard_map/ppermute | solution.py:346
  (8 other events, 5.8 us)

commit v4 on v3

--- a/solution.py
+++ b/solution.py
@@ -25,6 +25,7 @@
 TAP_ROWS = TAPS * TAPS
 GAIN, SCALE, INVERSE, PARAM_ROWS = TAP_ROWS, TAP_ROWS + 1, TAP_ROWS + 2, 56
 OUT_ROWS = C // DP
+PARAMS = pltpu.CompilerParams(vmem_limit_bytes=56 * 1024 * 1024)
 SMALL = pltpu.CompilerParams(vmem_limit_bytes=24 * 1024 * 1024)
 
 
@@ -280,7 +281,7 @@
             bytes_accessed=2 * C * C * max(pieces, 1),
             transcendentals=0,
         ),
-        compiler_params=SMALL,
+        compiler_params=SMALL if pieces < MP else PARAMS,
     )(active, *operands.values(), *weights)
     return dict(zip(outs, results))
 

time: 244 us -> 228 us (0.934)
  the two profiles are of different devices: /device:TPU:8 before, /device:TPU:2 now
where the time goes in v4:
time: 228 us
  waiting for transfers between devices  118 us (52%)
  starting transfers between devices  59 us (26%)
  Pallas kernels  21.5 us (9%)
  blocking collectives  13.3 us (6%)
  local copies, waits for them, and re-layouts  9.76 us (4%)
  other arithmetic  3.54 us (2%)
    ppermute x6, waiting for transfers between devices, shards(): send = lambda v, source, to: lax.ppermute(v, 'section', [(source, to)])  57.1 us
    ppermute x9, waiting for transfers between devices, shards(): move = lambda v, pairs: lax.ppermute(v, 'mp', pairs)  31.4 us
    ppermute x2, waiting for transfers between devices, sum_over_dp(): lax.ppermute(v, ('dp', 'mp'), [(z * MP + j, (z ^ by[j % 2]) * MP + j) for...  24.6 us
    ppermute x3, starting transfers between devices, sum_over_dp(): total = total + lax.ppermute(block(ahead), 'dp', pairs).astype(F32)  24.4 us
    ppermute x9, starting transfers between devices, shards(): move = lambda v, pairs: lax.ppermute(v, 'mp', pairs)  22 us
    pallas_call x8, Pallas kernels, call_block(): pl.pallas_call(functools.partial(block_kernel, body, names, places), in_s...  18.9 us
    all_to_all x1, blocking collectives, shards(): lax.all_to_all(jnp.broadcast_to(mine[None], (CHIPS, TOK, C)), 'mp', 0, 0,...  13.3 us
    ppermute x6, starting transfers between devices, shards(): send = lambda v, source, to: lax.ppermute(v, 'section', [(source, to)])  6.52 us
  transfers between devices with their start and end apart: 20, of which 12 were waited for; matrix products, arithmetic and copies ran while one was open for 2% of the time, Pallas kernels for 0%

profile of v4, /device:TPU:2, one launch (start us, length us, event | category | flops | bytes accessed | tf_op | source)
XLA Modules:
  0.0 227.7 jit_solution(9339638856140321233)
XLA Ops:
  0.6 1.2 slice_bitcast_fusion.1
  2.0 3.5 %collective-permute-start = (bf16[768,768]{1,0:T(8,128)(2,1)S(1)}, bf16[768,768]{1,0:T(8,128)(2,1)}, u32[]{:S(2)}, u32[]{:S(2)}) collective-permute-start(bf16[768,768]{1,0:T(8,128)(2,1)S(1)} %pad_maximum_fusion.refs_2_.refs_3_.refs_5_), channel_id=1, source_target_pairs={{0,2},{1,7},{2,4},{3,1},{4,6},{5,3},{6,0},{7,5},{8,10},{9,15},{10,... | collective-permute-start | bytes 3538952 | tf_op jit(solution)/shard_map/ppermute | solution.py:360
  7.3 2.0 concatenate.11.refs_1_.refs_2_
  9.3 1.7 multiply_bitcast_fusion
  11.0 10.4 %collective-permute-done.refs_3_.refs_4_.refs_6_ = bf16[768,768]{1,0:T(8,128)(2,1)} collective-permute-done((bf16[768,768]{1,0:T(8,128)(2,1)S(1)}, bf16[768,768]{1,0:T(8,128)(2,1)}, u32[]{:S(2)}, u32[]{:S(2)}) %collective-permute-start) | collective-permute-done | bytes 1179680 | tf_op jit(solution)/shard_map/ppermute | solution.py:360
  21.4 3.7 %collective-permute-start.1 = (bf16[768,768]{1,0:T(8,128)(2,1)S(1)}, bf16[768,768]{1,0:T(8,128)(2,1)S(1)}, u32[]{:S(2)}, u32[]{:S(2)}) collective-permute-start(bf16[768,768]{1,0:T(8,128)(2,1)S(1)} %pad_maximum_fusion.refs_2_.refs_3_.refs_5_), channel_id=1, source_target_pairs={{0,6},{1,3},{2,0},{3,5},{4,2},{5,7},{6,4},{7,1},{8,14},{9,11},{10,... | collective-permute-start | bytes 3538952 | tf_op jit(solution)/shard_map/ppermute | solution.py:360
  25.1 2.1 collective-permute-start.2
  27.3 0.9 copy-done.3
  28.2 0.9 copy-done.8
  29.5 1.9 collective-permute-start.5
  31.4 2.4 %collective-permute-start.6 = (bf16[768,768]{1,0:T(8,128)(2,1)}, bf16[768,768]{1,0:T(8,128)(2,1)}, u32[]{:S(2)}, u32[]{:S(2)}) collective-permute-start(bf16[768,768]{1,0:T(8,128)(2,1)} %collective-permute-done.refs_3_.refs_4_.refs_6_), channel_id=1, source_target_pairs={{0,1},{1,0},{2,3},{3,2},{4,5},{5,4},{6,7},{7,6},{8,9},{9,8},{10,11... | collective-permute-start | bytes 3538952 | tf_op jit(solution)/shard_map/ppermute | solution.py:360
  33.8 18.1 %collective-permute-done.1.refs_2_.refs_6_.refs_7_.refs_9_ = bf16[768,768]{1,0:T(8,128)(2,1)S(1)} collective-permute-done((bf16[768,768]{1,0:T(8,128)(2,1)S(1)}, bf16[768,768]{1,0:T(8,128)(2,1)S(1)}, u32[]{:S(2)}, u32[]{:S(2)}) %collective-permute-start.1) | collective-permute-done | bytes 1179680 | tf_op jit(solution)/shard_map/ppermute | solution.py:360
  52.3 0.6 copy-done.1
  52.9 1.9 collective-permute-start.7
  54.9 2.4 %collective-permute-start.8 = (bf16[768,768]{1,0:T(8,128)(2,1)S(1)}, bf16[768,768]{1,0:T(8,128)(2,1)}, u32[]{:S(2)}, u32[]{:S(2)}) collective-permute-start(bf16[768,768]{1,0:T(8,128)(2,1)S(1)} %collective-permute-done.2.refs_3_.refs_7_.refs_8_.refs_10_), channel_id=1, source_target_pairs={{0,1},{1,0},{2,3},{3,2},{4,5},{5,4},{6,7},{7,6},{8,9},{9,8},{10,11... | collective-permute-start | bytes 3538952 | tf_op jit(solution)/shard_map/ppermute | solution.py:360
  57.3 1.9 collective-permute-start.3
  59.2 1.3 collective-permute-done.3.refs_3_
  60.9 1.3 collective-permute-start.4
  62.3 8.4 %collective-permute-done.4.refs_0_ = bf16[96,768]{1,0:T(8,128)(2,1)} collective-permute-done((bf16[96,768]{1,0:T(8,128)(2,1)}, bf16[96,768]{1,0:T(8,128)(2,1)}, u32[]{:S(2)}, u32[]{:S(2)}) %collective-permute-start.4) | collective-permute-done | bytes 147488 | tf_op jit(solution)/shard_map/ppermute | solution.py:391
  70.6 7.7 %shard_map.98 = (bf16[96,768]{1,0:T(8,128)(2,1)}, bf16[96,768]{1,0:T(8,128)(2,1)}, f32[96,128]{1,0:T(8,128)}, f32[8,96,384]{2,1,0:T(8,128)}) custom-call(s32[1]{0:T(128)} %bitcast.16.sc, bf16[96,768]{1,0:T(8,128)(2,1)} %collective-permute-done.4.refs_0_, f32[56,768]{1,0:T(8,128)} %concatenate.11.refs_1_.refs_2_, bf16[768,768]{1,0:T(8,128)(2,1)} %copy-done, ...), custom_call_target="tpu_custom_call" | custom-call | flops 905969664 | bytes 9437184 | tf_op jit(solution)/shard_map/pallas_call | solution.py:272
  78.4 1.3 collective-permute-start.9
  79.7 3.5 %collective-permute-done.9.refs_0_ = bf16[96,768]{1,0:T(8,128)(2,1)S(1)} collective-permute-done((bf16[96,768]{1,0:T(8,128)(2,1)}, bf16[96,768]{1,0:T(8,128)(2,1)S(1)}, u32[]{:S(2)}, u32[]{:S(2)}) %collective-permute-start.9) | collective-permute-done | bytes 147488 | tf_op jit(solution)/shard_map/ppermute | solution.py:391
  83.1 0.7 copy-done.21
  84.2 0.7 collective-permute-start.10
  84.9 0.6 copy-done.22
  85.9 0.7 collective-permute-start.11
  86.6 0.6 copy-done.16
  87.6 1.3 collective-permute-start.12
  88.9 42.4 %collective-permute-done.12.refs_0_ = bf16[96,768]{1,0:T(8,128)(2,1)S(1)} collective-permute-done((bf16[96,768]{1,0:T(8,128)(2,1)}, bf16[96,768]{1,0:T(8,128)(2,1)S(1)}, u32[]{:S(2)}, u32[]{:S(2)}) %collective-permute-start.12) | collective-permute-done | bytes 147488 | tf_op jit(solution)/shard_map/ppermute | solution.py:391
  131.3 0.7 copy-done.18
  132.0 9.0 %shard_map.102 = bf16[96,768]{1,0:T(8,128)(2,1)} custom-call(s32[1]{0:T(128)} %bitcast.16.sc, bf16[96,768]{1,0:T(8,128)(2,1)} %copy-done.18, f32[56,768]{1,0:T(8,128)} %concatenate.11.refs_1_.refs_2_, bf16[96,768]{1,0:T(8,128)(2,1)} %get-tuple-element.39.refs_2_, f32[96,128]{1,0:T(8,128)} %get-tuple-element.48.refs_3_, ...), custom_call_target="tpu_custom_call" | custom-call | flops 905969664 | bytes 9437184 | tf_op jit(solution)/shard_map/pallas_call | solution.py:272
  141.0 1.3 collective-permute-start.13
  142.4 2.9 %collective-permute-done.13 = bf16[96,768]{1,0:T(8,128)(2,1)S(1)} collective-permute-done((bf16[96,768]{1,0:T(8,128)(2,1)}, bf16[96,768]{1,0:T(8,128)(2,1)S(1)}, u32[]{:S(2)}, u32[]{:S(2)}) %collective-permute-start.13) | collective-permute-done | bytes 147488 | tf_op jit(solution)/shard_map/ppermute | solution.py:391
  145.3 0.9 select_bitcast_fusion
  146.4 13.3 %all_to_all.5.recv = bf16[4,96,768]{2,1,0:T(8,128)(2,1)S(1)} all-to-all(bf16[4,96,768]{2,1,0:T(8,128)(2,1)S(1)} %broadcast_in_dim.46), channel_id=1, replica_groups={{0,2,4,6},{1,3,5,7},{8,10,12,14},{9,11,13,15},{16,18,20,22},{17,19,21,2..., dimensions={0} | all-to-all | bytes 1179648 | tf_op jit(solution)/shard_map/all_to_all | solution.py:471
  159.7 2.1 collective-permute-start.14
  162.0 1.6 collective-permute-done.14.other
  163.6 2.6 %shard_map.103 = (bf16[8,48,768]{2,1,0:T(8,128)(2,1)S(1)}, bf16[8,48,768]{2,1,0:T(8,128)(2,1)S(1)}) custom-call(s32[3]{0:T(128)S(1)} %pad_add_fusion.sc, bf16[4,96,768]{2,1,0:T(8,128)(2,1)S(1)} %all_to_all.5.recv, bf16[4,96,768]{2,1,0:T(8,128)(2,1)S(1)} %collective-permute-done.14.other, f32[1,768]{1,0:T(1,128)S(1)} %copy-done.12, ...), custom_call_target="tpu_custom_call" | custom-call | tf_op jit(solution)/shard_map/pallas_call | solution.py:322
  166.2 2.7 %collective-permute-start.15 = (bf16[8,48,768]{2,1,0:T(8,128)(2,1)S(1)}, bf16[8,48,768]{2,1,0:T(8,128)(2,1)S(1)}, u32[]{:S(2)}, u32[]{:S(2)}) collective-permute-start(bf16[8,48,768]{2,1,0:T(8,128)(2,1)S(1)} %get-tuple-element.51), channel_id=1, source_target_pairs={{0,8},{1,17},{2,10},{3,19},{4,12},{5,21},{6,14},{7,23},{8,0},{9,25... | collective-permute-start | bytes 1769480 | tf_op jit(solution)/shard_map/ppermute | solution.py:333
  168.9 15.4 %collective-permute-done.15 = bf16[8,48,768]{2,1,0:T(8,128)(2,1)S(1)} collective-permute-done((bf16[8,48,768]{2,1,0:T(8,128)(2,1)S(1)}, bf16[8,48,768]{2,1,0:T(8,128)(2,1)S(1)}, u32[]{:S(2)}, u32[]{:S(2)}) %collective-permute-start.15) | collective-permute-done | bytes 589856 | tf_op jit(solution)/shard_map/ppermute | solution.py:333
  184.4 3.4 %collective-permute-start.16 = (bf16[4,48,768]{2,1,0:T(8,128)(2,1)S(1)}, bf16[4,48,768]{2,1,0:T(8,128)(2,1)S(1)}, u32[]{:S(2)}, u32[]{:S(2)}) collective-permute-start(bf16[4,48,768]{2,1,0:T(8,128)(2,1)S(1)} %slice.43), channel_id=1, source_target_pairs={{0,16},{1,9},{2,18},{3,11},{4,20},{5,13},{6,22},{7,15},{8,24},{9,1... | collective-permute-start | bytes 884744 | tf_op jit(solution)/shard_map/ppermute | solution.py:333
  187.9 9.2 %collective-permute-done.16 = bf16[4,48,768]{2,1,0:T(8,128)(2,1)S(1)} collective-permute-done((bf16[4,48,768]{2,1,0:T(8,128)(2,1)S(1)}, bf16[4,48,768]{2,1,0:T(8,128)(2,1)S(1)}, u32[]{:S(2)}, u32[]{:S(2)}) %collective-permute-start.16) | collective-permute-done | bytes 294944 | tf_op jit(solution)/shard_map/ppermute | solution.py:333
  197.2 11.6 %collective-permute-start.19 = (bf16[48,768]{1,0:T(8,128)(2,1)S(1)}, bf16[48,768]{1,0:T(8,128)(2,1)S(1)}, u32[]{:S(2)}, u32[]{:S(2)}) collective-permute-start(bf16[48,768]{1,0:T(8,128)(2,1)S(1)} %get-tuple-element.55), channel_id=1, source_target_pairs={{0,96},{8,104},{16,112},{24,120},{32,0},{40,8},{48,16},{56,24},{64... | collective-permute-start | bytes 221192 | tf_op jit(solution)/shard_map/ppermute | solution.py:347
  208.9 4.9 %collective-permute-start.18 = (bf16[48,768]{1,0:T(8,128)(2,1)S(1)}, bf16[48,768]{1,0:T(8,128)(2,1)S(1)}, u32[]{:S(2)}, u32[]{:S(2)}) collective-permute-start(bf16[48,768]{1,0:T(8,128)(2,1)S(1)} %get-tuple-element.56), channel_id=1, source_target_pairs={{0,64},{8,72},{16,80},{24,88},{32,96},{40,104},{48,112},{56,120},{... | collective-permute-start | bytes 221192 | tf_op jit(solution)/shard_map/ppermute | solution.py:347
  213.8 7.8 %collective-permute-start.17 = (bf16[48,768]{1,0:T(8,128)(2,1)S(1)}, bf16[48,768]{1,0:T(8,128)(2,1)S(1)}, u32[]{:S(2)}, u32[]{:S(2)}) collective-permute-start(bf16[48,768]{1,0:T(8,128)(2,1)S(1)} %get-tuple-element.54), channel_id=1, source_target_pairs={{0,32},{8,40},{16,48},{24,56},{32,64},{40,72},{48,80},{56,88},{64,... | collective-permute-start | bytes 221192 | tf_op jit(solution)/shard_map/ppermute | solution.py:347
  221.6 4.6 %collective-permute-done.18 = bf16[48,768]{1,0:T(8,128)(2,1)S(1)} collective-permute-done((bf16[48,768]{1,0:T(8,128)(2,1)S(1)}, bf16[48,768]{1,0:T(8,128)(2,1)S(1)}, u32[]{:S(2)}, u32[]{:S(2)}) %collective-permute-start.18) | collective-permute-done | bytes 73760 | tf_op jit(solution)/shard_map/ppermute | solution.py:347
  226.3 0.7 collective-permute-done.17
  227.0 0.6 slice_bitcast_fusion.2
  (72 shorter events, 3.9 us)
Async XLA Ops:
  0.6 1.2 copy-start.6
  1.9 3.7 %copy-start.24 = (s32[2]{0:T(128)S(1)}, s32[2]{0:T(128)}, u32[]{:S(2)}) copy-start(s32[2]{0:T(128)} %param.10) | copy-start | bytes 28
  1.9 4.9 %copy-start.19 = (f32[1,7,7,768]{3,0,2,1:T(1,128)S(1)}, f32[1,7,7,768]{3,0,2,1:T(1,128)}, u32[]{:S(2)}) copy-start(f32[1,7,7,768]{3,0,2,1:T(1,128)} %param.11) | copy-start | bytes 451588
  1.9 5.3 %copy-start.23 = (f32[1,768]{1,0:T(1,128)S(1)}, f32[1,768]{1,0:T(1,128)}, u32[]{:S(2)}) copy-start(f32[1,768]{1,0:T(1,128)} %param.12) | copy-start | bytes 9220
  1.9 5.4 %copy-start.12 = (f32[1,768]{1,0:T(1,128)S(1)}, f32[1,768]{1,0:T(1,128)}, u32[]{:S(2)}) copy-start(f32[1,768]{1,0:T(1,128)} %scale.1) | copy-start | bytes 9220
  2.0 27.5 %copy-start = (bf16[768,768]{1,0:T(8,128)(2,1)}, bf16[768,768]{1,0:T(8,128)(2,1)S(1)}, u32[]{:S(2)}) copy-start(bf16[768,768]{1,0:T(8,128)(2,1)S(1)} %pad_maximum_fusion.refs_2_.refs_3_.refs_5_) | copy-start | bytes 3538948
  2.0 19.4 %collective-permute-start = (bf16[768,768]{1,0:T(8,128)(2,1)S(1)}, bf16[768,768]{1,0:T(8,128)(2,1)}, u32[]{:S(2)}, u32[]{:S(2)}) collective-permute-start(bf16[768,768]{1,0:T(8,128)(2,1)S(1)} %pad_maximum_fusion.refs_2_.refs_3_.refs_5_), channel_id=1, source_target_pairs={{0,2},{1,7},{2,4},{3,1},{4,6},{5,3},{6,0},{7,5},{8,10},{9,15},{10,... | collective-permute-start | bytes 3538952 | tf_op jit(solution)/shard_map/ppermute | solution.py:360
  21.4 30.5 %collective-permute-start.1 = (bf16[768,768]{1,0:T(8,128)(2,1)S(1)}, bf16[768,768]{1,0:T(8,128)(2,1)S(1)}, u32[]{:S(2)}, u32[]{:S(2)}) collective-permute-start(bf16[768,768]{1,0:T(8,128)(2,1)S(1)} %pad_maximum_fusion.refs_2_.refs_3_.refs_5_), channel_id=1, source_target_pairs={{0,6},{1,3},{2,0},{3,5},{4,2},{5,7},{6,4},{7,1},{8,14},{9,11},{10,... | collective-permute-start | bytes 3538952 | tf_op jit(solution)/shard_map/ppermute | solution.py:360
  25.1 26.8 %collective-permute-start.2 = (bf16[768,768]{1,0:T(8,128)(2,1)}, bf16[768,768]{1,0:T(8,128)(2,1)S(1)}, u32[]{:S(2)}, u32[]{:S(2)}) collective-permute-start(bf16[768,768]{1,0:T(8,128)(2,1)} %collective-permute-done.refs_3_.refs_4_.refs_6_), channel_id=1, source_target_pairs={{0,2},{1,7},{2,4},{3,1},{4,6},{5,3},{6,0},{7,5},{8,10},{9,15},{10,... | collective-permute-start | bytes 3538952 | tf_op jit(solution)/shard_map/ppermute | solution.py:360
  27.3 0.9 copy-start.3
  28.2 0.9 copy-start.8
  29.5 22.9 %copy-start.10 = (bf16[96,768]{1,0:T(8,128)(2,1)}, bf16[96,768]{1,0:T(8,128)(2,1)S(1)}, u32[]{:S(2)}) copy-start(bf16[96,768]{1,0:T(8,128)(2,1)S(1)} %get-tuple-element.31.refs_0_) | copy-start | bytes 442372
  29.5 32.8 %collective-permute-start.5 = (bf16[768,768]{1,0:T(8,128)(2,1)S(1)}, bf16[768,768]{1,0:T(8,128)(2,1)}, u32[]{:S(2)}, u32[]{:S(2)}) collective-permute-start(bf16[768,768]{1,0:T(8,128)(2,1)S(1)} %pad_maximum_fusion.refs_2_.refs_3_.refs_5_), channel_id=1, source_target_pairs={{0,1},{1,0},{2,3},{3,2},{4,5},{5,4},{6,7},{7,6},{8,9},{9,8},{10,11... | collective-permute-start | bytes 3538952 | tf_op jit(solution)/shard_map/ppermute | solution.py:360
  31.4 30.8 %collective-permute-start.6 = (bf16[768,768]{1,0:T(8,128)(2,1)}, bf16[768,768]{1,0:T(8,128)(2,1)}, u32[]{:S(2)}, u32[]{:S(2)}) collective-permute-start(bf16[768,768]{1,0:T(8,128)(2,1)} %collective-permute-done.refs_3_.refs_4_.refs_6_), channel_id=1, source_target_pairs={{0,1},{1,0},{2,3},{3,2},{4,5},{5,4},{6,7},{7,6},{8,9},{9,8},{10,11... | collective-permute-start | bytes 3538952 | tf_op jit(solution)/shard_map/ppermute | solution.py:360
  51.9 1.0 copy-start.1
  51.9 3.0 %copy-start.2 = (bf16[768,768]{1,0:T(8,128)(2,1)}, bf16[768,768]{1,0:T(8,128)(2,1)S(1)}, u32[]{:S(2)}) copy-start(bf16[768,768]{1,0:T(8,128)(2,1)S(1)} %collective-permute-done.2.refs_3_.refs_7_.refs_8_.refs_10_) | copy-start | bytes 3538948
  51.9 8.6 %copy-start.4 = (f32[56,768]{1,0:T(8,128)S(1)}, f32[56,768]{1,0:T(8,128)}, u32[]{:S(2)}) copy-start(f32[56,768]{1,0:T(8,128)} %concatenate.11.refs_1_.refs_2_) | copy-start | bytes 516100
  51.9 8.6 %copy-start.9 = (bf16[96,768]{1,0:T(8,128)(2,1)S(1)}, bf16[96,768]{1,0:T(8,128)(2,1)}, u32[]{:S(2)}) copy-start(bf16[96,768]{1,0:T(8,128)(2,1)} %get-tuple-element.27.refs_0_) | copy-start | bytes 442372
  52.9 17.7 %collective-permute-start.7 = (bf16[768,768]{1,0:T(8,128)(2,1)S(1)}, bf16[768,768]{1,0:T(8,128)(2,1)}, u32[]{:S(2)}, u32[]{:S(2)}) collective-permute-start(bf16[768,768]{1,0:T(8,128)(2,1)S(1)} %collective-permute-done.1.refs_2_.refs_6_.refs_7_.refs_9_), channel_id=1, source_target_pairs={{0,1},{1,0},{2,3},{3,2},{4,5},{5,4},{6,7},{7,6},{8,9},{9,8},{10,11... | collective-permute-start | bytes 3538952 | tf_op jit(solution)/shard_map/ppermute | solution.py:360
  54.9 15.8 %collective-permute-start.8 = (bf16[768,768]{1,0:T(8,128)(2,1)S(1)}, bf16[768,768]{1,0:T(8,128)(2,1)}, u32[]{:S(2)}, u32[]{:S(2)}) collective-permute-start(bf16[768,768]{1,0:T(8,128)(2,1)S(1)} %collective-permute-done.2.refs_3_.refs_7_.refs_8_.refs_10_), channel_id=1, source_target_pairs={{0,1},{1,0},{2,3},{3,2},{4,5},{5,4},{6,7},{7,6},{8,9},{9,8},{10,11... | collective-permute-start | bytes 3538952 | tf_op jit(solution)/shard_map/ppermute | solution.py:360
  57.3 3.3 %collective-permute-start.3 = (bf16[96,768]{1,0:T(8,128)(2,1)S(1)}, bf16[96,768]{1,0:T(8,128)(2,1)S(1)}, u32[]{:S(2)}, u32[]{:S(2)}) collective-permute-start(bf16[96,768]{1,0:T(8,128)(2,1)S(1)} %shard_map.96.refs_2_), channel_id=1, source_target_pairs={{0,1},{1,0},{2,3},{3,2},{4,5},{5,4},{6,7},{7,6},{8,9},{9,8},{10,11... | collective-permute-start | bytes 442376 | tf_op jit(solution)/shard_map/ppermute | solution.py:360
  60.9 9.7 %collective-permute-start.4 = (bf16[96,768]{1,0:T(8,128)(2,1)}, bf16[96,768]{1,0:T(8,128)(2,1)}, u32[]{:S(2)}, u32[]{:S(2)}) collective-permute-start(bf16[96,768]{1,0:T(8,128)(2,1)} %shard_map.97), channel_id=1, source_target_pairs={{0,128},{1,129},{2,130},{3,131},{4,132},{5,133},{6,134},{7,135},{8... | collective-permute-start | bytes 442376 | tf_op jit(solution)/shard_map/ppermute | solution.py:391
  78.4 4.8 %collective-permute-start.9 = (bf16[96,768]{1,0:T(8,128)(2,1)}, bf16[96,768]{1,0:T(8,128)(2,1)S(1)}, u32[]{:S(2)}, u32[]{:S(2)}) collective-permute-start(bf16[96,768]{1,0:T(8,128)(2,1)} %get-tuple-element.40), channel_id=1, source_target_pairs={{128,256},{129,257},{130,258},{131,259},{132,260},{133,261},{134,2... | collective-permute-start | bytes 442376 | tf_op jit(solution)/shard_map/ppermute | solution.py:391
  83.1 0.7 copy-start.21
  84.2 0.7 collective-permute-start.10
  84.9 0.7 copy-start.22
  85.9 0.7 collective-permute-start.11
  86.6 0.7 copy-start.16
  87.6 43.7 %collective-permute-start.12 = (bf16[96,768]{1,0:T(8,128)(2,1)}, bf16[96,768]{1,0:T(8,128)(2,1)S(1)}, u32[]{:S(2)}, u32[]{:S(2)}) collective-permute-start(bf16[96,768]{1,0:T(8,128)(2,1)} %shard_map.101), channel_id=1, source_target_pairs={{256,128},{257,129},{258,130},{259,131},{260,132},{261,133},{262,1... | collective-permute-start | bytes 442376 | tf_op jit(solution)/shard_map/ppermute | solution.py:391
  131.3 0.7 copy-start.18
  132.0 10.4 %copy-start.11 = (bf16[96,768]{1,0:T(8,128)(2,1)S(1)}, bf16[96,768]{1,0:T(8,128)(2,1)}, u32[]{:S(2)}) copy-start(bf16[96,768]{1,0:T(8,128)(2,1)} %copy-done.10) | copy-start | bytes 442372
  132.0 10.4 %copy-start.14 = (bf16[96,768]{1,0:T(8,128)(2,1)S(1)}, bf16[96,768]{1,0:T(8,128)(2,1)}, u32[]{:S(2)}) copy-start(bf16[96,768]{1,0:T(8,128)(2,1)} %get-tuple-element.39.refs_2_) | copy-start | bytes 442372
  132.0 10.4 %copy-start.15 = (bf16[96,768]{1,0:T(8,128)(2,1)S(1)}, bf16[96,768]{1,0:T(8,128)(2,1)}, u32[]{:S(2)}) copy-start(bf16[96,768]{1,0:T(8,128)(2,1)} %get-tuple-element.41.refs_2_) | copy-start | bytes 442372
  132.0 10.4 %copy-start.20 = (bf16[96,768]{1,0:T(8,128)(2,1)S(1)}, bf16[96,768]{1,0:T(8,128)(2,1)}, u32[]{:S(2)}) copy-start(bf16[96,768]{1,0:T(8,128)(2,1)} %get-tuple-element.44) | copy-start | bytes 442372
  132.0 13.3 %copy-start.13 = (bf16[96,768]{1,0:T(8,128)(2,1)S(1)}, bf16[96,768]{1,0:T(8,128)(2,1)}, u32[]{:S(2)}) copy-start(bf16[96,768]{1,0:T(8,128)(2,1)} %get-tuple-element.43.refs_1_) | copy-start | bytes 442372
  132.0 13.3 %copy-start.17 = (bf16[96,768]{1,0:T(8,128)(2,1)S(1)}, bf16[96,768]{1,0:T(8,128)(2,1)}, u32[]{:S(2)}) copy-start(bf16[96,768]{1,0:T(8,128)(2,1)} %copy-done.16) | copy-start | bytes 442372
  141.0 4.3 %collective-permute-start.13 = (bf16[96,768]{1,0:T(8,128)(2,1)}, bf16[96,768]{1,0:T(8,128)(2,1)S(1)}, u32[]{:S(2)}, u32[]{:S(2)}) collective-permute-start(bf16[96,768]{1,0:T(8,128)(2,1)} %shard_map.102), channel_id=1, source_target_pairs={{128,0},{129,1},{130,2},{131,3},{132,4},{133,5},{134,6},{135,7},{1... | collective-permute-start | bytes 442376 | tf_op jit(solution)/shard_map/ppermute | solution.py:391
  146.3 17.3 %copy-start.5 = (bf16[1,768,384]{2,1,0:T(8,128)(2,1)S(1)}, bf16[1,768,384]{2,1,0:T(8,128)(2,1)}, u32[]{:S(2)}) copy-start(bf16[1,768,384]{2,1,0:T(8,128)(2,1)} %param.13) | copy-start | bytes 1769476
  146.3 17.3 %copy-start.7 = (bf16[1,384,768]{2,1,0:T(8,128)(2,1)S(1)}, bf16[1,384,768]{2,1,0:T(8,128)(2,1)}, u32[]{:S(2)}) copy-start(bf16[1,384,768]{2,1,0:T(8,128)(2,1)} %param.14) | copy-start | bytes 1769476
  159.7 3.9 %collective-permute-start.14 = (bf16[4,96,768]{2,1,0:T(8,128)(2,1)S(1)}, bf16[4,96,768]{2,1,0:T(8,128)(2,1)S(1)}, u32[]{:S(2)}, u32[]{:S(2)}) collective-permute-start(bf16[4,96,768]{2,1,0:T(8,128)(2,1)S(1)} %all_to_all.5.recv), channel_id=1, source_target_pairs={{0,1},{1,0},{2,3},{3,2},{4,5},{5,4},{6,7},{7,6},{8,9},{9,8},{10,11... | collective-permute-start | bytes 1769480 | tf_op jit(solution)/shard_map/ppermute | solution.py:360
  166.2 18.1 %collective-permute-start.15 = (bf16[8,48,768]{2,1,0:T(8,128)(2,1)S(1)}, bf16[8,48,768]{2,1,0:T(8,128)(2,1)S(1)}, u32[]{:S(2)}, u32[]{:S(2)}) collective-permute-start(bf16[8,48,768]{2,1,0:T(8,128)(2,1)S(1)} %get-tuple-element.51), channel_id=1, source_target_pairs={{0,8},{1,17},{2,10},{3,19},{4,12},{5,21},{6,14},{7,23},{8,0},{9,25... | collective-permute-start | bytes 1769480 | tf_op jit(solution)/shard_map/ppermute | solution.py:333
  184.4 12.7 %collective-permute-start.16 = (bf16[4,48,768]{2,1,0:T(8,128)(2,1)S(1)}, bf16[4,48,768]{2,1,0:T(8,128)(2,1)S(1)}, u32[]{:S(2)}, u32[]{:S(2)}) collective-permute-start(bf16[4,48,768]{2,1,0:T(8,128)(2,1)S(1)} %slice.43), channel_id=1, source_target_pairs={{0,16},{1,9},{2,18},{3,11},{4,20},{5,13},{6,22},{7,15},{8,24},{9,1... | collective-permute-start | bytes 884744 | tf_op jit(solution)/shard_map/ppermute | solution.py:333
  197.2 24.4 %collective-permute-start.19 = (bf16[48,768]{1,0:T(8,128)(2,1)S(1)}, bf16[48,768]{1,0:T(8,128)(2,1)S(1)}, u32[]{:S(2)}, u32[]{:S(2)}) collective-permute-start(bf16[48,768]{1,0:T(8,128)(2,1)S(1)} %get-tuple-element.55), channel_id=1, source_target_pairs={{0,96},{8,104},{16,112},{24,120},{32,0},{40,8},{48,16},{56,24},{64... | collective-permute-start | bytes 221192 | tf_op jit(solution)/shard_map/ppermute | solution.py:347
  208.9 17.4 %collective-permute-start.18 = (bf16[48,768]{1,0:T(8,128)(2,1)S(1)}, bf16[48,768]{1,0:T(8,128)(2,1)S(1)}, u32[]{:S(2)}, u32[]{:S(2)}) collective-permute-start(bf16[48,768]{1,0:T(8,128)(2,1)S(1)} %get-tuple-element.56), channel_id=1, source_target_pairs={{0,64},{8,72},{16,80},{24,88},{32,96},{40,104},{48,112},{56,120},{... | collective-permute-start | bytes 221192 | tf_op jit(solution)/shard_map/ppermute | solution.py:347
  213.8 13.2 %collective-permute-start.17 = (bf16[48,768]{1,0:T(8,128)(2,1)S(1)}, bf16[48,768]{1,0:T(8,128)(2,1)S(1)}, u32[]{:S(2)}, u32[]{:S(2)}) collective-permute-start(bf16[48,768]{1,0:T(8,128)(2,1)S(1)} %get-tuple-element.54), channel_id=1, source_target_pairs={{0,32},{8,40},{16,48},{24,56},{32,64},{40,72},{48,80},{56,88},{64,... | collective-permute-start | bytes 221192 | tf_op jit(solution)/shard_map/ppermute | solution.py:347

commit v5 on v4

--- a/solution.py
+++ b/solution.py
@@ -68,10 +68,15 @@
 class Weights:
     def __init__(self, refs, places, buffer, sems, slope=None, slopes=None):
         self.places = places
-        self.ahead = len(places) if slope is None else 3
+        self.ahead = len(places) if slope is None else 5
         self.copies = []
         for at, (ref, group) in enumerate(zip(refs, places)):
-            copies = [pltpu.make_async_copy(ref, buffer.at[group], sems.at[at])]
+            copies = []
+            for half, sem in ((1, 40 + at), (0, at)):
+                rows = pl.ds(half * HID, HID)
+                copies.append(
+                    pltpu.make_async_copy(ref.at[rows], buffer.at[group, rows], sems.at[sem])
+                )
             if slope is not None:
                 copies.append(
                     pltpu.make_async_copy(
@@ -144,7 +149,7 @@
     "total": pltpu.VMEM((TOK, C), F32),
     "slopes": pltpu.VMEM((MP, TOK, HID), F32),
     "buffer": pltpu.VMEM((MP, C, C), BF16),
-    "sems": pltpu.SemaphoreType.DMA((40,)),
+    "sems": pltpu.SemaphoreType.DMA((48,)),
 }
 
 

time: 228 us -> 229 us (level)
  the two profiles are of different devices: /device:TPU:2 before, /device:TPU:8 now
where the time goes in v5:
time: 229 us; the launch traced here: 228 us
  waiting for transfers between devices  129 us (56%)
  starting transfers between devices  60.2 us (26%)
  Pallas kernels  12.9 us (6%)
  blocking collectives  12 us (5%)
  local copies, waits for them, and re-layouts  9.11 us (4%)
  other arithmetic  2.63 us (1%)
    ppermute x6, waiting for transfers between devices, shards(): send = lambda v, source, to: lax.ppermute(v, 'section', [(source, to)])  72.2 us
    ppermute x9, waiting for transfers between devices, shards(): move = lambda v, pairs: lax.ppermute(v, 'mp', pairs)  27.1 us
    ppermute x2, waiting for transfers between devices, sum_over_dp(): lax.ppermute(v, ('dp', 'mp'), [(z * MP + j, (z ^ by[j % 2]) * MP + j) for...  24.6 us
    ppermute x3, starting transfers between devices, sum_over_dp(): total = total + lax.ppermute(block(ahead), 'dp', pairs).astype(F32)  24.3 us
    ppermute x9, starting transfers between devices, shards(): move = lambda v, pairs: lax.ppermute(v, 'mp', pairs)  23.8 us
    all_to_all x1, blocking collectives, shards(): lax.all_to_all(jnp.broadcast_to(mine[None], (CHIPS, TOK, C)), 'mp', 0, 0,...  12 us
    pallas_call x8, Pallas kernels, call_block(): pl.pallas_call(functools.partial(block_kernel, body, names, places), in_s...  10.3 us
    ppermute x2, starting transfers between devices, sum_over_dp(): lax.ppermute(v, ('dp', 'mp'), [(z * MP + j, (z ^ by[j % 2]) * MP + j) for...  6.08 us
  transfers between devices with their start and end apart: 20, of which 10 were waited for; matrix products, arithmetic and copies ran while one was open for 2% of the time, Pallas kernels for 4%

profile of v5, /device:TPU:8, one launch (start us, length us, event | category | flops | bytes accessed | tf_op | source)
XLA Modules:
  0.0 228.0 jit_solution(3798518276853477440)
XLA Ops:
  0.6 1.2 slice_bitcast_fusion.1
  2.0 3.5 %collective-permute-start = (bf16[768,768]{1,0:T(8,128)(2,1)S(1)}, bf16[768,768]{1,0:T(8,128)(2,1)}, u32[]{:S(2)}, u32[]{:S(2)}) collective-permute-start(bf16[768,768]{1,0:T(8,128)(2,1)S(1)} %pad_maximum_fusion.refs_2_.refs_3_.refs_5_), channel_id=1, source_target_pairs={{0,2},{1,7},{2,4},{3,1},{4,6},{5,3},{6,0},{7,5},{8,10},{9,15},{10,... | collective-permute-start | bytes 3538952 | tf_op jit(solution)/shard_map/ppermute | solution.py:365
  5.5 0.6 dynamic_slice.25
  7.3 2.0 concatenate.11.refs_1_.refs_2_
  9.3 1.7 multiply_bitcast_fusion
  11.0 13.2 %collective-permute-done.refs_3_.refs_4_.refs_6_ = bf16[768,768]{1,0:T(8,128)(2,1)} collective-permute-done((bf16[768,768]{1,0:T(8,128)(2,1)S(1)}, bf16[768,768]{1,0:T(8,128)(2,1)}, u32[]{:S(2)}, u32[]{:S(2)}) %collective-permute-start) | collective-permute-done | bytes 1179680 | tf_op jit(solution)/shard_map/ppermute | solution.py:365
  24.2 5.7 %collective-permute-start.1 = (bf16[768,768]{1,0:T(8,128)(2,1)S(1)}, bf16[768,768]{1,0:T(8,128)(2,1)S(1)}, u32[]{:S(2)}, u32[]{:S(2)}) collective-permute-start(bf16[768,768]{1,0:T(8,128)(2,1)S(1)} %pad_maximum_fusion.refs_2_.refs_3_.refs_5_), channel_id=1, source_target_pairs={{0,6},{1,3},{2,0},{3,5},{4,2},{5,7},{6,4},{7,1},{8,14},{9,11},{10,... | collective-permute-start | bytes 3538952 | tf_op jit(solution)/shard_map/ppermute | solution.py:365
  29.9 1.9 collective-permute-start.2
  31.8 0.9 copy-done.3
  32.7 0.9 copy-done.8
  33.7 3.9 %shard_map.95 = (bf16[96,768]{1,0:T(8,128)(2,1)S(1)}, f32[96,768]{1,0:T(8,128)S(1)}) custom-call(s32[1]{0:T(128)} %bitcast.3.sc, bf16[96,768]{1,0:T(8,128)(2,1)S(1)} %copy-done.8, f32[56,768]{1,0:T(8,128)S(1)} %copy-done.3, bf16[768,768]{1,0:T(8,128)(2,1)S(1)} %pad_maximum_fusion.refs_2_.refs_3_.refs_5_, ...), custom_call_target="tpu_custom_call" | custom-call | flops 226492416 | bytes 2359296 | tf_op jit(solution)/shard_map/pallas_call | solution.py:277
  37.5 1.9 collective-permute-start.5
  39.5 2.4 %collective-permute-start.6 = (bf16[768,768]{1,0:T(8,128)(2,1)}, bf16[768,768]{1,0:T(8,128)(2,1)}, u32[]{:S(2)}, u32[]{:S(2)}) collective-permute-start(bf16[768,768]{1,0:T(8,128)(2,1)} %collective-permute-done.refs_3_.refs_4_.refs_6_), channel_id=1, source_target_pairs={{0,1},{1,0},{2,3},{3,2},{4,5},{5,4},{6,7},{7,6},{8,9},{9,8},{10,11... | collective-permute-start | bytes 3538952 | tf_op jit(solution)/shard_map/ppermute | solution.py:365
  41.9 10.9 %collective-permute-done.1.refs_2_.refs_6_.refs_7_.refs_9_ = bf16[768,768]{1,0:T(8,128)(2,1)S(1)} collective-permute-done((bf16[768,768]{1,0:T(8,128)(2,1)S(1)}, bf16[768,768]{1,0:T(8,128)(2,1)S(1)}, u32[]{:S(2)}, u32[]{:S(2)}) %collective-permute-start.1) | collective-permute-done | bytes 1179680 | tf_op jit(solution)/shard_map/ppermute | solution.py:365
  52.8 2.4 %shard_map.96.refs_2_ = bf16[96,768]{1,0:T(8,128)(2,1)S(1)} custom-call(s32[1]{0:T(128)} %bitcast.3.sc, bf16[96,768]{1,0:T(8,128)(2,1)S(1)} %get-tuple-element.31.refs_0_, f32[96,768]{1,0:T(8,128)S(1)} %get-tuple-element.33.refs_1_, bf16[768,768]{1,0:T(8,128)(2,1)S(1)} %collective-permute-done.1.refs_2_.refs_6_.refs_7_.refs_9_, ...), custom_call_target="tpu_custom_call" | custom-call | flops 226492416 | bytes 2359296 | tf_op jit(solution)/shard_map/pallas_call | solution.py:277
  55.2 1.9 collective-permute-start.7
  57.2 2.4 %collective-permute-start.8 = (bf16[768,768]{1,0:T(8,128)(2,1)S(1)}, bf16[768,768]{1,0:T(8,128)(2,1)}, u32[]{:S(2)}, u32[]{:S(2)}) collective-permute-start(bf16[768,768]{1,0:T(8,128)(2,1)S(1)} %collective-permute-done.2.refs_3_.refs_7_.refs_8_.refs_10_), channel_id=1, source_target_pairs={{0,1},{1,0},{2,3},{3,2},{4,5},{5,4},{6,7},{7,6},{8,9},{9,8},{10,11... | collective-permute-start | bytes 3538952 | tf_op jit(solution)/shard_map/ppermute | solution.py:365
  59.6 1.9 collective-permute-start.3
  61.5 1.3 collective-permute-done.3.refs_3_
  62.9 1.9 shard_map.97
  64.8 2.0 collective-permute-start.4
  66.8 3.3 %collective-permute-done.4.refs_0_ = bf16[96,768]{1,0:T(8,128)(2,1)} collective-permute-done((bf16[96,768]{1,0:T(8,128)(2,1)}, bf16[96,768]{1,0:T(8,128)(2,1)}, u32[]{:S(2)}, u32[]{:S(2)}) %collective-permute-start.4) | collective-permute-done | bytes 147488 | tf_op jit(solution)/shard_map/ppermute | solution.py:396
  70.1 0.4 shard_map.98
  70.5 0.7 collective-permute-start.9
  71.2 0.6 copy-done.21
  72.3 0.7 collective-permute-start.10
  73.0 0.6 copy-done.22
  74.1 0.7 collective-permute-start.11
  74.8 0.6 copy-done.16
  75.9 0.7 collective-permute-start.12
  76.6 0.6 copy-done.18
  77.3 0.4 shard_map.102
  77.7 1.3 collective-permute-start.13
  79.1 68.9 %collective-permute-done.13 = bf16[96,768]{1,0:T(8,128)(2,1)S(1)} collective-permute-done((bf16[96,768]{1,0:T(8,128)(2,1)}, bf16[96,768]{1,0:T(8,128)(2,1)S(1)}, u32[]{:S(2)}, u32[]{:S(2)}) %collective-permute-start.13) | collective-permute-done | bytes 147488 | tf_op jit(solution)/shard_map/ppermute | solution.py:396
  148.2 12.0 %all_to_all.5.recv = bf16[4,96,768]{2,1,0:T(8,128)(2,1)S(1)} all-to-all(bf16[4,96,768]{2,1,0:T(8,128)(2,1)S(1)} %broadcast_in_dim.46), channel_id=1, replica_groups={{0,2,4,6},{1,3,5,7},{8,10,12,14},{9,11,13,15},{16,18,20,22},{17,19,21,2..., dimensions={0} | all-to-all | bytes 1179648 | tf_op jit(solution)/shard_map/all_to_all | solution.py:476
  160.2 2.1 collective-permute-start.14
  162.5 1.6 collective-permute-done.14.other
  164.1 2.6 %shard_map.103 = (bf16[8,48,768]{2,1,0:T(8,128)(2,1)S(1)}, bf16[8,48,768]{2,1,0:T(8,128)(2,1)S(1)}) custom-call(s32[3]{0:T(128)S(1)} %pad_add_fusion.sc, bf16[4,96,768]{2,1,0:T(8,128)(2,1)S(1)} %all_to_all.5.recv, bf16[4,96,768]{2,1,0:T(8,128)(2,1)S(1)} %collective-permute-done.14.other, f32[1,768]{1,0:T(1,128)S(1)} %copy-done.12, ...), custom_call_target="tpu_custom_call" | custom-call | tf_op jit(solution)/shard_map/pallas_call | solution.py:327
  166.6 2.7 %collective-permute-start.15 = (bf16[8,48,768]{2,1,0:T(8,128)(2,1)S(1)}, bf16[8,48,768]{2,1,0:T(8,128)(2,1)S(1)}, u32[]{:S(2)}, u32[]{:S(2)}) collective-permute-start(bf16[8,48,768]{2,1,0:T(8,128)(2,1)S(1)} %get-tuple-element.51), channel_id=1, source_target_pairs={{0,8},{1,17},{2,10},{3,19},{4,12},{5,21},{6,14},{7,23},{8,0},{9,25... | collective-permute-start | bytes 1769480 | tf_op jit(solution)/shard_map/ppermute | solution.py:338
  169.3 15.4 %collective-permute-done.15 = bf16[8,48,768]{2,1,0:T(8,128)(2,1)S(1)} collective-permute-done((bf16[8,48,768]{2,1,0:T(8,128)(2,1)S(1)}, bf16[8,48,768]{2,1,0:T(8,128)(2,1)S(1)}, u32[]{:S(2)}, u32[]{:S(2)}) %collective-permute-start.15) | collective-permute-done | bytes 589856 | tf_op jit(solution)/shard_map/ppermute | solution.py:338
  184.9 3.4 %collective-permute-start.16 = (bf16[4,48,768]{2,1,0:T(8,128)(2,1)S(1)}, bf16[4,48,768]{2,1,0:T(8,128)(2,1)S(1)}, u32[]{:S(2)}, u32[]{:S(2)}) collective-permute-start(bf16[4,48,768]{2,1,0:T(8,128)(2,1)S(1)} %slice.43), channel_id=1, source_target_pairs={{0,16},{1,9},{2,18},{3,11},{4,20},{5,13},{6,22},{7,15},{8,24},{9,1... | collective-permute-start | bytes 884744 | tf_op jit(solution)/shard_map/ppermute | solution.py:338
  188.4 9.2 %collective-permute-done.16 = bf16[4,48,768]{2,1,0:T(8,128)(2,1)S(1)} collective-permute-done((bf16[4,48,768]{2,1,0:T(8,128)(2,1)S(1)}, bf16[4,48,768]{2,1,0:T(8,128)(2,1)S(1)}, u32[]{:S(2)}, u32[]{:S(2)}) %collective-permute-start.16) | collective-permute-done | bytes 294944 | tf_op jit(solution)/shard_map/ppermute | solution.py:338
  197.7 11.6 %collective-permute-start.19 = (bf16[48,768]{1,0:T(8,128)(2,1)S(1)}, bf16[48,768]{1,0:T(8,128)(2,1)S(1)}, u32[]{:S(2)}, u32[]{:S(2)}) collective-permute-start(bf16[48,768]{1,0:T(8,128)(2,1)S(1)} %get-tuple-element.55), channel_id=1, source_target_pairs={{0,96},{8,104},{16,112},{24,120},{32,0},{40,8},{48,16},{56,24},{64... | collective-permute-start | bytes 221192 | tf_op jit(solution)/shard_map/ppermute | solution.py:352
  209.3 4.9 %collective-permute-start.18 = (bf16[48,768]{1,0:T(8,128)(2,1)S(1)}, bf16[48,768]{1,0:T(8,128)(2,1)S(1)}, u32[]{:S(2)}, u32[]{:S(2)}) collective-permute-start(bf16[48,768]{1,0:T(8,128)(2,1)S(1)} %get-tuple-element.56), channel_id=1, source_target_pairs={{0,64},{8,72},{16,80},{24,88},{32,96},{40,104},{48,112},{56,120},{... | collective-permute-start | bytes 221192 | tf_op jit(solution)/shard_map/ppermute | solution.py:352
  214.2 7.8 %collective-permute-start.17 = (bf16[48,768]{1,0:T(8,128)(2,1)S(1)}, bf16[48,768]{1,0:T(8,128)(2,1)S(1)}, u32[]{:S(2)}, u32[]{:S(2)}) collective-permute-start(bf16[48,768]{1,0:T(8,128)(2,1)S(1)} %get-tuple-element.54), channel_id=1, source_target_pairs={{0,32},{8,40},{16,48},{24,56},{32,64},{40,72},{48,80},{56,88},{64,... | collective-permute-start | bytes 221192 | tf_op jit(solution)/shard_map/ppermute | solution.py:352
  222.1 4.5 %collective-permute-done.18 = bf16[48,768]{1,0:T(8,128)(2,1)S(1)} collective-permute-done((bf16[48,768]{1,0:T(8,128)(2,1)S(1)}, bf16[48,768]{1,0:T(8,128)(2,1)S(1)}, u32[]{:S(2)}, u32[]{:S(2)}) %collective-permute-start.18) | collective-permute-done | bytes 73760 | tf_op jit(solution)/shard_map/ppermute | solution.py:352
  226.6 0.7 collective-permute-done.17
  227.3 0.6 slice_bitcast_fusion.2
  (72 shorter events, 2.5 us)
Async XLA Ops:
  0.6 1.2 copy-start.6
  1.9 3.7 %copy-start.24 = (s32[2]{0:T(128)S(1)}, s32[2]{0:T(128)}, u32[]{:S(2)}) copy-start(s32[2]{0:T(128)} %param.10) | copy-start | bytes 28
  1.9 4.9 %copy-start.19 = (f32[1,7,7,768]{3,0,2,1:T(1,128)S(1)}, f32[1,7,7,768]{3,0,2,1:T(1,128)}, u32[]{:S(2)}) copy-start(f32[1,7,7,768]{3,0,2,1:T(1,128)} %param.11) | copy-start | bytes 451588
  1.9 5.3 %copy-start.23 = (f32[1,768]{1,0:T(1,128)S(1)}, f32[1,768]{1,0:T(1,128)}, u32[]{:S(2)}) copy-start(f32[1,768]{1,0:T(1,128)} %param.12) | copy-start | bytes 9220
  1.9 5.4 %copy-start.12 = (f32[1,768]{1,0:T(1,128)S(1)}, f32[1,768]{1,0:T(1,128)}, u32[]{:S(2)}) copy-start(f32[1,768]{1,0:T(1,128)} %scale.1) | copy-start | bytes 9220
  2.0 35.6 %copy-start = (bf16[768,768]{1,0:T(8,128)(2,1)}, bf16[768,768]{1,0:T(8,128)(2,1)S(1)}, u32[]{:S(2)}) copy-start(bf16[768,768]{1,0:T(8,128)(2,1)S(1)} %pad_maximum_fusion.refs_2_.refs_3_.refs_5_) | copy-start | bytes 3538948
  2.0 22.2 %collective-permute-start = (bf16[768,768]{1,0:T(8,128)(2,1)S(1)}, bf16[768,768]{1,0:T(8,128)(2,1)}, u32[]{:S(2)}, u32[]{:S(2)}) collective-permute-start(bf16[768,768]{1,0:T(8,128)(2,1)S(1)} %pad_maximum_fusion.refs_2_.refs_3_.refs_5_), channel_id=1, source_target_pairs={{0,2},{1,7},{2,4},{3,1},{4,6},{5,3},{6,0},{7,5},{8,10},{9,15},{10,... | collective-permute-start | bytes 3538952 | tf_op jit(solution)/shard_map/ppermute | solution.py:365
  24.2 28.6 %collective-permute-start.1 = (bf16[768,768]{1,0:T(8,128)(2,1)S(1)}, bf16[768,768]{1,0:T(8,128)(2,1)S(1)}, u32[]{:S(2)}, u32[]{:S(2)}) collective-permute-start(bf16[768,768]{1,0:T(8,128)(2,1)S(1)} %pad_maximum_fusion.refs_2_.refs_3_.refs_5_), channel_id=1, source_target_pairs={{0,6},{1,3},{2,0},{3,5},{4,2},{5,7},{6,4},{7,1},{8,14},{9,11},{10,... | collective-permute-start | bytes 3538952 | tf_op jit(solution)/shard_map/ppermute | solution.py:365
  29.9 22.9 %collective-permute-start.2 = (bf16[768,768]{1,0:T(8,128)(2,1)}, bf16[768,768]{1,0:T(8,128)(2,1)S(1)}, u32[]{:S(2)}, u32[]{:S(2)}) collective-permute-start(bf16[768,768]{1,0:T(8,128)(2,1)} %collective-permute-done.refs_3_.refs_4_.refs_6_), channel_id=1, source_target_pairs={{0,2},{1,7},{2,4},{3,1},{4,6},{5,3},{6,0},{7,5},{8,10},{9,15},{10,... | collective-permute-start | bytes 3538952 | tf_op jit(solution)/shard_map/ppermute | solution.py:365
  31.8 0.9 copy-start.3
  32.7 0.9 copy-start.8
  37.5 17.7 %copy-start.10 = (bf16[96,768]{1,0:T(8,128)(2,1)}, bf16[96,768]{1,0:T(8,128)(2,1)S(1)}, u32[]{:S(2)}) copy-start(bf16[96,768]{1,0:T(8,128)(2,1)S(1)} %get-tuple-element.31.refs_0_) | copy-start | bytes 442372
  37.5 29.2 %collective-permute-start.5 = (bf16[768,768]{1,0:T(8,128)(2,1)S(1)}, bf16[768,768]{1,0:T(8,128)(2,1)}, u32[]{:S(2)}, u32[]{:S(2)}) collective-permute-start(bf16[768,768]{1,0:T(8,128)(2,1)S(1)} %pad_maximum_fusion.refs_2_.refs_3_.refs_5_), channel_id=1, source_target_pairs={{0,1},{1,0},{2,3},{3,2},{4,5},{5,4},{6,7},{7,6},{8,9},{9,8},{10,11... | collective-permute-start | bytes 3538952 | tf_op jit(solution)/shard_map/ppermute | solution.py:365
  39.5 27.3 %collective-permute-start.6 = (bf16[768,768]{1,0:T(8,128)(2,1)}, bf16[768,768]{1,0:T(8,128)(2,1)}, u32[]{:S(2)}, u32[]{:S(2)}) collective-permute-start(bf16[768,768]{1,0:T(8,128)(2,1)} %collective-permute-done.refs_3_.refs_4_.refs_6_), channel_id=1, source_target_pairs={{0,1},{1,0},{2,3},{3,2},{4,5},{5,4},{6,7},{7,6},{8,9},{9,8},{10,11... | collective-permute-start | bytes 3538952 | tf_op jit(solution)/shard_map/ppermute | solution.py:365
  52.8 2.4 %copy-start.1 = (bf16[768,768]{1,0:T(8,128)(2,1)}, bf16[768,768]{1,0:T(8,128)(2,1)S(1)}, u32[]{:S(2)}) copy-start(bf16[768,768]{1,0:T(8,128)(2,1)S(1)} %collective-permute-done.1.refs_2_.refs_6_.refs_7_.refs_9_) | copy-start | bytes 3538948
  52.8 4.3 %copy-start.2 = (bf16[768,768]{1,0:T(8,128)(2,1)}, bf16[768,768]{1,0:T(8,128)(2,1)S(1)}, u32[]{:S(2)}) copy-start(bf16[768,768]{1,0:T(8,128)(2,1)S(1)} %collective-permute-done.2.refs_3_.refs_7_.refs_8_.refs_10_) | copy-start | bytes 3538948
  52.8 10.0 %copy-start.4 = (f32[56,768]{1,0:T(8,128)S(1)}, f32[56,768]{1,0:T(8,128)}, u32[]{:S(2)}) copy-start(f32[56,768]{1,0:T(8,128)} %concatenate.11.refs_1_.refs_2_) | copy-start | bytes 516100
  52.8 10.0 %copy-start.9 = (bf16[96,768]{1,0:T(8,128)(2,1)S(1)}, bf16[96,768]{1,0:T(8,128)(2,1)}, u32[]{:S(2)}) copy-start(bf16[96,768]{1,0:T(8,128)(2,1)} %get-tuple-element.27.refs_0_) | copy-start | bytes 442372
  55.2 14.9 %collective-permute-start.7 = (bf16[768,768]{1,0:T(8,128)(2,1)S(1)}, bf16[768,768]{1,0:T(8,128)(2,1)}, u32[]{:S(2)}, u32[]{:S(2)}) collective-permute-start(bf16[768,768]{1,0:T(8,128)(2,1)S(1)} %collective-permute-done.1.refs_2_.refs_6_.refs_7_.refs_9_), channel_id=1, source_target_pairs={{0,1},{1,0},{2,3},{3,2},{4,5},{5,4},{6,7},{7,6},{8,9},{9,8},{10,11... | collective-permute-start | bytes 3538952 | tf_op jit(solution)/shard_map/ppermute | solution.py:365
  57.2 12.9 %collective-permute-start.8 = (bf16[768,768]{1,0:T(8,128)(2,1)S(1)}, bf16[768,768]{1,0:T(8,128)(2,1)}, u32[]{:S(2)}, u32[]{:S(2)}) collective-permute-start(bf16[768,768]{1,0:T(8,128)(2,1)S(1)} %collective-permute-done.2.refs_3_.refs_7_.refs_8_.refs_10_), channel_id=1, source_target_pairs={{0,1},{1,0},{2,3},{3,2},{4,5},{5,4},{6,7},{7,6},{8,9},{9,8},{10,11... | collective-permute-start | bytes 3538952 | tf_op jit(solution)/shard_map/ppermute | solution.py:365
  59.6 3.3 %collective-permute-start.3 = (bf16[96,768]{1,0:T(8,128)(2,1)S(1)}, bf16[96,768]{1,0:T(8,128)(2,1)S(1)}, u32[]{:S(2)}, u32[]{:S(2)}) collective-permute-start(bf16[96,768]{1,0:T(8,128)(2,1)S(1)} %shard_map.96.refs_2_), channel_id=1, source_target_pairs={{0,1},{1,0},{2,3},{3,2},{4,5},{5,4},{6,7},{7,6},{8,9},{9,8},{10,11... | collective-permute-start | bytes 442376 | tf_op jit(solution)/shard_map/ppermute | solution.py:365
  64.8 5.3 %collective-permute-start.4 = (bf16[96,768]{1,0:T(8,128)(2,1)}, bf16[96,768]{1,0:T(8,128)(2,1)}, u32[]{:S(2)}, u32[]{:S(2)}) collective-permute-start(bf16[96,768]{1,0:T(8,128)(2,1)} %shard_map.97), channel_id=1, source_target_pairs={{0,128},{1,129},{2,130},{3,131},{4,132},{5,133},{6,134},{7,135},{8... | collective-permute-start | bytes 442376 | tf_op jit(solution)/shard_map/ppermute | solution.py:396
  70.5 0.7 collective-permute-start.9
  71.2 0.7 copy-start.21
  72.3 0.7 collective-permute-start.10
  73.0 0.7 copy-start.22
  74.1 0.7 collective-permute-start.11
  74.8 0.7 copy-start.16
  75.9 0.7 collective-permute-start.12
  76.6 0.7 copy-start.18
  77.3 1.8 copy-start.11
  77.3 1.8 copy-start.14
  77.3 1.8 copy-start.15
  77.3 1.8 copy-start.20
  77.3 70.7 %copy-start.13 = (bf16[96,768]{1,0:T(8,128)(2,1)S(1)}, bf16[96,768]{1,0:T(8,128)(2,1)}, u32[]{:S(2)}) copy-start(bf16[96,768]{1,0:T(8,128)(2,1)} %get-tuple-element.43.refs_1_) | copy-start | bytes 442372
  77.3 70.7 %copy-start.17 = (bf16[96,768]{1,0:T(8,128)(2,1)S(1)}, bf16[96,768]{1,0:T(8,128)(2,1)}, u32[]{:S(2)}) copy-start(bf16[96,768]{1,0:T(8,128)(2,1)} %copy-done.16) | copy-start | bytes 442372
  77.7 70.3 %collective-permute-start.13 = (bf16[96,768]{1,0:T(8,128)(2,1)}, bf16[96,768]{1,0:T(8,128)(2,1)S(1)}, u32[]{:S(2)}, u32[]{:S(2)}) collective-permute-start(bf16[96,768]{1,0:T(8,128)(2,1)} %shard_map.102), channel_id=1, source_target_pairs={{128,0},{129,1},{130,2},{131,3},{132,4},{133,5},{134,6},{135,7},{1... | collective-permute-start | bytes 442376 | tf_op jit(solution)/shard_map/ppermute | solution.py:396
  148.1 16.0 %copy-start.5 = (bf16[1,768,384]{2,1,0:T(8,128)(2,1)S(1)}, bf16[1,768,384]{2,1,0:T(8,128)(2,1)}, u32[]{:S(2)}) copy-start(bf16[1,768,384]{2,1,0:T(8,128)(2,1)} %param.13) | copy-start | bytes 1769476
  148.1 16.0 %copy-start.7 = (bf16[1,384,768]{2,1,0:T(8,128)(2,1)S(1)}, bf16[1,384,768]{2,1,0:T(8,128)(2,1)}, u32[]{:S(2)}) copy-start(bf16[1,384,768]{2,1,0:T(8,128)(2,1)} %param.14) | copy-start | bytes 1769476
  160.2 3.9 %collective-permute-start.14 = (bf16[4,96,768]{2,1,0:T(8,128)(2,1)S(1)}, bf16[4,96,768]{2,1,0:T(8,128)(2,1)S(1)}, u32[]{:S(2)}, u32[]{:S(2)}) collective-permute-start(bf16[4,96,768]{2,1,0:T(8,128)(2,1)S(1)} %all_to_all.5.recv), channel_id=1, source_target_pairs={{0,1},{1,0},{2,3},{3,2},{4,5},{5,4},{6,7},{7,6},{8,9},{9,8},{10,11... | collective-permute-start | bytes 1769480 | tf_op jit(solution)/shard_map/ppermute | solution.py:365
  166.6 18.1 %collective-permute-start.15 = (bf16[8,48,768]{2,1,0:T(8,128)(2,1)S(1)}, bf16[8,48,768]{2,1,0:T(8,128)(2,1)S(1)}, u32[]{:S(2)}, u32[]{:S(2)}) collective-permute-start(bf16[8,48,768]{2,1,0:T(8,128)(2,1)S(1)} %get-tuple-element.51), channel_id=1, source_target_pairs={{0,8},{1,17},{2,10},{3,19},{4,12},{5,21},{6,14},{7,23},{8,0},{9,25... | collective-permute-start | bytes 1769480 | tf_op jit(solution)/shard_map/ppermute | solution.py:338
  184.9 12.7 %collective-permute-start.16 = (bf16[4,48,768]{2,1,0:T(8,128)(2,1)S(1)}, bf16[4,48,768]{2,1,0:T(8,128)(2,1)S(1)}, u32[]{:S(2)}, u32[]{:S(2)}) collective-permute-start(bf16[4,48,768]{2,1,0:T(8,128)(2,1)S(1)} %slice.43), channel_id=1, source_target_pairs={{0,16},{1,9},{2,18},{3,11},{4,20},{5,13},{6,22},{7,15},{8,24},{9,1... | collective-permute-start | bytes 884744 | tf_op jit(solution)/shard_map/ppermute | solution.py:338
  197.7 24.4 %collective-permute-start.19 = (bf16[48,768]{1,0:T(8,128)(2,1)S(1)}, bf16[48,768]{1,0:T(8,128)(2,1)S(1)}, u32[]{:S(2)}, u32[]{:S(2)}) collective-permute-start(bf16[48,768]{1,0:T(8,128)(2,1)S(1)} %get-tuple-element.55), channel_id=1, source_target_pairs={{0,96},{8,104},{16,112},{24,120},{32,0},{40,8},{48,16},{56,24},{64... | collective-permute-start | bytes 221192 | tf_op jit(solution)/shard_map/ppermute | solution.py:352
  209.3 17.3 %collective-permute-start.18 = (bf16[48,768]{1,0:T(8,128)(2,1)S(1)}, bf16[48,768]{1,0:T(8,128)(2,1)S(1)}, u32[]{:S(2)}, u32[]{:S(2)}) collective-permute-start(bf16[48,768]{1,0:T(8,128)(2,1)S(1)} %get-tuple-element.56), channel_id=1, source_target_pairs={{0,64},{8,72},{16,80},{24,88},{32,96},{40,104},{48,112},{56,120},{... | collective-permute-start | bytes 221192 | tf_op jit(solution)/shard_map/ppermute | solution.py:352
  214.2 13.1 %collective-permute-start.17 = (bf16[48,768]{1,0:T(8,128)(2,1)S(1)}, bf16[48,768]{1,0:T(8,128)(2,1)S(1)}, u32[]{:S(2)}, u32[]{:S(2)}) collective-permute-start(bf16[48,768]{1,0:T(8,128)(2,1)S(1)} %get-tuple-element.54), channel_id=1, source_target_pairs={{0,32},{8,40},{16,48},{24,56},{32,64},{40,72},{48,80},{56,88},{64,... | collective-permute-start | bytes 221192 | tf_op jit(solution)/shard_map/ppermute | solution.py:352
